TPU v7x, 128 devices: a whole 4x4x4 slice. The times are simulated.
128 devices in a mesh: doc: 16 (over y, z), feat: 8 (over x, core).
Axes of the slice: x: 4, y: 4, z: 4, core: 2. Of those that a mesh axis runs over, the one named last changes fastest.
Arguments:
- embeddings: bfloat16 [16384, 4096], P('doc'), may hold values from -6 to 6
- projection: bfloat16 [4096, 16384], P(None, 'feat'), may hold values from -0.1875 to 0.1875
- phases: float32 [16384], P('feat'), may hold values from 0 to 6.2831855
- domain_ids: int32 [16384], P('doc'), may hold values from 0 to 511, as said below
- domain_counts: int32 [512], replicated, may hold values from 1 to 2048, as said below
Outputs:
- distances: float32 [512, 512], P('doc')
Inputs may be any that keep to these rules, and one draw needn't show every extreme that they name: `domain_ids`: every domain has at least one document. domain_counts[k] is the number of documents whose domain_ids is k.
All inputs are finite; a program needn't handle non-finite values.
Results may differ from a plain program's by a relative error of at most 0.0003.
Values sent between devices are 32-bit elements; how exact they have to be, the bound alone decides.
No kernel may reach another device: no remote copies, remote signals or barrier semaphores. Data moves between devices by JAX's collectives and lax.ppermute only.
A program may use at most 128 MiB of HBM per device.

v0:
```python
import math

import jax
import jax.numpy as jnp
from jax import lax
from jax.sharding import PartitionSpec as P

F = 16384
K = 512


def per_device(embeddings, projection, phases, domain_ids, domain_counts):
    scale = math.sqrt(2.0 / F)
    angles = jnp.dot(embeddings, projection, preferred_element_type=jnp.float32) + phases[None, :]
    features = (scale * jnp.cos(angles)).astype(jnp.bfloat16)
    owned = K // lax.axis_size("doc")
    first_row = lax.axis_index("doc") * owned
    onehot = (
        domain_ids[:, None] == jnp.arange(owned * lax.axis_size("doc"), dtype=jnp.int32)[None, :]
    ).astype(jnp.bfloat16)
    sums = lax.psum_scatter(
        lax.dot_general(
            onehot, features, (((0,), (0,)), ((), ())), preferred_element_type=jnp.float32
        ),
        "doc",
        scatter_dimension=0,
        tiled=True,
    )
    my_counts = lax.dynamic_slice_in_dim(domain_counts, first_row, owned).astype(jnp.float32)
    mine = sums / my_counts[:, None]
    piece = lax.all_gather(mine, "doc", axis=0, tiled=True)
    product = jnp.dot(mine, piece.T, precision=lax.Precision.HIGHEST)
    norms_now = jnp.sum(piece * piece, axis=1)
    cross = product
    norms = norms_now
    cross, norms = lax.psum((cross, norms), "feat")
    own_norms = lax.dynamic_slice_in_dim(norms, first_row, owned)
    return own_norms[:, None] + norms[None, :] - 2.0 * cross


def solution(mesh):
    in_specs = (P("doc", None), P(None, "feat"), P("feat"), P("doc"), P())
    out_specs = P("doc", None)
    return jax.shard_map(
        per_device, mesh=mesh, in_specs=in_specs, out_specs=out_specs, check_vma=False
    )
```

profile of v0, /device:TPU:1, one launch (start us, length us, event | category | flops | bytes accessed | tf_op | source)
XLA Modules:
  0.0 258.8 jit_solution(12930297920088834612)
XLA Ops:
  6.5 0.0 reduce-scatter.2.cloned.1.call-start
  6.5 1.0 iota_compare_fusion.5
  7.6 45.7 %fusion = f32[512,2048]{1,0:T(8,128)} fusion(bf16[1024,4096]{1,0:T(8,128)(2,1)} %param.5, bf16[4096,2048]{1,0:T(8,128)(2,1)} %param.6, f32[2048]{0:T(1024)} %param.7, pred[1024,512]{1,0:T(32,128)(4,1)S(1)} %iota_compare_fusion.5), kind=kOutput, calls=%fused_computation.3 | convolution fusion | flops 19333644288 | bytes 29892608 | tf_op jit(solution)/shard_map/dot_general | solution.py:22
  53.3 0.0 reduce-scatter.2.cloned.1.call-update
  53.3 0.0 all-gather.2.cloned.1.call-start
  53.3 0.8 dynamic-slice_convert_fusion
  54.1 78.8 %reduce-scatter.2.cloned.1.call-done = f32[32,2048]{1,0:T(8,128)} async-done(((f32[512,2048]{1,0:T(8,128)}), f32[32,2048]{1,0:T(8,128)}) %reduce-scatter.2.cloned.1.call-update) | async-done | bytes 262160 | tf_op jit(solution)/shard_map/reduce_scatter | solution.py:21
  132.9 1.7 broadcast_divide_fusion
  134.6 0.0 all-gather.2.cloned.1.call-update
  134.6 0.0 all-reduce.2.cloned.1.call-start
  134.7 53.1 %all-gather.2.cloned.1.call-done = f32[512,2048]{1,0:T(8,128)} async-done(((f32[32,2048]{1,0:T(8,128)}), f32[512,2048]{1,0:T(8,128)}) %all-gather.2.cloned.1.call-update) | async-done | bytes 4194320 | tf_op jit(solution)/shard_map/all_gather | solution.py:31
  187.8 6.7 %fusion.2 = f32[32,512]{1,0:T(8,128)} fusion(f32[32,2048]{1,0:T(8,128)} %broadcast_divide_fusion, f32[512,2048]{1,0:T(8,128)} %all-gather.2.cloned.1.call-done), kind=kOutput, calls=%fused_computation.8 | convolution fusion | flops 402653184 | bytes 4521984 | tf_op jit(solution)/shard_map/dot_general | solution.py:32
  194.5 0.0 all-reduce.2.cloned.1.call-update
  194.5 2.5 multiply_reduce_fusion
  197.1 12.4 %psum.14 = f32[512]{0:T(512)S(1)} all-reduce(f32[512]{0:T(512)S(1)} %multiply_reduce_fusion), channel_id=1, replica_groups=mesh['doc'=16,'feat'=8] {'feat'}, use_global_device_ids=true, to_apply=%region_2.0 | all-reduce | flops 512 | bytes 4096 | tf_op jit(solution)/shard_map/psum | solution.py:36
  209.5 0.1 dynamic_slice.7
  209.6 41.2 %all-reduce.2.cloned.1.call-done = f32[32,512]{1,0:T(8,128)} async-done(((f32[32,512]{1,0:T(8,128)}), f32[32,512]{1,0:T(8,128)}) %all-reduce.2.cloned.1.call-update) | async-done | bytes 65552 | tf_op jit(solution)/shard_map/psum | solution.py:36
  250.8 1.5 multiply_subtract_fusion
Async XLA Ops:
  6.5 126.3 %reduce-scatter.2.cloned.1.call-start = ((), (), s32[]{:S(2)}) async-start(), calls=%async_computation.1 | async-start | bytes 4456448 | tf_op jit(solution)/shard_map/reduce_scatter | solution.py:21
  53.3 134.5 %all-gather.2.cloned.1.call-start = ((), (), s32[]{:S(2)}) async-start(), calls=%async_computation.2 | async-start | bytes 4456448 | tf_op jit(solution)/shard_map/all_gather | solution.py:31
  134.6 116.2 %all-reduce.2.cloned.1.call-start = ((), (), s32[]{:S(2)}) async-start(), calls=%async_computation.3 | async-start | bytes 131072 | tf_op jit(solution)/shard_map/psum | solution.py:36
Sparse Core Ops, SparseCore 0:
  53.4 79.4 reduce-scatter.1
  135.2 52.4 all-gather.1
  194.7 56.0 all-reduce.1
where the time goes:
time: 260 us; the launch traced here: 259 us
  waiting for transfers between devices  173 us (67%)
  matrix products  52.4 us (20%)
  between operations  13.1 us (5%)
  blocking collectives  12.4 us (5%)
  other arithmetic  7.61 us (3%)
    reduce_scatter x1, waiting for transfers between devices, per_device(): lax.psum_scatter(lax.dot_general(onehot, features, (((0,), (0,)), ((), ()...  78.8 us
    all_gather x1, waiting for transfers between devices, per_device(): piece = lax.all_gather(mine, 'doc', axis=0, tiled=True)  53.1 us
    dot_general x1, matrix products, per_device(): lax.dot_general(onehot, features, (((0,), (0,)), ((), ())), preferred_ele...  45.7 us
    psum x1, waiting for transfers between devices, per_device(): cross, norms = lax.psum((cross, norms), 'feat')  41.2 us
    psum x1, blocking collectives, per_device(): cross, norms = lax.psum((cross, norms), 'feat')  12.4 us
    dot_general x1, matrix products, per_device(): product = jnp.dot(mine, piece.T, precision=lax.Precision.HIGHEST)  6.75 us
  transfers between devices with their start and end apart: 3, of which 3 were waited for; matrix products, arithmetic and copies ran while one was open for 1% of the time, Pallas kernels for 0%

commit v1 on v0

v1 whole, which is shorter than its diff:
```python
import functools
import math

import jax
import jax.numpy as jnp
from jax import lax
from jax.experimental import pallas as pl
from jax.experimental.pallas import tpu as pltpu
from jax.sharding import PartitionSpec as P

F = 16384
K = 512
RING = 4
LANES = 128
TILE = 256

TWO_PI = 2.0 * math.pi
COS = (0.999999989056354, -19.73920449855692, 64.939117412055, -85.45013861233012, 60.16762307755228, -25.967568454490465, 6.528613369785716)


def scaled_cos(turns):
    r = turns - jnp.round(turns)
    u = r * r
    scale = math.sqrt(2.0 / F)
    value = jnp.float32(scale * COS[-1])
    for c in COS[-2::-1]:
        value = value * u + jnp.float32(scale * c)
    return value


def sums_kernel(n_pieces, where_ref, ids_ref, phase_ref, emb_ref, proj_ref, *rest):
    outs, (angle, onehot) = rest[:n_pieces], rest[n_pieces:]
    piece, half = pl.program_id(0), pl.program_id(1)
    me2 = where_ref[1]
    docs = ids_ref.shape[1]
    last = pl.num_programs(1) - 1

    @pl.when((piece == 0) & (half == 0))
    def _():
        onehot[...] = (
            ids_ref[...] == lax.broadcasted_iota(jnp.int32, (K, docs), 0)
        ).astype(jnp.bfloat16)

    def multiply(slot):
        angle[slot] = jnp.dot(
            emb_ref[slot * TILE : (slot + 1) * TILE, :],
            proj_ref[...],
            preferred_element_type=jnp.float32,
        )

    def collect(out, slot, first_doc, fresh):
        turns = angle[slot] * (1.0 / TWO_PI) + phase_ref[...] * (1.0 / TWO_PI)
        features = scaled_cos(turns).astype(jnp.bfloat16)
        part = jnp.dot(
            onehot[:, pl.ds(first_doc, TILE)], features, preferred_element_type=jnp.float32
        )
        for b in range(RING):
            spot = lax.rem(b - me2 + RING, RING)
            columns = part[:, b * LANES : (b + 1) * LANES]
            out[spot] = columns if fresh else out[spot] + columns

    for p in range(n_pieces):

        @pl.when((piece == p) & (half == 0))
        def _(p=p):
            multiply(0)
            multiply(1)
            collect(outs[p], 0, 0, True)

        @pl.when((piece == p) & (half == last))
        def _(p=p):
            multiply(0)
            collect(outs[p], 1, TILE, False)
            multiply(1)
            collect(outs[p], 0, 2 * TILE, False)
            collect(outs[p], 1, 3 * TILE, False)


def domain_sums(offsets, where, ids, phases, embeddings, projection):
    docs, depth = embeddings.shape
    width = projection.shape[1] // RING
    n = len(offsets)
    step = offsets[1] - offsets[0] if n > 1 else 0

    def column(piece, half, where_ref):
        return (0, lax.rem(where_ref[0] + offsets[0] + piece * step, RING))

    spec = pltpu.PrefetchScalarGridSpec(
        num_scalar_prefetch=1,
        grid=(n, docs // (2 * TILE)),
        in_specs=[
            pl.BlockSpec((1, docs), lambda p, h, w: (0, 0)),
            pl.BlockSpec((1, width), column),
            pl.BlockSpec((2 * TILE, depth), lambda p, h, w: (h, 0)),
            pl.BlockSpec((depth, width), column),
        ],
        out_specs=[pl.BlockSpec((RING, K, LANES), lambda p, h, w: (0, 0, 0))] * n,
        scratch_shapes=[
            pltpu.VMEM((2, TILE, width), jnp.float32),
            pltpu.VMEM((K, docs), jnp.bfloat16),
        ],
    )
    return pl.pallas_call(
        functools.partial(sums_kernel, n),
        grid_spec=spec,
        out_shape=[jax.ShapeDtypeStruct((RING, K, LANES), jnp.float32)] * n,
        compiler_params=pltpu.CompilerParams(vmem_limit_bytes=44 << 20),
        cost_estimate=pl.CostEstimate(
            flops=2 * n * docs * width * (depth + K),
            bytes_accessed=n * (2 * docs * depth + 2 * depth * width + 4 * K * width),
            transcendentals=0,
        ),
        name="domain_sums",
    )(where, ids, phases, embeddings, projection)


def distances_kernel(place_ref, mine_ref, other_ref, *rest):
    outs, (rows,) = rest[:RING], rest[RING:]
    y, z, core = place_ref[0], place_ref[1], place_ref[2]
    part = K // (RING * RING * 2)
    means = jnp.concatenate([mine_ref[...], other_ref[...]], axis=1)
    for s1 in range(RING):
        for s2 in range(RING):
            along_y = lax.rem(y + jnp.where(core == 0, s2, s1), RING)
            along_z = lax.rem(z + jnp.where(core == 0, s1, s2), RING)
            first = pl.multiple_of(((along_y * RING + along_z) * 2 + core) * part, part)
            spot = (s1 * RING + s2) * part
            rows[spot : spot + part, :LANES] = mine_ref[pl.ds(first, part), :]
            rows[spot : spot + part, LANES:] = other_ref[pl.ds(first, part), :]
    picked = rows[...]
    nt = (((1,), (1,)), ((), ()))
    cross = lax.dot_general(
        picked, means, nt, precision=lax.Precision.HIGHEST, preferred_element_type=jnp.float32
    )
    norms = lax.dot_general(
        jnp.ones((8, 2 * LANES), jnp.float32),
        means * means,
        nt,
        precision=lax.Precision.HIGHEST,
        preferred_element_type=jnp.float32,
    )
    own = jnp.sum(picked * picked, axis=1, keepdims=True)
    partial = own + norms[:1, :] - 2.0 * cross
    for s1 in range(RING):
        outs[s1][...] = partial[s1 * RING * part : (s1 + 1) * RING * part].reshape(RING, part, K)


def partial_distances(place, mine, other):
    part = K // (RING * RING * 2)
    return pl.pallas_call(
        distances_kernel,
        out_shape=[jax.ShapeDtypeStruct((RING, part, K), jnp.float32)] * RING,
        in_specs=[
            pl.BlockSpec(memory_space=pltpu.SMEM),
            pl.BlockSpec(memory_space=pltpu.VMEM),
            pl.BlockSpec(memory_space=pltpu.VMEM),
        ],
        out_specs=[pl.BlockSpec(memory_space=pltpu.VMEM)] * RING,
        scratch_shapes=[pltpu.VMEM((K // 2, 2 * LANES), jnp.float32)],
        compiler_params=pltpu.CompilerParams(vmem_limit_bytes=16 << 20),
        name="partial_distances",
    )(place, mine, other)


def device(y, z, x, core):
    return (y % RING * RING + z % RING) * (2 * RING) + x % RING * 2 + core


def everywhere():
    for y in range(RING):
        for z in range(RING):
            for x in range(RING):
                for core in range(2):
                    yield y, z, x, core


def shift(stage, by):
    pairs = []
    for y, z, x, core in everywhere():
        along_z = (core == 0) == (stage == 0)
        target = device(y, z + by, x, core) if along_z else device(y + by, z, x, core)
        pairs.append((device(y, z, x, core), target))
    return pairs


def shift_x(by):
    return [(device(y, z, x, c), device(y, z, x + by, c)) for y, z, x, c in everywhere()]


def swap_core():
    return [(device(y, z, x, c), device(y, z, x, 1 - c)) for y, z, x, c in everywhere()]


def send(value, pairs):
    return lax.ppermute(value, ("doc", "feat"), pairs)


def per_device(embeddings, projection, phases, domain_ids, domain_counts):
    doc, feat = lax.axis_index("doc"), lax.axis_index("feat")
    y, z, core = doc // RING, doc % RING, feat % 2
    me1 = jnp.where(core == 0, z, y)
    me2 = jnp.where(core == 0, y, z)
    where = jnp.stack([me1, me2]).astype(jnp.int32)
    place = jnp.stack([y, z, core]).astype(jnp.int32)
    ids = domain_ids[None, :]
    shifts = phases[None, :]

    (far,) = domain_sums([2], where, ids, shifts, embeddings, projection)
    from_far = send(far, shift(0, 2))
    right, left = domain_sums([1, 3], where, ids, shifts, embeddings, projection)
    from_left = send(right, shift(0, 1))
    from_right = send(left, shift(0, 3))
    (kept,) = domain_sums([0], where, ids, shifts, embeddings, projection)

    blocks = [kept[s] + from_far[s] + from_left[s] + from_right[s] for s in range(RING)]
    sums = blocks[0]
    for s in (2, 1, 3):
        sums = sums + send(blocks[s], shift(1, s))
    means = sums / domain_counts.astype(jnp.float32)[:, None]
    other = send(means, swap_core())

    parts = partial_distances(place, means, other)
    total = parts[0]
    for s in (2, 1, 3):
        total = total + send(parts[s], shift(0, s))
    mine = total[0]
    for s in (2, 1, 3):
        mine = mine + send(total[s], shift(1, s))
    across = [send(mine, shift_x(s)) for s in (2, 1, 3)]
    mine = (mine + across[0]) + (across[1] + across[2])
    theirs = send(mine, swap_core())
    return jnp.where(
        core == 0,
        jnp.concatenate([mine, theirs], axis=0),
        jnp.concatenate([theirs, mine], axis=0),
    )


def solution(mesh):
    in_specs = (P("doc", None), P(None, "feat"), P("feat"), P("doc"), P())
    out_specs = P("doc", None)
    return jax.shard_map(
        per_device, mesh=mesh, in_specs=in_specs, out_specs=out_specs, check_vma=False
    )
```

time: 260 us -> 95.6 us (0.37)
  waiting for transfers between devices: 173 us -> 28.7 us
  matrix products: 52.4 us -> 0 us
  Pallas kernels: 0 us -> 36.3 us
  starting transfers between devices: 0.09 us -> 27.6 us
  between operations: 13.1 us -> 0.1 us
  blocking collectives: 12.4 us -> 0 us
  other arithmetic: 7.61 us -> 1.24 us
    reduce_scatter x1 -> x0, waiting for transfers between devices: 78.8 us -> none  [per_device(): lax.psum_scatter(lax.dot_general(onehot, features, (((0,), (0,)), ((), ()...]
    all_gather x1 -> x0, waiting for transfers between devices: 53.1 us -> none  [per_device(): piece = lax.all_gather(mine, 'doc', axis=0, tiled=True)]
    dot_general x2 -> x0, matrix products: 52.4 us -> none  [the longest x1 45.7 us: per_device(): lax.dot_general(onehot, features, (((0,), (0,)), ((), ())), preferred_ele...]
    psum x1 -> x0, waiting for transfers between devices: 41.2 us -> none  [per_device(): cross, norms = lax.psum((cross, norms), 'feat')]
    pallas_call x0 -> x4, Pallas kernels: none -> 36.3 us  [the longest x3 34.7 us: domain_sums(): pl.pallas_call(functools.partial(sums_kernel, n), grid_spec=spec, out_sha...]
    ppermute x0 -> x17, waiting for transfers between devices: none -> 28.7 us  [send(): return lax.ppermute(value, ('doc', 'feat'), pairs)]
    ppermute x0 -> x17, starting transfers between devices: none -> 27.6 us  [send(): return lax.ppermute(value, ('doc', 'feat'), pairs)]
    psum x1 -> x0, blocking collectives: 12.4 us -> none  [per_device(): cross, norms = lax.psum((cross, norms), 'feat')]
  transfers between devices with their start and end apart: 3 -> 17, of which waited for: 3 -> 12; matrix products, arithmetic and copies ran while one was open for 1% -> 0% of each run, Pallas kernels for 0% -> 19%
where the time goes in v1:
time: 95.6 us; the launch traced here: 95.4 us
  Pallas kernels  36.3 us (38%)
  waiting for transfers between devices  28.7 us (30%)
  starting transfers between devices  27.6 us (29%)
  local copies, waits for them, and re-layouts  1.4 us (1%)
  other arithmetic  1.24 us (1%)
    pallas_call x3, Pallas kernels, domain_sums(): pl.pallas_call(functools.partial(sums_kernel, n), grid_spec=spec, out_sha...  34.7 us
    ppermute x17, waiting for transfers between devices, send(): return lax.ppermute(value, ('doc', 'feat'), pairs)  28.7 us
    ppermute x17, starting transfers between devices, send(): return lax.ppermute(value, ('doc', 'feat'), pairs)  27.6 us
  transfers between devices with their start and end apart: 17, of which 12 were waited for; matrix products, arithmetic and copies ran while one was open for 0% of the time, Pallas kernels for 19%

profile of v1, /device:TPU:1, one launch (start us, length us, event | category | flops | bytes accessed | tf_op | source)
XLA Modules:
  0.0 95.4 jit_solution(18199387859737000845)
XLA Ops:
  0.0 0.1 pad_add_fusion.1.where_ref
  0.1 0.7 copy-done.1
  0.8 0.7 copy-done.2
  1.5 16.8 %domain_sums.5 = (f32[4,512,128]{2,1,0:T(8,128)S(1)}, f32[4,512,128]{2,1,0:T(8,128)S(1)}) custom-call(s32[2]{0:T(128)S(1)} %pad_add_fusion.1.where_ref, s32[1,1024]{1,0:T(1,128)S(1)} %bitcast.40, f32[1,2048]{1,0:T(1,128)S(1)} %bitcast.37, bf16[1024,4096]{1,0:T(8,128)(2,1)} %emb_ref.5, bf16[4096,2048]{1,0:T(8,128)(2,1)} %proj_ref.5), custom_call_target="tpu_custom_call" | custom-call | flops 9663676416 | bytes 27262976 | tf_op jit(solution)/shard_map/domain_sums/pallas_call | solution.py:103
  18.3 3.6 %collective-permute-start.2 = (f32[4,512,128]{2,1,0:T(8,128)S(1)}, f32[4,512,128]{2,1,0:T(8,128)S(1)}, u32[]{:S(2)}, u32[]{:S(2)}) collective-permute-start(f32[4,512,128]{2,1,0:T(8,128)S(1)} %get-tuple-element.12), channel_id=1, source_target_pairs={{0,24},{1,97},{2,26},{3,99},{4,28},{5,101},{6,30},{7,103},{8,0},{9... | collective-permute-start | bytes 3145736 | tf_op jit(solution)/shard_map/ppermute | solution.py:195
  21.9 0.0 collective-permute-start.1
  21.9 0.0 copy-done
  21.9 9.0 %domain_sums.4 = f32[4,512,128]{2,1,0:T(8,128)S(1)} custom-call(s32[2]{0:T(128)S(1)} %pad_add_fusion.1.where_ref, s32[1,1024]{1,0:T(1,128)S(1)} %bitcast.41, f32[1,2048]{1,0:T(1,128)S(1)} %bitcast.38, bf16[1024,4096]{1,0:T(8,128)(2,1)S(1)} %copy-done, bf16[4096,2048]{1,0:T(8,128)(2,1)} %proj_ref.5), custom_call_target="tpu_custom_call" | custom-call | flops 4831838208 | bytes 13631488 | tf_op jit(solution)/shard_map/domain_sums/pallas_call | solution.py:103
  30.9 0.0 copy-start.3
  30.9 1.7 %collective-permute-start = (f32[4,512,128]{2,1,0:T(8,128)S(1)}, f32[4,512,128]{2,1,0:T(8,128)S(1)}, u32[]{:S(2)}, u32[]{:S(2)}) collective-permute-start(f32[4,512,128]{2,1,0:T(8,128)S(1)} %domain_sums.4), channel_id=1, source_target_pairs={{0,16},{1,65},{2,18},{3,67},{4,20},{5,69},{6,22},{7,71},{8,24},{9,... | collective-permute-start | bytes 3145736 | tf_op jit(solution)/shard_map/ppermute | solution.py:195
  32.6 9.0 %domain_sums.3 = f32[4,512,128]{2,1,0:T(8,128)S(1)} custom-call(s32[2]{0:T(128)S(1)} %pad_add_fusion.1.where_ref, s32[1,1024]{1,0:T(1,128)S(1)} %bitcast.42, f32[1,2048]{1,0:T(1,128)S(1)} %bitcast.39, bf16[1024,4096]{1,0:T(8,128)(2,1)S(1)} %copy-done, bf16[4096,2048]{1,0:T(8,128)(2,1)} %proj_ref.5), custom_call_target="tpu_custom_call" | custom-call | flops 4831838208 | bytes 13631488 | tf_op jit(solution)/shard_map/domain_sums/pallas_call | solution.py:103
  41.6 0.0 collective-permute-done.2
  41.6 6.7 %collective-permute-done.1 = f32[4,512,128]{2,1,0:T(8,128)S(1)} collective-permute-done((f32[4,512,128]{2,1,0:T(8,128)S(1)}, f32[4,512,128]{2,1,0:T(8,128)S(1)}, u32[]{:S(2)}, u32[]{:S(2)}) %collective-permute-start.1) | collective-permute-done | bytes 1048608 | tf_op jit(solution)/shard_map/ppermute | solution.py:195
  48.3 0.0 collective-permute-done
  48.3 0.2 fusion.2
  48.5 3.6 %collective-permute-start.5 = (f32[512,128]{1,0:T(8,128)S(1)}, f32[512,128]{1,0:T(8,128)S(1)}, u32[]{:S(2)}, u32[]{:S(2)}) collective-permute-start(f32[512,128]{1,0:T(8,128)S(1)} %get-tuple-element.18), channel_id=1, source_target_pairs={{0,96},{1,25},{2,98},{3,27},{4,100},{5,29},{6,102},{7,31},{8,104},... | collective-permute-start | bytes 786440 | tf_op jit(solution)/shard_map/ppermute | solution.py:195
  52.1 0.0 collective-permute-start.4
  52.1 1.3 %collective-permute-start.3 = (f32[512,128]{1,0:T(8,128)S(1)}, f32[512,128]{1,0:T(8,128)S(1)}, u32[]{:S(2)}, u32[]{:S(2)}) collective-permute-start(f32[512,128]{1,0:T(8,128)S(1)} %get-tuple-element.17), channel_id=1, source_target_pairs={{0,64},{1,17},{2,66},{3,19},{4,68},{5,21},{6,70},{7,23},{8,72},{9,... | collective-permute-start | bytes 786440 | tf_op jit(solution)/shard_map/ppermute | solution.py:195
  53.3 0.0 copy-done.3
  53.4 2.0 %collective-permute-done.5 = f32[512,128]{1,0:T(8,128)S(1)} collective-permute-done((f32[512,128]{1,0:T(8,128)S(1)}, f32[512,128]{1,0:T(8,128)S(1)}, u32[]{:S(2)}, u32[]{:S(2)}) %collective-permute-start.5) | collective-permute-done | bytes 262176 | tf_op jit(solution)/shard_map/ppermute | solution.py:195
  55.4 6.2 %collective-permute-done.4 = f32[512,128]{1,0:T(8,128)S(1)} collective-permute-done((f32[512,128]{1,0:T(8,128)S(1)}, f32[512,128]{1,0:T(8,128)S(1)}, u32[]{:S(2)}, u32[]{:S(2)}) %collective-permute-start.4) | collective-permute-done | bytes 262176 | tf_op jit(solution)/shard_map/ppermute | solution.py:195
  61.6 0.0 collective-permute-done.3
  61.6 0.2 fusion.7.mine_ref
  61.8 3.5 %collective-permute-start.6 = (f32[512,128]{1,0:T(8,128)S(1)}, f32[512,128]{1,0:T(8,128)S(1)}, u32[]{:S(2)}, u32[]{:S(2)}) collective-permute-start(f32[512,128]{1,0:T(8,128)S(1)} %fusion.7.mine_ref), channel_id=1, source_target_pairs={{0,1},{1,0},{2,3},{3,2},{4,5},{5,4},{6,7},{7,6},{8,9},{9,8},{10,11... | collective-permute-start | bytes 786440 | tf_op jit(solution)/shard_map/ppermute | solution.py:195
  65.3 0.1 pad_add_fusion.place_ref
  65.4 1.1 %collective-permute-done.6.other_ref = f32[512,128]{1,0:T(8,128)S(1)} collective-permute-done((f32[512,128]{1,0:T(8,128)S(1)}, f32[512,128]{1,0:T(8,128)S(1)}, u32[]{:S(2)}, u32[]{:S(2)}) %collective-permute-start.6) | collective-permute-done | bytes 262176 | tf_op jit(solution)/shard_map/ppermute | solution.py:195
  66.5 1.6 %partial_distances.1 = (f32[4,16,512]{2,1,0:T(8,128)S(1)}, f32[4,16,512]{2,1,0:T(8,128)S(1)}, f32[4,16,512]{2,1,0:T(8,128)S(1)}, f32[4,16,512]{2,1,0:T(8,128)S(1)}) custom-call(s32[3]{0:T(128)S(1)} %pad_add_fusion.place_ref, f32[512,128]{1,0:T(8,128)S(1)} %fusion.7.mine_ref, f32[512,128]{1,0:T(8,128)S(1)} %collective-permute-done.6.other_ref), custom_call_target="tpu_custom_call" | custom-call | tf_op jit(solution)/shard_map/partial_distances/pallas_call | solution.py:150
  68.1 0.5 collective-permute-start.9
  68.6 1.0 %collective-permute-start.8 = (f32[4,16,512]{2,1,0:T(8,128)S(1)}, f32[4,16,512]{2,1,0:T(8,128)S(1)}, u32[]{:S(2)}, u32[]{:S(2)}) collective-permute-start(f32[4,16,512]{2,1,0:T(8,128)S(1)} %get-tuple-element.15), channel_id=1, source_target_pairs={{0,8},{1,33},{2,10},{3,35},{4,12},{5,37},{6,14},{7,39},{8,16},{9,4... | collective-permute-start | bytes 393224 | tf_op jit(solution)/shard_map/ppermute | solution.py:195
  69.6 0.2 collective-permute-start.7
  69.9 2.4 %collective-permute-done.9 = f32[4,16,512]{2,1,0:T(8,128)S(1)} collective-permute-done((f32[4,16,512]{2,1,0:T(8,128)S(1)}, f32[4,16,512]{2,1,0:T(8,128)S(1)}, u32[]{:S(2)}, u32[]{:S(2)}) %collective-permute-start.9) | collective-permute-done | bytes 131104 | tf_op jit(solution)/shard_map/ppermute | solution.py:195
  72.3 1.4 %collective-permute-done.8 = f32[4,16,512]{2,1,0:T(8,128)S(1)} collective-permute-done((f32[4,16,512]{2,1,0:T(8,128)S(1)}, f32[4,16,512]{2,1,0:T(8,128)S(1)}, u32[]{:S(2)}, u32[]{:S(2)}) %collective-permute-start.8) | collective-permute-done | bytes 131104 | tf_op jit(solution)/shard_map/ppermute | solution.py:195
  73.6 1.6 %collective-permute-done.7 = f32[4,16,512]{2,1,0:T(8,128)S(1)} collective-permute-done((f32[4,16,512]{2,1,0:T(8,128)S(1)}, f32[4,16,512]{2,1,0:T(8,128)S(1)}, u32[]{:S(2)}, u32[]{:S(2)}) %collective-permute-start.7) | collective-permute-done | bytes 131104 | tf_op jit(solution)/shard_map/ppermute | solution.py:195
  75.3 0.9 collective-permute-start.12
  76.2 0.6 collective-permute-start.11
  76.9 0.6 collective-permute-start.10
  77.5 0.7 collective-permute-done.12
  78.2 2.0 %collective-permute-done.11 = f32[16,512]{1,0:T(8,128)S(1)} collective-permute-done((f32[16,512]{1,0:T(8,128)S(1)}, f32[16,512]{1,0:T(8,128)S(1)}, u32[]{:S(2)}, u32[]{:S(2)}) %collective-permute-start.11) | collective-permute-done | bytes 32800 | tf_op jit(solution)/shard_map/ppermute | solution.py:195
  80.2 0.9 collective-permute-done.10
  81.1 1.3 %collective-permute-start.14 = (f32[16,512]{1,0:T(8,128)S(1)}, f32[16,512]{1,0:T(8,128)S(1)}, u32[]{:S(2)}, u32[]{:S(2)}) collective-permute-start(f32[16,512]{1,0:T(8,128)S(1)} %fusion.10), channel_id=1, source_target_pairs={{0,2},{1,3},{2,4},{3,5},{4,6},{5,7},{6,0},{7,1},{8,10},{9,11},{10,... | collective-permute-start | bytes 98312 | tf_op jit(solution)/shard_map/ppermute | solution.py:195
  82.4 1.5 %collective-permute-start.15 = (f32[16,512]{1,0:T(8,128)S(1)}, f32[16,512]{1,0:T(8,128)S(1)}, u32[]{:S(2)}, u32[]{:S(2)}) collective-permute-start(f32[16,512]{1,0:T(8,128)S(1)} %fusion.10), channel_id=1, source_target_pairs={{0,6},{1,7},{2,0},{3,1},{4,2},{5,3},{6,4},{7,5},{8,14},{9,15},{10,... | collective-permute-start | bytes 98312 | tf_op jit(solution)/shard_map/ppermute | solution.py:195
  83.9 1.5 %collective-permute-start.13 = (f32[16,512]{1,0:T(8,128)S(1)}, f32[16,512]{1,0:T(8,128)S(1)}, u32[]{:S(2)}, u32[]{:S(2)}) collective-permute-start(f32[16,512]{1,0:T(8,128)S(1)} %fusion.10), channel_id=1, source_target_pairs={{0,4},{1,5},{2,6},{3,7},{4,0},{5,1},{6,2},{7,3},{8,12},{9,13},{10,... | collective-permute-start | bytes 98312 | tf_op jit(solution)/shard_map/ppermute | solution.py:195
  85.4 0.0 collective-permute-done.14
  85.4 0.0 collective-permute-done.15
  85.4 2.7 %collective-permute-done.13 = f32[16,512]{1,0:T(8,128)S(1)} collective-permute-done((f32[16,512]{1,0:T(8,128)S(1)}, f32[16,512]{1,0:T(8,128)S(1)}, u32[]{:S(2)}, u32[]{:S(2)}) %collective-permute-start.13) | collective-permute-done | bytes 32800 | tf_op jit(solution)/shard_map/ppermute | solution.py:195
  88.2 5.7 %collective-permute-start.16 = (f32[16,512]{1,0:T(8,128)S(1)}, f32[16,512]{1,0:T(8,128)S(1)}, u32[]{:S(2)}, u32[]{:S(2)}) collective-permute-start(f32[16,512]{1,0:T(8,128)S(1)} %add_add_fusion.1), channel_id=1, source_target_pairs={{0,1},{1,0},{2,3},{3,2},{4,5},{5,4},{6,7},{7,6},{8,9},{9,8},{10,11... | collective-permute-start | bytes 98312 | tf_op jit(solution)/shard_map/ppermute | solution.py:195
  93.9 0.9 collective-permute-done.16
  94.7 0.6 maximum_select_fusion
  (8 shorter events, 0.1 us)
Async XLA Ops:
  0.1 0.7 copy-start.1
  0.8 0.7 copy-start.2
  1.5 20.4 %copy-start = (bf16[1024,4096]{1,0:T(8,128)(2,1)S(1)}, bf16[1024,4096]{1,0:T(8,128)(2,1)}, u32[]{:S(2)}) copy-start(bf16[1024,4096]{1,0:T(8,128)(2,1)} %emb_ref.5) | copy-start | bytes 25165828
  18.3 23.3 %collective-permute-start.2 = (f32[4,512,128]{2,1,0:T(8,128)S(1)}, f32[4,512,128]{2,1,0:T(8,128)S(1)}, u32[]{:S(2)}, u32[]{:S(2)}) collective-permute-start(f32[4,512,128]{2,1,0:T(8,128)S(1)} %get-tuple-element.12), channel_id=1, source_target_pairs={{0,24},{1,97},{2,26},{3,99},{4,28},{5,101},{6,30},{7,103},{8,0},{9... | collective-permute-start | bytes 3145736 | tf_op jit(solution)/shard_map/ppermute | solution.py:195
  21.9 26.4 %collective-permute-start.1 = (f32[4,512,128]{2,1,0:T(8,128)S(1)}, f32[4,512,128]{2,1,0:T(8,128)S(1)}, u32[]{:S(2)}, u32[]{:S(2)}) collective-permute-start(f32[4,512,128]{2,1,0:T(8,128)S(1)} %get-tuple-element.11), channel_id=1, source_target_pairs={{0,8},{1,33},{2,10},{3,35},{4,12},{5,37},{6,14},{7,39},{8,16},{9,4... | collective-permute-start | bytes 3145736 | tf_op jit(solution)/shard_map/ppermute | solution.py:195
  30.9 22.5 %copy-start.3 = (s32[512]{0:T(512)S(1)}, s32[512]{0:T(512)}, u32[]{:S(2)}) copy-start(s32[512]{0:T(512)} %param.9) | copy-start | bytes 6148
  30.9 17.4 %collective-permute-start = (f32[4,512,128]{2,1,0:T(8,128)S(1)}, f32[4,512,128]{2,1,0:T(8,128)S(1)}, u32[]{:S(2)}, u32[]{:S(2)}) collective-permute-start(f32[4,512,128]{2,1,0:T(8,128)S(1)} %domain_sums.4), channel_id=1, source_target_pairs={{0,16},{1,65},{2,18},{3,67},{4,20},{5,69},{6,22},{7,71},{8,24},{9,... | collective-permute-start | bytes 3145736 | tf_op jit(solution)/shard_map/ppermute | solution.py:195
  48.5 6.9 %collective-permute-start.5 = (f32[512,128]{1,0:T(8,128)S(1)}, f32[512,128]{1,0:T(8,128)S(1)}, u32[]{:S(2)}, u32[]{:S(2)}) collective-permute-start(f32[512,128]{1,0:T(8,128)S(1)} %get-tuple-element.18), channel_id=1, source_target_pairs={{0,96},{1,25},{2,98},{3,27},{4,100},{5,29},{6,102},{7,31},{8,104},... | collective-permute-start | bytes 786440 | tf_op jit(solution)/shard_map/ppermute | solution.py:195
  52.1 9.5 %collective-permute-start.4 = (f32[512,128]{1,0:T(8,128)S(1)}, f32[512,128]{1,0:T(8,128)S(1)}, u32[]{:S(2)}, u32[]{:S(2)}) collective-permute-start(f32[512,128]{1,0:T(8,128)S(1)} %get-tuple-element.19), channel_id=1, source_target_pairs={{0,32},{1,9},{2,34},{3,11},{4,36},{5,13},{6,38},{7,15},{8,40},{9,1... | collective-permute-start | bytes 786440 | tf_op jit(solution)/shard_map/ppermute | solution.py:195
  52.1 9.5 %collective-permute-start.3 = (f32[512,128]{1,0:T(8,128)S(1)}, f32[512,128]{1,0:T(8,128)S(1)}, u32[]{:S(2)}, u32[]{:S(2)}) collective-permute-start(f32[512,128]{1,0:T(8,128)S(1)} %get-tuple-element.17), channel_id=1, source_target_pairs={{0,64},{1,17},{2,66},{3,19},{4,68},{5,21},{6,70},{7,23},{8,72},{9,... | collective-permute-start | bytes 786440 | tf_op jit(solution)/shard_map/ppermute | solution.py:195
  61.8 4.7 %collective-permute-start.6 = (f32[512,128]{1,0:T(8,128)S(1)}, f32[512,128]{1,0:T(8,128)S(1)}, u32[]{:S(2)}, u32[]{:S(2)}) collective-permute-start(f32[512,128]{1,0:T(8,128)S(1)} %fusion.7.mine_ref), channel_id=1, source_target_pairs={{0,1},{1,0},{2,3},{3,2},{4,5},{5,4},{6,7},{7,6},{8,9},{9,8},{10,11... | collective-permute-start | bytes 786440 | tf_op jit(solution)/shard_map/ppermute | solution.py:195
  68.1 4.2 %collective-permute-start.9 = (f32[4,16,512]{2,1,0:T(8,128)S(1)}, f32[4,16,512]{2,1,0:T(8,128)S(1)}, u32[]{:S(2)}, u32[]{:S(2)}) collective-permute-start(f32[4,16,512]{2,1,0:T(8,128)S(1)} %get-tuple-element.16), channel_id=1, source_target_pairs={{0,24},{1,97},{2,26},{3,99},{4,28},{5,101},{6,30},{7,103},{8,0},{9... | collective-permute-start | bytes 393224 | tf_op jit(solution)/shard_map/ppermute | solution.py:195
  68.6 5.0 %collective-permute-start.8 = (f32[4,16,512]{2,1,0:T(8,128)S(1)}, f32[4,16,512]{2,1,0:T(8,128)S(1)}, u32[]{:S(2)}, u32[]{:S(2)}) collective-permute-start(f32[4,16,512]{2,1,0:T(8,128)S(1)} %get-tuple-element.15), channel_id=1, source_target_pairs={{0,8},{1,33},{2,10},{3,35},{4,12},{5,37},{6,14},{7,39},{8,16},{9,4... | collective-permute-start | bytes 393224 | tf_op jit(solution)/shard_map/ppermute | solution.py:195
  69.6 5.6 %collective-permute-start.7 = (f32[4,16,512]{2,1,0:T(8,128)S(1)}, f32[4,16,512]{2,1,0:T(8,128)S(1)}, u32[]{:S(2)}, u32[]{:S(2)}) collective-permute-start(f32[4,16,512]{2,1,0:T(8,128)S(1)} %get-tuple-element.14), channel_id=1, source_target_pairs={{0,16},{1,65},{2,18},{3,67},{4,20},{5,69},{6,22},{7,71},{8,24},{9,... | collective-permute-start | bytes 393224 | tf_op jit(solution)/shard_map/ppermute | solution.py:195
  75.3 2.8 %collective-permute-start.12 = (f32[16,512]{1,0:T(8,128)S(1)}, f32[16,512]{1,0:T(8,128)S(1)}, u32[]{:S(2)}, u32[]{:S(2)}) collective-permute-start(f32[16,512]{1,0:T(8,128)S(1)} %get-tuple-element.21), channel_id=1, source_target_pairs={{0,96},{1,25},{2,98},{3,27},{4,100},{5,29},{6,102},{7,31},{8,104},... | collective-permute-start | bytes 98312 | tf_op jit(solution)/shard_map/ppermute | solution.py:195
  76.2 4.0 %collective-permute-start.11 = (f32[16,512]{1,0:T(8,128)S(1)}, f32[16,512]{1,0:T(8,128)S(1)}, u32[]{:S(2)}, u32[]{:S(2)}) collective-permute-start(f32[16,512]{1,0:T(8,128)S(1)} %get-tuple-element.22), channel_id=1, source_target_pairs={{0,32},{1,9},{2,34},{3,11},{4,36},{5,13},{6,38},{7,15},{8,40},{9,1... | collective-permute-start | bytes 98312 | tf_op jit(solution)/shard_map/ppermute | solution.py:195
  76.9 4.3 %collective-permute-start.10 = (f32[16,512]{1,0:T(8,128)S(1)}, f32[16,512]{1,0:T(8,128)S(1)}, u32[]{:S(2)}, u32[]{:S(2)}) collective-permute-start(f32[16,512]{1,0:T(8,128)S(1)} %get-tuple-element.20), channel_id=1, source_target_pairs={{0,64},{1,17},{2,66},{3,19},{4,68},{5,21},{6,70},{7,23},{8,72},{9,... | collective-permute-start | bytes 98312 | tf_op jit(solution)/shard_map/ppermute | solution.py:195
  81.1 4.3 %collective-permute-start.14 = (f32[16,512]{1,0:T(8,128)S(1)}, f32[16,512]{1,0:T(8,128)S(1)}, u32[]{:S(2)}, u32[]{:S(2)}) collective-permute-start(f32[16,512]{1,0:T(8,128)S(1)} %fusion.10), channel_id=1, source_target_pairs={{0,2},{1,3},{2,4},{3,5},{4,6},{5,7},{6,0},{7,1},{8,10},{9,11},{10,... | collective-permute-start | bytes 98312 | tf_op jit(solution)/shard_map/ppermute | solution.py:195
  82.4 3.0 %collective-permute-start.15 = (f32[16,512]{1,0:T(8,128)S(1)}, f32[16,512]{1,0:T(8,128)S(1)}, u32[]{:S(2)}, u32[]{:S(2)}) collective-permute-start(f32[16,512]{1,0:T(8,128)S(1)} %fusion.10), channel_id=1, source_target_pairs={{0,6},{1,7},{2,0},{3,1},{4,2},{5,3},{6,4},{7,5},{8,14},{9,15},{10,... | collective-permute-start | bytes 98312 | tf_op jit(solution)/shard_map/ppermute | solution.py:195
  83.9 4.3 %collective-permute-start.13 = (f32[16,512]{1,0:T(8,128)S(1)}, f32[16,512]{1,0:T(8,128)S(1)}, u32[]{:S(2)}, u32[]{:S(2)}) collective-permute-start(f32[16,512]{1,0:T(8,128)S(1)} %fusion.10), channel_id=1, source_target_pairs={{0,4},{1,5},{2,6},{3,7},{4,0},{5,1},{6,2},{7,3},{8,12},{9,13},{10,... | collective-permute-start | bytes 98312 | tf_op jit(solution)/shard_map/ppermute | solution.py:195
  88.2 6.6 %collective-permute-start.16 = (f32[16,512]{1,0:T(8,128)S(1)}, f32[16,512]{1,0:T(8,128)S(1)}, u32[]{:S(2)}, u32[]{:S(2)}) collective-permute-start(f32[16,512]{1,0:T(8,128)S(1)} %add_add_fusion.1), channel_id=1, source_target_pairs={{0,1},{1,0},{2,3},{3,2},{4,5},{5,4},{6,7},{7,6},{8,9},{9,8},{10,11... | collective-permute-start | bytes 98312 | tf_op jit(solution)/shard_map/ppermute | solution.py:195

commit v2 on v0

v2 whole, which is shorter than its diff:
```python
import functools
import math

import jax
import jax.numpy as jnp
from jax import lax
from jax.experimental import pallas as pl
from jax.experimental.pallas import tpu as pltpu
from jax.sharding import PartitionSpec as P

F = 16384
K = 512
RING = 4
GROUP = K // RING
OWNED = GROUP // RING
DEEP = 4

TWO_PI = 2.0 * math.pi
COS = (0.999999989056354, -19.73920449855692, 64.939117412055, -85.45013861233012, 60.16762307755228, -25.967568454490465, 6.528613369785716)

VMEM = pl.BlockSpec(memory_space=pltpu.VMEM)
SMEM = pl.BlockSpec(memory_space=pltpu.SMEM)
HBM = pl.BlockSpec(memory_space=pltpu.HBM)


def scaled_cos(turns):
    r = turns - jnp.round(turns)
    u = r * r
    scale = math.sqrt(2.0 / F)
    value = jnp.float32(scale * COS[-1])
    for c in COS[-2::-1]:
        value = value * u + jnp.float32(scale * c)
    return value


def span_of(place_ref, piece, width):
    offset, start, size = piece
    first = (place_ref[0] ^ offset) * width + start
    return pl.ds(pl.multiple_of(first, size), size)


def copies_of(place_ref, pieces, width, proj_hbm, into, sems):
    deep = into.shape[0] // DEEP
    copies, at = [], 0
    for piece in pieces:
        columns = span_of(place_ref, piece, width)
        for i in range(DEEP):
            k = pl.ds(i * deep, deep)
            copies.append(
                pltpu.make_async_copy(
                    proj_hbm.at[k, columns], into.at[k, pl.ds(at, piece[2])], sems.at[len(copies)]
                )
            )
        at += piece[2]
    return copies


def phases_of(phase_ref, place_ref, pieces, width):
    parts = [phase_ref[:, span_of(place_ref, piece, width)] for piece in pieces]
    return jnp.concatenate(parts, axis=1) * (1.0 / TWO_PI)


def collect(first, rows, angle, phase, onehot, outs, initial=None):
    span = slice(first, first + rows)
    turns = angle[span] * (1.0 / TWO_PI) + phase
    features = scaled_cos(turns).astype(jnp.bfloat16)
    part = jnp.dot(onehot[:, span], features, preferred_element_type=jnp.float32)
    at = 0
    for out in outs:
        columns = part[:, at : at + out.shape[1]]
        at += out.shape[1]
        if first > 0:
            out[...] += columns
        elif initial is None:
            out[...] = columns
        else:
            out[...] = columns + initial()


def first_kernel(
    offset, after, place_ref, ids_ref, phase_ref, emb_hbm, proj_hbm,
    out_ref, emb_ref, onehot_ref, next_ref,
    proj, angle, sems,
):
    docs, depth = emb_hbm.shape
    width = proj.shape[1]
    half, deep, tile = docs // 2, depth // DEEP, docs // 4
    columns = span_of(place_ref, (offset, 0, width), width)

    copies = []
    for i in range(DEEP):
        k = pl.ds(i * deep, deep)
        copies.append((
            pltpu.make_async_copy(proj_hbm.at[k, columns], proj.at[k], sems.at[2 * i]),
            pltpu.make_async_copy(
                emb_hbm.at[pl.ds(0, half), k], emb_ref.at[pl.ds(0, half), k], sems.at[2 * i + 1]
            ),
        ))
    rest = [
        pltpu.make_async_copy(
            emb_hbm.at[pl.ds(half + i * tile, tile)],
            emb_ref.at[pl.ds(half + i * tile, tile)],
            sems.at[2 * DEEP + i],
        )
        for i in range(2)
    ]
    ahead = copies_of(
        place_ref, after, width, proj_hbm, next_ref, sems.at[pl.ds(2 * DEEP + 2, DEEP * len(after))]
    )
    batches = [list(pair) for pair in copies] + [[copy] for copy in rest] + [ahead]

    def start(i):
        for copy in batches[i]:
            copy.start()

    def wait(i):
        for copy in batches[i]:
            copy.wait()

    always = pl.when(place_ref[0] >= 0)
    for i in range(3):
        start(i)

    @always
    def _():
        row = lax.broadcasted_iota(jnp.int32, (K, 1), 0)
        group = place_ref[1] ^ (row // GROUP)
        inner = row % GROUP
        domain = jnp.where(
            place_ref[2] == 0,
            group * GROUP + inner,
            (inner // OWNED) * GROUP + group * OWNED + inner % OWNED,
        )
        onehot_ref[...] = (ids_ref[...] == domain.astype(jnp.float32)).astype(jnp.bfloat16)

    for i in range(DEEP):
        wait(i)
        start(i + 3)

        @always
        def _(i=i):
            k = slice(i * deep, (i + 1) * deep)
            part = jnp.dot(emb_ref[:half, k], proj[k], preferred_element_type=jnp.float32)
            if i == 0:
                angle[:half] = part
            else:
                angle[:half] += part

    phase = phases_of(phase_ref, place_ref, [(offset, 0, width)], width)
    for i in range(2):
        wait(DEEP + i)

        @always
        def _(i=i):
            span = slice(half + i * tile, half + (i + 1) * tile)
            angle[span] = jnp.dot(emb_ref[span], proj[...], preferred_element_type=jnp.float32)
            if i == 0:
                collect(0, half, angle, phase, onehot_ref, [out_ref])
            else:
                collect(half, tile, angle, phase, onehot_ref, [out_ref])
                collect(half + tile, tile, angle, phase, onehot_ref, [out_ref])

    wait(DEEP + 2)


def next_kernel(
    pieces, after, place_ref, phase_ref, emb_ref, onehot_ref, proj_ref, proj_hbm, *rest
):
    outs, rest = rest[: len(pieces)], rest[len(pieces) :]
    next_ref, angle, sems = rest
    docs, width = emb_ref.shape[0], proj_ref.shape[1]
    tile = docs // 4
    phase = phases_of(phase_ref, place_ref, pieces, width)
    ahead = copies_of(place_ref, after, width, proj_hbm, next_ref, sems)
    for copy in ahead:
        copy.start()

    @pl.when(place_ref[0] >= 0)
    def _():
        for i in range(4):
            span = slice(i * tile, (i + 1) * tile)
            angle[span] = jnp.dot(
                emb_ref[span], proj_ref[...], preferred_element_type=jnp.float32
            )
            if i > 0:
                collect((i - 1) * tile, tile, angle, phase, onehot_ref, outs)
        collect(3 * tile, tile, angle, phase, onehot_ref, outs)

    for copy in ahead:
        copy.wait()


def last_kernel(
    place_ref, phase_ref, emb_ref, onehot_ref, proj_ref, far_ref, left_ref, right_ref, out_ref, angle
):
    docs, width = emb_ref.shape[0], proj_ref.shape[1]
    tile, half = docs // 4, width // 2
    phase = phases_of(phase_ref, place_ref, [(0, 0, width)], width)

    def arrived():
        near = left_ref[...] + right_ref[...]
        return far_ref[...] + jnp.concatenate([near, jnp.zeros_like(near)], axis=1)

    for i in range(4):
        span = slice(i * tile, (i + 1) * tile)
        angle[span] = jnp.dot(emb_ref[span], proj_ref[...], preferred_element_type=jnp.float32)
        if i > 0:
            collect((i - 1) * tile, tile, angle, phase, onehot_ref, [out_ref], arrived)
    collect(3 * tile, tile, angle, phase, onehot_ref, [out_ref], arrived)


def work(docs, depth, width):
    return pl.CostEstimate(
        flops=2 * docs * width * (depth + K),
        bytes_accessed=4 * K * width,
        transcendentals=0,
    )


def first_sums(offset, after, place, ids, phases, embeddings, projection):
    docs, depth = embeddings.shape
    width = projection.shape[1] // RING
    return pl.pallas_call(
        functools.partial(first_kernel, offset, after),
        out_shape=[
            jax.ShapeDtypeStruct((K, width), jnp.float32),
            jax.ShapeDtypeStruct((docs, depth), jnp.bfloat16),
            jax.ShapeDtypeStruct((K, docs), jnp.bfloat16),
            jax.ShapeDtypeStruct((depth, width), jnp.bfloat16),
        ],
        in_specs=[SMEM, VMEM, VMEM, HBM, HBM],
        out_specs=[VMEM] * 4,
        scratch_shapes=[
            pltpu.VMEM((depth, width), jnp.bfloat16),
            pltpu.VMEM((docs, width), jnp.float32),
            pltpu.SemaphoreType.DMA((2 * DEEP + 2 + DEEP * len(after),)),
        ],
        compiler_params=pltpu.CompilerParams(vmem_limit_bytes=32 << 20),
        cost_estimate=work(docs, depth, width),
        name="first_sums",
    )(place, ids, phases, embeddings, projection)


def next_sums(pieces, after, place, phases, emb, onehot, columns, projection):
    docs, depth = emb.shape
    width = columns.shape[1]
    out_shape = [jax.ShapeDtypeStruct((K, size), jnp.float32) for _, _, size in pieces]
    out_shape.append(jax.ShapeDtypeStruct((depth, width), jnp.bfloat16))
    return pl.pallas_call(
        functools.partial(next_kernel, pieces, after),
        out_shape=out_shape,
        in_specs=[SMEM, VMEM, VMEM, VMEM, VMEM, HBM],
        out_specs=[VMEM] * len(out_shape),
        scratch_shapes=[
            pltpu.VMEM((docs, width), jnp.float32),
            pltpu.SemaphoreType.DMA((DEEP * len(after),)),
        ],
        compiler_params=pltpu.CompilerParams(vmem_limit_bytes=24 << 20),
        cost_estimate=work(docs, depth, width),
        name="next_sums",
    )(place, phases, emb, onehot, columns, projection)


def last_sums(place, phases, emb, onehot, columns, far, left, right):
    docs, depth = emb.shape
    width = columns.shape[1]
    return pl.pallas_call(
        last_kernel,
        out_shape=jax.ShapeDtypeStruct((K, width), jnp.float32),
        in_specs=[SMEM] + [VMEM] * 7,
        out_specs=VMEM,
        scratch_shapes=[pltpu.VMEM((docs, width), jnp.float32)],
        compiler_params=pltpu.CompilerParams(vmem_limit_bytes=24 << 20),
        cost_estimate=work(docs, depth, width),
        name="last_sums",
    )(place, phases, emb, onehot, columns, far, left, right)


def distances_kernel(place_ref, *refs):
    groups, outs, (means, rows) = refs[:RING], refs[RING : 2 * RING], refs[2 * RING :]
    me1, me2, core = place_ref[0], place_ref[1], place_ref[2]
    for s in range(RING):
        group = me2 ^ s
        for f in range(RING):
            first = jnp.where(core == 0, group * GROUP + f * OWNED, f * GROUP + group * OWNED)
            first = pl.multiple_of(first, OWNED)
            means[pl.ds(first, OWNED)] = groups[s][f * OWNED : (f + 1) * OWNED]
        owner = pl.multiple_of((me1 ^ s) * OWNED, OWNED)
        rows[s * OWNED : (s + 1) * OWNED] = groups[0][pl.ds(owner, OWNED)]
    nt = (((1,), (1,)), ((), ()))
    every, picked = means[...], rows[...]
    cross = lax.dot_general(
        picked, every, nt, precision=lax.Precision.HIGHEST, preferred_element_type=jnp.float32
    )
    squares = every * every
    lanes = sum(squares[:, i : i + 128] for i in range(0, squares.shape[1], 128))
    norms = jnp.sum(lanes.T, axis=0, keepdims=True)
    own = jnp.sum(picked * picked, axis=1, keepdims=True)
    partial = own + norms - 2.0 * cross
    for s in range(RING):
        outs[s][...] = partial[s * OWNED : (s + 1) * OWNED]


def partial_distances(place, groups):
    width = groups[0].shape[1]
    return pl.pallas_call(
        distances_kernel,
        out_shape=[jax.ShapeDtypeStruct((OWNED, K), jnp.float32)] * RING,
        in_specs=[SMEM] + [VMEM] * RING,
        out_specs=[VMEM] * RING,
        scratch_shapes=[
            pltpu.VMEM((K, width), jnp.float32),
            pltpu.VMEM((GROUP, width), jnp.float32),
        ],
        compiler_params=pltpu.CompilerParams(vmem_limit_bytes=16 << 20),
        name="partial_distances",
    )(place, *groups)


def device(y, z, x, core):
    return (y * RING + z) * (2 * RING) + x * 2 + core


def everywhere():
    for y in range(RING):
        for z in range(RING):
            for x in range(RING):
                for core in range(2):
                    yield y, z, x, core


def across_ring(stage, by):
    pairs = []
    for y, z, x, core in everywhere():
        along_z = (core == 0) == (stage == 0)
        target = device(y, z ^ by, x, core) if along_z else device(y ^ by, z, x, core)
        pairs.append((device(y, z, x, core), target))
    return pairs


def across_x(by):
    return [(device(y, z, x, c), device(y, z, x ^ by, c)) for y, z, x, c in everywhere()]


def across_core():
    return [(device(y, z, x, c), device(y, z, x, 1 - c)) for y, z, x, c in everywhere()]


def send(value, pairs):
    return lax.ppermute(value, ("doc", "feat"), pairs)


def group_counts(domain_counts, me2, core):
    by_y = lax.dynamic_slice_in_dim(domain_counts, me2 * GROUP, GROUP)
    by_z = lax.dynamic_index_in_dim(domain_counts.reshape(RING, RING, OWNED), me2, 1, False)
    return jnp.where(core == 0, by_y, by_z.reshape(GROUP)).astype(jnp.float32)


def per_device(embeddings, projection, phases, domain_ids, domain_counts):
    doc, feat = lax.axis_index("doc"), lax.axis_index("feat")
    y, z, core = doc // RING, doc % RING, feat % 2
    me1 = jnp.where(core == 0, z, y)
    me2 = jnp.where(core == 0, y, z)
    place = jnp.stack([me1, me2, core]).astype(jnp.int32)
    ids = domain_ids.astype(jnp.float32)[None, :]
    phases = phases[None, :]

    width = projection.shape[1] // RING
    half = width // 2
    near = [[(1, at, half), (3, at, half)] for at in (0, half)]
    kept = [(0, 0, width)]
    far, emb, onehot, columns = first_sums(2, near[0], place, ids, phases, embeddings, projection)
    from_far = send(far, across_ring(0, 2))
    right, left, columns = next_sums(
        near[0], near[1], place, phases, emb, onehot, columns, projection
    )
    from_left, from_right = send(right, across_ring(0, 1)), send(left, across_ring(0, 3))
    right, left, columns = next_sums(near[1], kept, place, phases, emb, onehot, columns, projection)
    late = send(right, across_ring(0, 1)), send(left, across_ring(0, 3))
    sums = last_sums(place, phases, emb, onehot, columns, from_far, from_left, from_right)

    sums = jnp.concatenate([sums[:, :half], sums[:, half:] + (late[0] + late[1])], axis=1)
    sums = sums.reshape(RING, GROUP, width)
    mine = sums[0]
    for s in (2, 1, 3):
        mine = mine + send(sums[s], across_ring(1, s))
    mine = mine / group_counts(domain_counts, me2, core)[:, None]
    groups = [mine] + [send(mine, across_ring(1, s)) for s in (1, 2, 3)]

    parts = partial_distances(place, groups)
    total = parts[0]
    for s in (2, 1, 3):
        total = total + send(parts[s], across_ring(0, s))
    across = [send(total, across_x(s)) for s in (2, 1, 3)]
    total = (total + across[0]) + (across[1] + across[2])
    return total + send(total, across_core())


def solution(mesh):
    in_specs = (P("doc", None), P(None, "feat"), P("feat"), P("doc"), P())
    out_specs = P("doc", None)
    return jax.shard_map(
        per_device, mesh=mesh, in_specs=in_specs, out_specs=out_specs, check_vma=False
    )
```

time: 260 us -> 85.6 us (0.33)
  waiting for transfers between devices: 173 us -> 24 us
  matrix products: 52.4 us -> 0 us
  starting transfers between devices: 0.09 us -> 29.7 us
  Pallas kernels: 0 us -> 28.8 us
  between operations: 13.1 us -> 0.1 us
  blocking collectives: 12.4 us -> 0 us
  other arithmetic: 7.61 us -> 1.85 us
    reduce_scatter x1 -> x0, waiting for transfers between devices: 78.8 us -> none  [per_device(): lax.psum_scatter(lax.dot_general(onehot, features, (((0,), (0,)), ((), ()...]
    all_gather x1 -> x0, waiting for transfers between devices: 53.1 us -> none  [per_device(): piece = lax.all_gather(mine, 'doc', axis=0, tiled=True)]
    dot_general x2 -> x0, matrix products: 52.4 us -> none  [the longest x1 45.7 us: per_device(): lax.dot_general(onehot, features, (((0,), (0,)), ((), ())), preferred_ele...]
    psum x1 -> x0, waiting for transfers between devices: 41.2 us -> none  [per_device(): cross, norms = lax.psum((cross, norms), 'feat')]
    ppermute x0 -> x18, starting transfers between devices: none -> 29.7 us  [send(): return lax.ppermute(value, ('doc', 'feat'), pairs)]
    pallas_call x0 -> x5, Pallas kernels: none -> 28.8 us  [the longest x2 12.2 us: next_sums(): pl.pallas_call(functools.partial(next_kernel, pieces, after), out_shape=o...]
    ppermute x0 -> x18, waiting for transfers between devices: none -> 24 us  [send(): return lax.ppermute(value, ('doc', 'feat'), pairs)]
    psum x1 -> x0, blocking collectives: 12.4 us -> none  [per_device(): cross, norms = lax.psum((cross, norms), 'feat')]
  transfers between devices with their start and end apart: 3 -> 18, of which waited for: 3 -> 13; matrix products, arithmetic and copies ran while one was open for 1% -> 0% of each run, Pallas kernels for 0% -> 21%
where the time goes in v2:
time: 85.6 us; the launch traced here: 85.4 us
  starting transfers between devices  29.7 us (35%)
  Pallas kernels  28.8 us (34%)
  waiting for transfers between devices  24 us (28%)
  other arithmetic  1.85 us (2%)
  local copies, waits for them, and re-layouts  0.89 us (1%)
    ppermute x18, starting transfers between devices, send(): return lax.ppermute(value, ('doc', 'feat'), pairs)  29.7 us
    ppermute x18, waiting for transfers between devices, send(): return lax.ppermute(value, ('doc', 'feat'), pairs)  24 us
    pallas_call x2, Pallas kernels, next_sums(): pl.pallas_call(functools.partial(next_kernel, pieces, after), out_shape=o...  12.2 us
    pallas_call x1, Pallas kernels, first_sums(): pl.pallas_call(functools.partial(first_kernel, offset, after), out_shape=...  8.94 us
    pallas_call x1, Pallas kernels, last_sums(): pl.pallas_call(last_kernel, out_shape=jax.ShapeDtypeStruct((K, width), jn...  5.84 us
    pallas_call x1, Pallas kernels, partial_distances(): pl.pallas_call(distances_kernel, out_shape=[jax.ShapeDtypeStruct((OWNED,...  1.77 us
  transfers between devices with their start and end apart: 18, of which 13 were waited for; matrix products, arithmetic and copies ran while one was open for 0% of the time, Pallas kernels for 21%

profile of v2, /device:TPU:1, one launch (start us, length us, event | category | flops | bytes accessed | tf_op | source)
XLA Modules:
  0.0 85.4 jit_solution(4919768106682113687)
XLA Ops:
  0.0 0.7 convert_element_type.6
  0.7 0.1 pad_add_fusion.place_ref
  0.8 0.7 copy-done
  1.5 8.9 %first_sums.1 = (f32[512,512]{1,0:T(8,128)S(1)}, bf16[1024,4096]{1,0:T(8,128)(2,1)S(1)}, bf16[512,1024]{1,0:T(8,128)(2,1)S(1)}, bf16[4096,512]{1,0:T(8,128)(2,1)S(1)}) custom-call(s32[3]{0:T(128)S(1)} %pad_add_fusion.place_ref, f32[1,1024]{1,0:T(1,128)S(1)} %bitcast.9, f32[1,2048]{1,0:T(1,128)S(1)} %bitcast.5, bf16[1024,4096]{1,0:T(8,128)(2,1)} %emb_hbm.1, ...), custom_call_target="tpu_custom_call" | custom-call | flops 4831838208 | bytes 1048576 | tf_op jit(solution)/shard_map/first_sums/pallas_call | solution.py:223
  10.4 3.8 %collective-permute-start = (f32[512,512]{1,0:T(8,128)S(1)}, f32[512,512]{1,0:T(8,128)S(1)}, u32[]{:S(2)}, u32[]{:S(2)}) collective-permute-start(f32[512,512]{1,0:T(8,128)S(1)} %get-tuple-element.24), channel_id=1, source_target_pairs={{0,16},{1,65},{2,18},{3,67},{4,20},{5,69},{6,22},{7,71},{8,24},{9,... | collective-permute-start | bytes 3145736 | tf_op jit(solution)/shard_map/ppermute | solution.py:350
  14.2 5.9 %next_sums.2 = (f32[512,256]{1,0:T(8,128)S(1)}, f32[512,256]{1,0:T(8,128)S(1)}, bf16[4096,512]{1,0:T(8,128)(2,1)S(1)}) custom-call(s32[3]{0:T(128)S(1)} %pad_add_fusion.place_ref, f32[1,2048]{1,0:T(1,128)S(1)} %bitcast.6, bf16[1024,4096]{1,0:T(8,128)(2,1)S(1)} %get-tuple-element.19.emb_ref, bf16[512,1024]{1,0:T(8,128)(2,1)S(1)} %get-tuple-element.20.onehot_ref, ...), custom_call_target="tpu_custom_call" | custom-call | flops 4831838208 | bytes 1048576 | tf_op jit(solution)/shard_map/next_sums/pallas_call | solution.py:249
  20.2 0.5 collective-permute-start.1
  20.7 0.5 collective-permute-start.2
  21.1 6.3 %next_sums.3 = (f32[512,256]{1,0:T(8,128)S(1)}, f32[512,256]{1,0:T(8,128)S(1)}, bf16[4096,512]{1,0:T(8,128)(2,1)S(1)}) custom-call(s32[3]{0:T(128)S(1)} %pad_add_fusion.place_ref, f32[1,2048]{1,0:T(1,128)S(1)} %bitcast.7, bf16[1024,4096]{1,0:T(8,128)(2,1)S(1)} %get-tuple-element.19.emb_ref, bf16[512,1024]{1,0:T(8,128)(2,1)S(1)} %get-tuple-element.20.onehot_ref, ...), custom_call_target="tpu_custom_call" | custom-call | flops 4831838208 | bytes 1048576 | tf_op jit(solution)/shard_map/next_sums/pallas_call | solution.py:249
  27.4 0.8 collective-permute-start.3
  28.3 1.9 %collective-permute-start.4 = (f32[512,256]{1,0:T(8,128)S(1)}, f32[512,256]{1,0:T(8,128)S(1)}, u32[]{:S(2)}, u32[]{:S(2)}) collective-permute-start(f32[512,256]{1,0:T(8,128)S(1)} %get-tuple-element.28), channel_id=1, source_target_pairs={{0,24},{1,97},{2,26},{3,99},{4,28},{5,101},{6,30},{7,103},{8,16},{... | collective-permute-start | bytes 1572872 | tf_op jit(solution)/shard_map/ppermute | solution.py:350
  30.2 2.6 %collective-permute-done.1.left_ref = f32[512,256]{1,0:T(8,128)S(1)} collective-permute-done((f32[512,256]{1,0:T(8,128)S(1)}, f32[512,256]{1,0:T(8,128)S(1)}, u32[]{:S(2)}, u32[]{:S(2)}) %collective-permute-start.1) | collective-permute-done | bytes 524320 | tf_op jit(solution)/shard_map/ppermute | solution.py:350
  32.8 0.0 collective-permute-done.2.right_ref
  32.8 5.8 %last_sums.1 = f32[512,512]{1,0:T(8,128)S(1)} custom-call(s32[3]{0:T(128)S(1)} %pad_add_fusion.place_ref, f32[1,2048]{1,0:T(1,128)S(1)} %bitcast.8, bf16[1024,4096]{1,0:T(8,128)(2,1)S(1)} %get-tuple-element.19.emb_ref, bf16[512,1024]{1,0:T(8,128)(2,1)S(1)} %get-tuple-element.20.onehot_ref, bf16[4096,512]{1,0:T(8,128)(2,1)S(1)} %get-tuple-element.23.proj_ref, ...), custom_call_target="tpu_custom_call" | custom-call | flops 4831838208 | bytes 1048576 | tf_op jit(solution)/shard_map/last_sums/pallas_call | solution.py:267
  38.6 0.0 collective-permute-done.3
  38.6 0.0 collective-permute-done.4
  38.6 0.1 fusion.8
  38.8 0.1 fusion.6
  38.9 3.7 %collective-permute-start.5 = (f32[128,512]{1,0:T(8,128)S(1)}, f32[128,512]{1,0:T(8,128)S(1)}, u32[]{:S(2)}, u32[]{:S(2)}) collective-permute-start(f32[128,512]{1,0:T(8,128)S(1)} %get-tuple-element.33), channel_id=1, source_target_pairs={{0,64},{1,17},{2,66},{3,19},{4,68},{5,21},{6,70},{7,23},{8,72},{9,... | collective-permute-start | bytes 786440 | tf_op jit(solution)/shard_map/ppermute | solution.py:350
  42.6 0.4 collective-permute-start.7
  43.0 0.3 collective-permute-start.6
  43.3 0.1 reshape.17
  43.4 0.1 reshape.18
  43.5 0.1 fusion.7
  43.6 3.0 %collective-permute-done.5 = f32[128,512]{1,0:T(8,128)S(1)} collective-permute-done((f32[128,512]{1,0:T(8,128)S(1)}, f32[128,512]{1,0:T(8,128)S(1)}, u32[]{:S(2)}, u32[]{:S(2)}) %collective-permute-start.5) | collective-permute-done | bytes 262176 | tf_op jit(solution)/shard_map/ppermute | solution.py:350
  46.6 2.8 %collective-permute-done.7 = f32[128,512]{1,0:T(8,128)S(1)} collective-permute-done((f32[128,512]{1,0:T(8,128)S(1)}, f32[128,512]{1,0:T(8,128)S(1)}, u32[]{:S(2)}, u32[]{:S(2)}) %collective-permute-start.7) | collective-permute-done | bytes 262176 | tf_op jit(solution)/shard_map/ppermute | solution.py:350
  49.4 0.8 collective-permute-done.6
  50.2 0.1 fusion.5.refs_0_
  50.3 2.4 %collective-permute-start.10 = (f32[128,512]{1,0:T(8,128)S(1)}, f32[128,512]{1,0:T(8,128)S(1)}, u32[]{:S(2)}, u32[]{:S(2)}) collective-permute-start(f32[128,512]{1,0:T(8,128)S(1)} %fusion.5.refs_0_), channel_id=1, source_target_pairs={{0,96},{1,25},{2,98},{3,27},{4,100},{5,29},{6,102},{7,31},{8,104},... | collective-permute-start | bytes 786440 | tf_op jit(solution)/shard_map/ppermute | solution.py:350
  52.7 0.2 collective-permute-start.9
  52.9 0.7 collective-permute-start.8
  53.7 6.3 %collective-permute-done.10.refs_3_ = f32[128,512]{1,0:T(8,128)S(1)} collective-permute-done((f32[128,512]{1,0:T(8,128)S(1)}, f32[128,512]{1,0:T(8,128)S(1)}, u32[]{:S(2)}, u32[]{:S(2)}) %collective-permute-start.10) | collective-permute-done | bytes 262176 | tf_op jit(solution)/shard_map/ppermute | solution.py:350
  59.9 0.6 collective-permute-done.8.refs_1_
  60.6 1.8 %partial_distances.1 = (f32[32,512]{1,0:T(8,128)S(1)}, f32[32,512]{1,0:T(8,128)S(1)}, f32[32,512]{1,0:T(8,128)S(1)}, f32[32,512]{1,0:T(8,128)S(1)}) custom-call(s32[3]{0:T(128)S(1)} %pad_add_fusion.place_ref, f32[128,512]{1,0:T(8,128)S(1)} %fusion.5.refs_0_, f32[128,512]{1,0:T(8,128)S(1)} %collective-permute-done.8.refs_1_, ...), custom_call_target="tpu_custom_call" | custom-call | tf_op jit(solution)/shard_map/partial_distances/pallas_call | solution.py:306
  62.3 2.6 %collective-permute-start.11 = (f32[32,512]{1,0:T(8,128)S(1)}, f32[32,512]{1,0:T(8,128)S(1)}, u32[]{:S(2)}, u32[]{:S(2)}) collective-permute-start(f32[32,512]{1,0:T(8,128)S(1)} %get-tuple-element.30), channel_id=1, source_target_pairs={{0,16},{1,65},{2,18},{3,67},{4,20},{5,69},{6,22},{7,71},{8,24},{9,... | collective-permute-start | bytes 196616 | tf_op jit(solution)/shard_map/ppermute | solution.py:350
  64.9 0.4 collective-permute-start.12
  65.3 0.5 collective-permute-start.13
  65.9 1.2 %collective-permute-done.11 = f32[32,512]{1,0:T(8,128)S(1)} collective-permute-done((f32[32,512]{1,0:T(8,128)S(1)}, f32[32,512]{1,0:T(8,128)S(1)}, u32[]{:S(2)}, u32[]{:S(2)}) %collective-permute-start.11) | collective-permute-done | bytes 65568 | tf_op jit(solution)/shard_map/ppermute | solution.py:350
  67.0 1.0 %collective-permute-done.12 = f32[32,512]{1,0:T(8,128)S(1)} collective-permute-done((f32[32,512]{1,0:T(8,128)S(1)}, f32[32,512]{1,0:T(8,128)S(1)}, u32[]{:S(2)}, u32[]{:S(2)}) %collective-permute-start.12) | collective-permute-done | bytes 65568 | tf_op jit(solution)/shard_map/ppermute | solution.py:350
  68.1 1.6 %collective-permute-done.13 = f32[32,512]{1,0:T(8,128)S(1)} collective-permute-done((f32[32,512]{1,0:T(8,128)S(1)}, f32[32,512]{1,0:T(8,128)S(1)}, u32[]{:S(2)}, u32[]{:S(2)}) %collective-permute-start.13) | collective-permute-done | bytes 65568 | tf_op jit(solution)/shard_map/ppermute | solution.py:350
  69.7 2.6 %collective-permute-start.16 = (f32[32,512]{1,0:T(8,128)S(1)}, f32[32,512]{1,0:T(8,128)S(1)}, u32[]{:S(2)}, u32[]{:S(2)}) collective-permute-start(f32[32,512]{1,0:T(8,128)S(1)} %add_add_fusion.1), channel_id=1, source_target_pairs={{0,6},{1,7},{2,4},{3,5},{4,2},{5,3},{6,0},{7,1},{8,14},{9,15},{10,... | collective-permute-start | bytes 196616 | tf_op jit(solution)/shard_map/ppermute | solution.py:350
  72.2 1.4 %collective-permute-start.14 = (f32[32,512]{1,0:T(8,128)S(1)}, f32[32,512]{1,0:T(8,128)S(1)}, u32[]{:S(2)}, u32[]{:S(2)}) collective-permute-start(f32[32,512]{1,0:T(8,128)S(1)} %add_add_fusion.1), channel_id=1, source_target_pairs={{0,4},{1,5},{2,6},{3,7},{4,0},{5,1},{6,2},{7,3},{8,12},{9,13},{10,... | collective-permute-start | bytes 196616 | tf_op jit(solution)/shard_map/ppermute | solution.py:350
  73.6 0.8 collective-permute-done.16
  74.4 1.0 %collective-permute-done.15 = f32[32,512]{1,0:T(8,128)S(1)} collective-permute-done((f32[32,512]{1,0:T(8,128)S(1)}, f32[32,512]{1,0:T(8,128)S(1)}, u32[]{:S(2)}, u32[]{:S(2)}) %collective-permute-start.15) | collective-permute-done | bytes 65568 | tf_op jit(solution)/shard_map/ppermute | solution.py:350
  75.4 1.5 %collective-permute-done.14 = f32[32,512]{1,0:T(8,128)S(1)} collective-permute-done((f32[32,512]{1,0:T(8,128)S(1)}, f32[32,512]{1,0:T(8,128)S(1)}, u32[]{:S(2)}, u32[]{:S(2)}) %collective-permute-start.14) | collective-permute-done | bytes 65568 | tf_op jit(solution)/shard_map/ppermute | solution.py:350
  76.9 7.0 %collective-permute-start.17 = (f32[32,512]{1,0:T(8,128)S(1)}, f32[32,512]{1,0:T(8,128)S(1)}, u32[]{:S(2)}, u32[]{:S(2)}) collective-permute-start(f32[32,512]{1,0:T(8,128)S(1)} %add_add_fusion), channel_id=1, source_target_pairs={{0,1},{1,0},{2,3},{3,2},{4,5},{5,4},{6,7},{7,6},{8,9},{9,8},{10,11... | collective-permute-start | bytes 196616 | tf_op jit(solution)/shard_map/ppermute | solution.py:350
  83.8 0.9 %collective-permute-done.17 = f32[32,512]{1,0:T(8,128)S(1)} collective-permute-done((f32[32,512]{1,0:T(8,128)S(1)}, f32[32,512]{1,0:T(8,128)S(1)}, u32[]{:S(2)}, u32[]{:S(2)}) %collective-permute-start.17) | collective-permute-done | bytes 65568 | tf_op jit(solution)/shard_map/ppermute | solution.py:350
  84.7 0.6 add.66
  (9 shorter events, 0.1 us)
Async XLA Ops:
  0.8 0.7 copy-start
  10.4 22.4 %collective-permute-start = (f32[512,512]{1,0:T(8,128)S(1)}, f32[512,512]{1,0:T(8,128)S(1)}, u32[]{:S(2)}, u32[]{:S(2)}) collective-permute-start(f32[512,512]{1,0:T(8,128)S(1)} %get-tuple-element.24), channel_id=1, source_target_pairs={{0,16},{1,65},{2,18},{3,67},{4,20},{5,69},{6,22},{7,71},{8,24},{9,... | collective-permute-start | bytes 3145736 | tf_op jit(solution)/shard_map/ppermute | solution.py:350
  20.2 12.6 %collective-permute-start.1 = (f32[512,256]{1,0:T(8,128)S(1)}, f32[512,256]{1,0:T(8,128)S(1)}, u32[]{:S(2)}, u32[]{:S(2)}) collective-permute-start(f32[512,256]{1,0:T(8,128)S(1)} %get-tuple-element.25), channel_id=1, source_target_pairs={{0,8},{1,33},{2,10},{3,35},{4,12},{5,37},{6,14},{7,39},{8,0},{9,41... | collective-permute-start | bytes 1572872 | tf_op jit(solution)/shard_map/ppermute | solution.py:350
  20.7 12.1 %collective-permute-start.2 = (f32[512,256]{1,0:T(8,128)S(1)}, f32[512,256]{1,0:T(8,128)S(1)}, u32[]{:S(2)}, u32[]{:S(2)}) collective-permute-start(f32[512,256]{1,0:T(8,128)S(1)} %get-tuple-element.26), channel_id=1, source_target_pairs={{0,24},{1,97},{2,26},{3,99},{4,28},{5,101},{6,30},{7,103},{8,16},{... | collective-permute-start | bytes 1572872 | tf_op jit(solution)/shard_map/ppermute | solution.py:350
  27.4 11.2 %collective-permute-start.3 = (f32[512,256]{1,0:T(8,128)S(1)}, f32[512,256]{1,0:T(8,128)S(1)}, u32[]{:S(2)}, u32[]{:S(2)}) collective-permute-start(f32[512,256]{1,0:T(8,128)S(1)} %get-tuple-element.27), channel_id=1, source_target_pairs={{0,8},{1,33},{2,10},{3,35},{4,12},{5,37},{6,14},{7,39},{8,0},{9,41... | collective-permute-start | bytes 1572872 | tf_op jit(solution)/shard_map/ppermute | solution.py:350
  28.3 10.4 %collective-permute-start.4 = (f32[512,256]{1,0:T(8,128)S(1)}, f32[512,256]{1,0:T(8,128)S(1)}, u32[]{:S(2)}, u32[]{:S(2)}) collective-permute-start(f32[512,256]{1,0:T(8,128)S(1)} %get-tuple-element.28), channel_id=1, source_target_pairs={{0,24},{1,97},{2,26},{3,99},{4,28},{5,101},{6,30},{7,103},{8,16},{... | collective-permute-start | bytes 1572872 | tf_op jit(solution)/shard_map/ppermute | solution.py:350
  32.8 10.6 %copy-start.1 = (s32[512]{0:T(512)S(1)}, s32[512]{0:T(512)}, u32[]{:S(2)}) copy-start(s32[512]{0:T(512)} %param.9) | copy-start | bytes 6148
  38.9 7.7 %collective-permute-start.5 = (f32[128,512]{1,0:T(8,128)S(1)}, f32[128,512]{1,0:T(8,128)S(1)}, u32[]{:S(2)}, u32[]{:S(2)}) collective-permute-start(f32[128,512]{1,0:T(8,128)S(1)} %get-tuple-element.33), channel_id=1, source_target_pairs={{0,64},{1,17},{2,66},{3,19},{4,68},{5,21},{6,70},{7,23},{8,72},{9,... | collective-permute-start | bytes 786440 | tf_op jit(solution)/shard_map/ppermute | solution.py:350
  42.6 6.9 %collective-permute-start.7 = (f32[128,512]{1,0:T(8,128)S(1)}, f32[128,512]{1,0:T(8,128)S(1)}, u32[]{:S(2)}, u32[]{:S(2)}) collective-permute-start(f32[128,512]{1,0:T(8,128)S(1)} %get-tuple-element.34), channel_id=1, source_target_pairs={{0,96},{1,25},{2,98},{3,27},{4,100},{5,29},{6,102},{7,31},{8,104},... | collective-permute-start | bytes 786440 | tf_op jit(solution)/shard_map/ppermute | solution.py:350
  43.0 7.2 %collective-permute-start.6 = (f32[128,512]{1,0:T(8,128)S(1)}, f32[128,512]{1,0:T(8,128)S(1)}, u32[]{:S(2)}, u32[]{:S(2)}) collective-permute-start(f32[128,512]{1,0:T(8,128)S(1)} %get-tuple-element.35), channel_id=1, source_target_pairs={{0,32},{1,9},{2,34},{3,11},{4,36},{5,13},{6,38},{7,15},{8,40},{9,1... | collective-permute-start | bytes 786440 | tf_op jit(solution)/shard_map/ppermute | solution.py:350
  50.3 9.6 %collective-permute-start.10 = (f32[128,512]{1,0:T(8,128)S(1)}, f32[128,512]{1,0:T(8,128)S(1)}, u32[]{:S(2)}, u32[]{:S(2)}) collective-permute-start(f32[128,512]{1,0:T(8,128)S(1)} %fusion.5.refs_0_), channel_id=1, source_target_pairs={{0,96},{1,25},{2,98},{3,27},{4,100},{5,29},{6,102},{7,31},{8,104},... | collective-permute-start | bytes 786440 | tf_op jit(solution)/shard_map/ppermute | solution.py:350
  52.7 7.2 %collective-permute-start.9 = (f32[128,512]{1,0:T(8,128)S(1)}, f32[128,512]{1,0:T(8,128)S(1)}, u32[]{:S(2)}, u32[]{:S(2)}) collective-permute-start(f32[128,512]{1,0:T(8,128)S(1)} %fusion.5.refs_0_), channel_id=1, source_target_pairs={{0,64},{1,17},{2,66},{3,19},{4,68},{5,21},{6,70},{7,23},{8,72},{9,... | collective-permute-start | bytes 786440 | tf_op jit(solution)/shard_map/ppermute | solution.py:350
  52.9 7.6 %collective-permute-start.8 = (f32[128,512]{1,0:T(8,128)S(1)}, f32[128,512]{1,0:T(8,128)S(1)}, u32[]{:S(2)}, u32[]{:S(2)}) collective-permute-start(f32[128,512]{1,0:T(8,128)S(1)} %fusion.5.refs_0_), channel_id=1, source_target_pairs={{0,32},{1,9},{2,34},{3,11},{4,36},{5,13},{6,38},{7,15},{8,40},{9,1... | collective-permute-start | bytes 786440 | tf_op jit(solution)/shard_map/ppermute | solution.py:350
  62.3 4.7 %collective-permute-start.11 = (f32[32,512]{1,0:T(8,128)S(1)}, f32[32,512]{1,0:T(8,128)S(1)}, u32[]{:S(2)}, u32[]{:S(2)}) collective-permute-start(f32[32,512]{1,0:T(8,128)S(1)} %get-tuple-element.30), channel_id=1, source_target_pairs={{0,16},{1,65},{2,18},{3,67},{4,20},{5,69},{6,22},{7,71},{8,24},{9,... | collective-permute-start | bytes 196616 | tf_op jit(solution)/shard_map/ppermute | solution.py:350
  64.9 3.1 %collective-permute-start.12 = (f32[32,512]{1,0:T(8,128)S(1)}, f32[32,512]{1,0:T(8,128)S(1)}, u32[]{:S(2)}, u32[]{:S(2)}) collective-permute-start(f32[32,512]{1,0:T(8,128)S(1)} %get-tuple-element.31), channel_id=1, source_target_pairs={{0,8},{1,33},{2,10},{3,35},{4,12},{5,37},{6,14},{7,39},{8,0},{9,41... | collective-permute-start | bytes 196616 | tf_op jit(solution)/shard_map/ppermute | solution.py:350
  65.3 4.3 %collective-permute-start.13 = (f32[32,512]{1,0:T(8,128)S(1)}, f32[32,512]{1,0:T(8,128)S(1)}, u32[]{:S(2)}, u32[]{:S(2)}) collective-permute-start(f32[32,512]{1,0:T(8,128)S(1)} %get-tuple-element.32), channel_id=1, source_target_pairs={{0,24},{1,97},{2,26},{3,99},{4,28},{5,101},{6,30},{7,103},{8,16},{... | collective-permute-start | bytes 196616 | tf_op jit(solution)/shard_map/ppermute | solution.py:350
  69.7 4.7 %collective-permute-start.16 = (f32[32,512]{1,0:T(8,128)S(1)}, f32[32,512]{1,0:T(8,128)S(1)}, u32[]{:S(2)}, u32[]{:S(2)}) collective-permute-start(f32[32,512]{1,0:T(8,128)S(1)} %add_add_fusion.1), channel_id=1, source_target_pairs={{0,6},{1,7},{2,4},{3,5},{4,2},{5,3},{6,0},{7,1},{8,14},{9,15},{10,... | collective-permute-start | bytes 196616 | tf_op jit(solution)/shard_map/ppermute | solution.py:350
  72.2 3.1 %collective-permute-start.15 = (f32[32,512]{1,0:T(8,128)S(1)}, f32[32,512]{1,0:T(8,128)S(1)}, u32[]{:S(2)}, u32[]{:S(2)}) collective-permute-start(f32[32,512]{1,0:T(8,128)S(1)} %add_add_fusion.1), channel_id=1, source_target_pairs={{0,2},{1,3},{2,0},{3,1},{4,6},{5,7},{6,4},{7,5},{8,10},{9,11},{10,... | collective-permute-start | bytes 196616 | tf_op jit(solution)/shard_map/ppermute | solution.py:350
  72.2 4.6 %collective-permute-start.14 = (f32[32,512]{1,0:T(8,128)S(1)}, f32[32,512]{1,0:T(8,128)S(1)}, u32[]{:S(2)}, u32[]{:S(2)}) collective-permute-start(f32[32,512]{1,0:T(8,128)S(1)} %add_add_fusion.1), channel_id=1, source_target_pairs={{0,4},{1,5},{2,6},{3,7},{4,0},{5,1},{6,2},{7,3},{8,12},{9,13},{10,... | collective-permute-start | bytes 196616 | tf_op jit(solution)/shard_map/ppermute | solution.py:350
  76.9 7.9 %collective-permute-start.17 = (f32[32,512]{1,0:T(8,128)S(1)}, f32[32,512]{1,0:T(8,128)S(1)}, u32[]{:S(2)}, u32[]{:S(2)}) collective-permute-start(f32[32,512]{1,0:T(8,128)S(1)} %add_add_fusion), channel_id=1, source_target_pairs={{0,1},{1,0},{2,3},{3,2},{4,5},{5,4},{6,7},{7,6},{8,9},{9,8},{10,11... | collective-permute-start | bytes 196616 | tf_op jit(solution)/shard_map/ppermute | solution.py:350

commit v3 on v2

--- a/solution.py
+++ b/solution.py
@@ -11,6 +11,7 @@
 F = 16384
 K = 512
 RING = 4
+LANES = 128
 GROUP = K // RING
 OWNED = GROUP // RING
 DEEP = 4
@@ -55,122 +56,115 @@
     return copies
 
 
-def phases_of(phase_ref, place_ref, pieces, width):
-    parts = [phase_ref[:, span_of(place_ref, piece, width)] for piece in pieces]
-    return jnp.concatenate(parts, axis=1) * (1.0 / TWO_PI)
-
-
-def collect(first, rows, angle, phase, onehot, outs, initial=None):
+def phases_of(small_ref, place_ref, pieces, width):
+    rows = []
+    for offset, start, size in pieces:
+        first = ((place_ref[0] ^ offset) * width + start) // LANES
+        rows += [small_ref[pl.ds(first + i, 1)] for i in range(size // LANES)]
+    return jnp.concatenate(rows, axis=1) * (1.0 / TWO_PI)
+
+
+def collect(first, rows, angle, phase, onehot, outs, arrived=()):
     span = slice(first, first + rows)
     turns = angle[span] * (1.0 / TWO_PI) + phase
     features = scaled_cos(turns).astype(jnp.bfloat16)
     part = jnp.dot(onehot[:, span], features, preferred_element_type=jnp.float32)
     at = 0
-    for out in outs:
+    for i, out in enumerate(outs):
         columns = part[:, at : at + out.shape[1]]
         at += out.shape[1]
         if first > 0:
             out[...] += columns
-        elif initial is None:
+        elif arrived:
+            out[...] = columns + arrived[i][...]
+        else:
             out[...] = columns
-        else:
-            out[...] = columns + initial()
 
 
 def first_kernel(
-    offset, after, place_ref, ids_ref, phase_ref, emb_hbm, proj_hbm,
-    out_ref, emb_ref, onehot_ref, next_ref,
+    offset, after, place_ref, small_ref, emb_hbm, proj_hbm,
+    low_ref, high_ref, emb_ref, onehot_ref, next_ref,
     proj, angle, sems,
 ):
     docs, depth = emb_hbm.shape
     width = proj.shape[1]
     half, deep, tile = docs // 2, depth // DEEP, docs // 4
     columns = span_of(place_ref, (offset, 0, width), width)
-
-    copies = []
+    outs = [low_ref, high_ref]
+
+    copies, sides = [], (slice(0, half), slice(half, docs))
     for i in range(DEEP):
         k = pl.ds(i * deep, deep)
-        copies.append((
-            pltpu.make_async_copy(proj_hbm.at[k, columns], proj.at[k], sems.at[2 * i]),
-            pltpu.make_async_copy(
-                emb_hbm.at[pl.ds(0, half), k], emb_ref.at[pl.ds(0, half), k], sems.at[2 * i + 1]
-            ),
-        ))
-    rest = [
-        pltpu.make_async_copy(
-            emb_hbm.at[pl.ds(half + i * tile, tile)],
-            emb_ref.at[pl.ds(half + i * tile, tile)],
-            sems.at[2 * DEEP + i],
+        copies.append(
+            [pltpu.make_async_copy(proj_hbm.at[k, columns], proj.at[k], sems.at[3 * i])]
+            + [
+                pltpu.make_async_copy(
+                    emb_hbm.at[pl.ds(side * half, half), k],
+                    emb_ref.at[pl.ds(side * half, half), k],
+                    sems.at[3 * i + 1 + side],
+                )
+                for side in range(2)
+            ]
         )
-        for i in range(2)
-    ]
     ahead = copies_of(
-        place_ref, after, width, proj_hbm, next_ref, sems.at[pl.ds(2 * DEEP + 2, DEEP * len(after))]
-    )
-    batches = [list(pair) for pair in copies] + [[copy] for copy in rest] + [ahead]
+        place_ref, after, width, proj_hbm, next_ref, sems.at[pl.ds(3 * DEEP, DEEP * len(after))]
+    )
+    copies.append(ahead)
 
     def start(i):
-        for copy in batches[i]:
+        for copy in copies[i]:
             copy.start()
 
-    def wait(i):
-        for copy in batches[i]:
-            copy.wait()
-
-    always = pl.when(place_ref[0] >= 0)
-    for i in range(3):
+    for i in range(2):
         start(i)
-
-    @always
-    def _():
-        row = lax.broadcasted_iota(jnp.int32, (K, 1), 0)
-        group = place_ref[1] ^ (row // GROUP)
-        inner = row % GROUP
-        domain = jnp.where(
-            place_ref[2] == 0,
-            group * GROUP + inner,
-            (inner // OWNED) * GROUP + group * OWNED + inner % OWNED,
-        )
-        onehot_ref[...] = (ids_ref[...] == domain.astype(jnp.float32)).astype(jnp.bfloat16)
+    row = lax.broadcasted_iota(jnp.int32, (K, 1), 0)
+    group = place_ref[1] ^ (row // GROUP)
+    inner = row % GROUP
+    domain = jnp.where(
+        place_ref[2] == 0,
+        group * GROUP + inner,
+        (inner // OWNED) * GROUP + group * OWNED + inner % OWNED,
+    )
+    domain = domain.astype(jnp.float32)
+    first_row = RING * width // LANES
+    for i in range(docs // LANES):
+        ids = small_ref[first_row + i : first_row + i + 1]
+        onehot_ref[:, i * LANES : (i + 1) * LANES] = (ids == domain).astype(jnp.bfloat16)
+    phase = phases_of(small_ref, place_ref, [(offset, 0, width)], width)
+
+    def multiply(i, side):
+        k = slice(i * deep, (i + 1) * deep)
+        part = jnp.dot(emb_ref[sides[side], k], proj[k], preferred_element_type=jnp.float32)
+        if i == 0:
+            angle[sides[side]] = part
+        else:
+            angle[sides[side]] += part
 
     for i in range(DEEP):
-        wait(i)
-        start(i + 3)
-
-        @always
-        def _(i=i):
-            k = slice(i * deep, (i + 1) * deep)
-            part = jnp.dot(emb_ref[:half, k], proj[k], preferred_element_type=jnp.float32)
-            if i == 0:
-                angle[:half] = part
-            else:
-                angle[:half] += part
-
-    phase = phases_of(phase_ref, place_ref, [(offset, 0, width)], width)
-    for i in range(2):
-        wait(DEEP + i)
-
-        @always
-        def _(i=i):
-            span = slice(half + i * tile, half + (i + 1) * tile)
-            angle[span] = jnp.dot(emb_ref[span], proj[...], preferred_element_type=jnp.float32)
-            if i == 0:
-                collect(0, half, angle, phase, onehot_ref, [out_ref])
-            else:
-                collect(half, tile, angle, phase, onehot_ref, [out_ref])
-                collect(half + tile, tile, angle, phase, onehot_ref, [out_ref])
-
-    wait(DEEP + 2)
+        copies[i][0].wait()
+        copies[i][1].wait()
+        if i + 2 <= DEEP:
+            start(i + 2)
+        multiply(i, 0)
+        copies[i][2].wait()
+        multiply(i, 1)
+        if i == DEEP - 1:
+            collect(0, half, angle, phase, onehot_ref, outs)
+    collect(half, tile, angle, phase, onehot_ref, outs)
+    collect(half + tile, tile, angle, phase, onehot_ref, outs)
+    for copy in ahead:
+        copy.wait()
 
 
 def next_kernel(
-    pieces, after, place_ref, phase_ref, emb_ref, onehot_ref, proj_ref, proj_hbm, *rest
+    pieces, after, n_arrived, place_ref, small_ref, emb_ref, onehot_ref, proj_ref, proj_hbm, *rest
 ):
+    arrived, rest = rest[:n_arrived], rest[n_arrived:]
     outs, rest = rest[: len(pieces)], rest[len(pieces) :]
     next_ref, angle, sems = rest
     docs, width = emb_ref.shape[0], proj_ref.shape[1]
     tile = docs // 4
-    phase = phases_of(phase_ref, place_ref, pieces, width)
+    phase = phases_of(small_ref, place_ref, pieces, width)
     ahead = copies_of(place_ref, after, width, proj_hbm, next_ref, sems)
     for copy in ahead:
         copy.start()
@@ -183,7 +177,7 @@
                 emb_ref[span], proj_ref[...], preferred_element_type=jnp.float32
             )
             if i > 0:
-                collect((i - 1) * tile, tile, angle, phase, onehot_ref, outs)
+                collect((i - 1) * tile, tile, angle, phase, onehot_ref, outs, arrived)
         collect(3 * tile, tile, angle, phase, onehot_ref, outs)
 
     for copy in ahead:
@@ -191,22 +185,19 @@
 
 
 def last_kernel(
-    place_ref, phase_ref, emb_ref, onehot_ref, proj_ref, far_ref, left_ref, right_ref, out_ref, angle
+    place_ref, small_ref, emb_ref, onehot_ref, proj_ref, low_ref, high_ref, out_ref, angle
 ):
     docs, width = emb_ref.shape[0], proj_ref.shape[1]
     tile, half = docs // 4, width // 2
-    phase = phases_of(phase_ref, place_ref, [(0, 0, width)], width)
-
-    def arrived():
-        near = left_ref[...] + right_ref[...]
-        return far_ref[...] + jnp.concatenate([near, jnp.zeros_like(near)], axis=1)
-
+    phase = phases_of(small_ref, place_ref, [(0, 0, width)], width)
+    outs = [out_ref.at[:, :half], out_ref.at[:, half:]]
+    arrived = [low_ref, high_ref]
     for i in range(4):
         span = slice(i * tile, (i + 1) * tile)
         angle[span] = jnp.dot(emb_ref[span], proj_ref[...], preferred_element_type=jnp.float32)
         if i > 0:
-            collect((i - 1) * tile, tile, angle, phase, onehot_ref, [out_ref], arrived)
-    collect(3 * tile, tile, angle, phase, onehot_ref, [out_ref], arrived)
+            collect((i - 1) * tile, tile, angle, phase, onehot_ref, outs, arrived)
+    collect(3 * tile, tile, angle, phase, onehot_ref, outs)
 
 
 def work(docs, depth, width):
@@ -217,39 +208,40 @@
     )
 
 
-def first_sums(offset, after, place, ids, phases, embeddings, projection):
+def first_sums(offset, after, place, small, embeddings, projection):
     docs, depth = embeddings.shape
     width = projection.shape[1] // RING
     return pl.pallas_call(
         functools.partial(first_kernel, offset, after),
         out_shape=[
-            jax.ShapeDtypeStruct((K, width), jnp.float32),
+            jax.ShapeDtypeStruct((K, width // 2), jnp.float32),
+            jax.ShapeDtypeStruct((K, width // 2), jnp.float32),
             jax.ShapeDtypeStruct((docs, depth), jnp.bfloat16),
             jax.ShapeDtypeStruct((K, docs), jnp.bfloat16),
             jax.ShapeDtypeStruct((depth, width), jnp.bfloat16),
         ],
-        in_specs=[SMEM, VMEM, VMEM, HBM, HBM],
-        out_specs=[VMEM] * 4,
+        in_specs=[SMEM, VMEM, HBM, HBM],
+        out_specs=[VMEM] * 5,
         scratch_shapes=[
             pltpu.VMEM((depth, width), jnp.bfloat16),
             pltpu.VMEM((docs, width), jnp.float32),
-            pltpu.SemaphoreType.DMA((2 * DEEP + 2 + DEEP * len(after),)),
+            pltpu.SemaphoreType.DMA((3 * DEEP + DEEP * len(after),)),
         ],
         compiler_params=pltpu.CompilerParams(vmem_limit_bytes=32 << 20),
         cost_estimate=work(docs, depth, width),
         name="first_sums",
-    )(place, ids, phases, embeddings, projection)
-
-
-def next_sums(pieces, after, place, phases, emb, onehot, columns, projection):
+    )(place, small, embeddings, projection)
+
+
+def next_sums(pieces, after, place, small, emb, onehot, columns, projection, *arrived):
     docs, depth = emb.shape
     width = columns.shape[1]
     out_shape = [jax.ShapeDtypeStruct((K, size), jnp.float32) for _, _, size in pieces]
     out_shape.append(jax.ShapeDtypeStruct((depth, width), jnp.bfloat16))
     return pl.pallas_call(
-        functools.partial(next_kernel, pieces, after),
+        functools.partial(next_kernel, pieces, after, len(arrived)),
         out_shape=out_shape,
-        in_specs=[SMEM, VMEM, VMEM, VMEM, VMEM, HBM],
+        in_specs=[SMEM, VMEM, VMEM, VMEM, VMEM, HBM] + [VMEM] * len(arrived),
         out_specs=[VMEM] * len(out_shape),
         scratch_shapes=[
             pltpu.VMEM((docs, width), jnp.float32),
@@ -258,22 +250,22 @@
         compiler_params=pltpu.CompilerParams(vmem_limit_bytes=24 << 20),
         cost_estimate=work(docs, depth, width),
         name="next_sums",
-    )(place, phases, emb, onehot, columns, projection)
-
-
-def last_sums(place, phases, emb, onehot, columns, far, left, right):
+    )(place, small, emb, onehot, columns, projection, *arrived)
+
+
+def last_sums(place, small, emb, onehot, columns, low, high):
     docs, depth = emb.shape
     width = columns.shape[1]
     return pl.pallas_call(
         last_kernel,
         out_shape=jax.ShapeDtypeStruct((K, width), jnp.float32),
-        in_specs=[SMEM] + [VMEM] * 7,
+        in_specs=[SMEM] + [VMEM] * 6,
         out_specs=VMEM,
         scratch_shapes=[pltpu.VMEM((docs, width), jnp.float32)],
         compiler_params=pltpu.CompilerParams(vmem_limit_bytes=24 << 20),
         cost_estimate=work(docs, depth, width),
         name="last_sums",
-    )(place, phases, emb, onehot, columns, far, left, right)
+    )(place, small, emb, onehot, columns, low, high)
 
 
 def distances_kernel(place_ref, *refs):
@@ -362,24 +354,30 @@
     me1 = jnp.where(core == 0, z, y)
     me2 = jnp.where(core == 0, y, z)
     place = jnp.stack([me1, me2, core]).astype(jnp.int32)
-    ids = domain_ids.astype(jnp.float32)[None, :]
-    phases = phases[None, :]
+    phases, ids = phases.reshape(-1, LANES), domain_ids.reshape(-1, LANES)
+    small = jnp.pad(phases, ((0, ids.shape[0]), (0, 0)))
+    small = small + jnp.pad(ids, ((phases.shape[0], 0), (0, 0))).astype(jnp.float32)
 
     width = projection.shape[1] // RING
     half = width // 2
-    near = [[(1, at, half), (3, at, half)] for at in (0, half)]
+    first = [(1, 0, half), (3, half, half)]
+    second = [(3, 0, half), (1, half, half)]
     kept = [(0, 0, width)]
-    far, emb, onehot, columns = first_sums(2, near[0], place, ids, phases, embeddings, projection)
-    from_far = send(far, across_ring(0, 2))
-    right, left, columns = next_sums(
-        near[0], near[1], place, phases, emb, onehot, columns, projection
-    )
-    from_left, from_right = send(right, across_ring(0, 1)), send(left, across_ring(0, 3))
-    right, left, columns = next_sums(near[1], kept, place, phases, emb, onehot, columns, projection)
-    late = send(right, across_ring(0, 1)), send(left, across_ring(0, 3))
-    sums = last_sums(place, phases, emb, onehot, columns, from_far, from_left, from_right)
-
-    sums = jnp.concatenate([sums[:, :half], sums[:, half:] + (late[0] + late[1])], axis=1)
+    low, high, emb, onehot, columns = first_sums(
+        2, first, place, small, embeddings, projection
+    )
+    far_low, far_high = send(low, across_ring(0, 1)), send(high, across_ring(0, 3))
+    low, high, columns = next_sums(
+        first, second, place, small, emb, onehot, columns, projection
+    )
+    near_low, near_high = send(low, across_ring(0, 1)), send(high, across_ring(0, 3))
+    low, high, columns = next_sums(
+        second, kept, place, small, emb, onehot, columns, projection, far_low, far_high
+    )
+    late_low, late_high = send(low, across_ring(0, 3)), send(high, across_ring(0, 1))
+    sums = last_sums(place, small, emb, onehot, columns, near_low, near_high)
+
+    sums = jnp.concatenate([sums[:, :half] + late_low, sums[:, half:] + late_high], axis=1)
     sums = sums.reshape(RING, GROUP, width)
     mine = sums[0]
     for s in (2, 1, 3):

time: 85.6 us -> 84.2 us (0.984)
    ppermute x18 -> x19, waiting for transfers between devices: 24 us -> 23.6 us  [send(): return lax.ppermute(value, ('doc', 'feat'), pairs)]
    ppermute x18 -> x19, starting transfers between devices: 29.7 us -> 30 us  [send(): return lax.ppermute(value, ('doc', 'feat'), pairs)]
  transfers between devices with their start and end apart: 18 -> 19, of which waited for: 13 -> 15; matrix products, arithmetic and copies ran while one was open for 0% -> 0% of each run, Pallas kernels for 21% -> 21%
where the time goes in v3:
time: 84.2 us; the launch traced here: 84 us
  starting transfers between devices  30 us (36%)
  Pallas kernels  28.3 us (34%)
  waiting for transfers between devices  23.6 us (28%)
  other arithmetic  1.87 us (2%)
    ppermute x19, starting transfers between devices, send(): return lax.ppermute(value, ('doc', 'feat'), pairs)  30 us
    ppermute x19, waiting for transfers between devices, send(): return lax.ppermute(value, ('doc', 'feat'), pairs)  23.6 us
    pallas_call x2, Pallas kernels, next_sums(): pl.pallas_call(functools.partial(next_kernel, pieces, after, len(arrived)...  12 us
    pallas_call x1, Pallas kernels, first_sums(): pl.pallas_call(functools.partial(first_kernel, offset, after), out_shape=...  8.62 us
    pallas_call x1, Pallas kernels, last_sums(): pl.pallas_call(last_kernel, out_shape=jax.ShapeDtypeStruct((K, width), jn...  5.85 us
    pallas_call x1, Pallas kernels, partial_distances(): pl.pallas_call(distances_kernel, out_shape=[jax.ShapeDtypeStruct((OWNED,...  1.77 us
  transfers between devices with their start and end apart: 19, of which 15 were waited for; matrix products, arithmetic and copies ran while one was open for 0% of the time, Pallas kernels for 21%

profile of v3, /device:TPU:1, one launch (start us, length us, event | category | flops | bytes accessed | tf_op | source)
XLA Modules:
  0.0 84.0 jit_solution(7597850029616917771)
XLA Ops:
  0.0 0.7 convert_add_fusion.small_ref
  0.7 0.1 pad_add_fusion.place_ref
  0.8 8.6 %first_sums.1 = (f32[512,256]{1,0:T(8,128)S(1)}, f32[512,256]{1,0:T(8,128)S(1)}, bf16[1024,4096]{1,0:T(8,128)(2,1)S(1)}, bf16[512,1024]{1,0:T(8,128)(2,1)S(1)}, bf16[4096,512]{1,0:T(8,128)(2,1)S(1)}) custom-call(s32[3]{0:T(128)S(1)} %pad_add_fusion.place_ref, f32[24,128]{1,0:T(8,128)S(1)} %convert_add_fusion.small_ref, bf16[1024,4096]{1,0:T(8,128)(2,1)} %emb_hbm.1, ...), custom_call_target="tpu_custom_call" | custom-call | flops 4831838208 | bytes 1048576 | tf_op jit(solution)/shard_map/first_sums/pallas_call | solution.py:214
  9.4 2.2 %collective-permute-start = (f32[512,256]{1,0:T(8,128)S(1)}, f32[512,256]{1,0:T(8,128)S(1)}, u32[]{:S(2)}, u32[]{:S(2)}) collective-permute-start(f32[512,256]{1,0:T(8,128)S(1)} %get-tuple-element.24), channel_id=1, source_target_pairs={{0,8},{1,33},{2,10},{3,35},{4,12},{5,37},{6,14},{7,39},{8,0},{9,41... | collective-permute-start | bytes 1572872 | tf_op jit(solution)/shard_map/ppermute | solution.py:342
  11.6 1.9 %collective-permute-start.1 = (f32[512,256]{1,0:T(8,128)S(1)}, f32[512,256]{1,0:T(8,128)S(1)}, u32[]{:S(2)}, u32[]{:S(2)}) collective-permute-start(f32[512,256]{1,0:T(8,128)S(1)} %get-tuple-element.25), channel_id=1, source_target_pairs={{0,24},{1,97},{2,26},{3,99},{4,28},{5,101},{6,30},{7,103},{8,16},{... | collective-permute-start | bytes 1572872 | tf_op jit(solution)/shard_map/ppermute | solution.py:342
  13.5 6.0 %next_sums.2 = (f32[512,256]{1,0:T(8,128)S(1)}, f32[512,256]{1,0:T(8,128)S(1)}, bf16[4096,512]{1,0:T(8,128)(2,1)S(1)}) custom-call(s32[3]{0:T(128)S(1)} %pad_add_fusion.place_ref, f32[24,128]{1,0:T(8,128)S(1)} %convert_add_fusion.small_ref, bf16[1024,4096]{1,0:T(8,128)(2,1)S(1)} %get-tuple-element.20.emb_ref, ...), custom_call_target="tpu_custom_call" | custom-call | flops 4831838208 | bytes 1048576 | tf_op jit(solution)/shard_map/next_sums/pallas_call | solution.py:241
  19.5 0.5 collective-permute-start.2
  20.0 0.6 collective-permute-start.3
  20.6 0.6 collective-permute-done.1.rest_1_
  21.1 6.1 %next_sums.3 = (f32[512,256]{1,0:T(8,128)S(1)}, f32[512,256]{1,0:T(8,128)S(1)}, bf16[4096,512]{1,0:T(8,128)(2,1)S(1)}) custom-call(s32[3]{0:T(128)S(1)} %pad_add_fusion.place_ref, f32[24,128]{1,0:T(8,128)S(1)} %convert_add_fusion.small_ref, bf16[1024,4096]{1,0:T(8,128)(2,1)S(1)} %get-tuple-element.20.emb_ref, ...), custom_call_target="tpu_custom_call" | custom-call | flops 4831838208 | bytes 1048576 | tf_op jit(solution)/shard_map/next_sums/pallas_call | solution.py:241
  27.2 2.0 %collective-permute-start.4 = (f32[512,256]{1,0:T(8,128)S(1)}, f32[512,256]{1,0:T(8,128)S(1)}, u32[]{:S(2)}, u32[]{:S(2)}) collective-permute-start(f32[512,256]{1,0:T(8,128)S(1)} %get-tuple-element.29), channel_id=1, source_target_pairs={{0,24},{1,97},{2,26},{3,99},{4,28},{5,101},{6,30},{7,103},{8,16},{... | collective-permute-start | bytes 1572872 | tf_op jit(solution)/shard_map/ppermute | solution.py:342
  29.2 0.0 collective-permute-start.5
  29.2 0.0 collective-permute-done.2.low_ref
  29.2 0.3 collective-permute-done.3.high_ref
  29.5 5.8 %last_sums.1 = f32[512,512]{1,0:T(8,128)S(1)} custom-call(s32[3]{0:T(128)S(1)} %pad_add_fusion.place_ref, f32[24,128]{1,0:T(8,128)S(1)} %convert_add_fusion.small_ref, bf16[1024,4096]{1,0:T(8,128)(2,1)S(1)} %get-tuple-element.20.emb_ref, bf16[512,1024]{1,0:T(8,128)(2,1)S(1)} %get-tuple-element.21.onehot_ref, ...), custom_call_target="tpu_custom_call" | custom-call | flops 4831838208 | bytes 1048576 | tf_op jit(solution)/shard_map/last_sums/pallas_call | solution.py:259
  35.4 1.5 %collective-permute-done.4 = f32[512,256]{1,0:T(8,128)S(1)} collective-permute-done((f32[512,256]{1,0:T(8,128)S(1)}, f32[512,256]{1,0:T(8,128)S(1)}, u32[]{:S(2)}, u32[]{:S(2)}) %collective-permute-start.4) | collective-permute-done | bytes 524320 | tf_op jit(solution)/shard_map/ppermute | solution.py:342
  36.9 0.7 collective-permute-done.5
  37.6 0.1 slice_add_fusion.1
  37.7 0.1 fusion.6
  37.8 3.2 %collective-permute-start.6 = (f32[128,512]{1,0:T(8,128)S(1)}, f32[128,512]{1,0:T(8,128)S(1)}, u32[]{:S(2)}, u32[]{:S(2)}) collective-permute-start(f32[128,512]{1,0:T(8,128)S(1)} %get-tuple-element.35), channel_id=1, source_target_pairs={{0,64},{1,17},{2,66},{3,19},{4,68},{5,21},{6,70},{7,23},{8,72},{9,... | collective-permute-start | bytes 786440 | tf_op jit(solution)/shard_map/ppermute | solution.py:342
  41.0 0.7 collective-permute-start.8
  41.7 0.5 collective-permute-start.7
  42.2 0.1 reshape.25
  42.3 0.1 reshape.26
  42.4 0.1 fusion.7
  42.5 2.3 %collective-permute-done.6 = f32[128,512]{1,0:T(8,128)S(1)} collective-permute-done((f32[128,512]{1,0:T(8,128)S(1)}, f32[128,512]{1,0:T(8,128)S(1)}, u32[]{:S(2)}, u32[]{:S(2)}) %collective-permute-start.6) | collective-permute-done | bytes 262176 | tf_op jit(solution)/shard_map/ppermute | solution.py:342
  44.8 3.1 %collective-permute-done.8 = f32[128,512]{1,0:T(8,128)S(1)} collective-permute-done((f32[128,512]{1,0:T(8,128)S(1)}, f32[128,512]{1,0:T(8,128)S(1)}, u32[]{:S(2)}, u32[]{:S(2)}) %collective-permute-start.8) | collective-permute-done | bytes 262176 | tf_op jit(solution)/shard_map/ppermute | solution.py:342
  47.9 1.3 %collective-permute-done.7 = f32[128,512]{1,0:T(8,128)S(1)} collective-permute-done((f32[128,512]{1,0:T(8,128)S(1)}, f32[128,512]{1,0:T(8,128)S(1)}, u32[]{:S(2)}, u32[]{:S(2)}) %collective-permute-start.7) | collective-permute-done | bytes 262176 | tf_op jit(solution)/shard_map/ppermute | solution.py:342
  49.1 0.1 fusion.5.refs_0_
  49.2 2.2 %collective-permute-start.11 = (f32[128,512]{1,0:T(8,128)S(1)}, f32[128,512]{1,0:T(8,128)S(1)}, u32[]{:S(2)}, u32[]{:S(2)}) collective-permute-start(f32[128,512]{1,0:T(8,128)S(1)} %fusion.5.refs_0_), channel_id=1, source_target_pairs={{0,96},{1,25},{2,98},{3,27},{4,100},{5,29},{6,102},{7,31},{8,104},... | collective-permute-start | bytes 786440 | tf_op jit(solution)/shard_map/ppermute | solution.py:342
  51.5 1.1 %collective-permute-start.9 = (f32[128,512]{1,0:T(8,128)S(1)}, f32[128,512]{1,0:T(8,128)S(1)}, u32[]{:S(2)}, u32[]{:S(2)}) collective-permute-start(f32[128,512]{1,0:T(8,128)S(1)} %fusion.5.refs_0_), channel_id=1, source_target_pairs={{0,32},{1,9},{2,34},{3,11},{4,36},{5,13},{6,38},{7,15},{8,40},{9,1... | collective-permute-start | bytes 786440 | tf_op jit(solution)/shard_map/ppermute | solution.py:342
  52.6 6.3 %collective-permute-done.11.refs_3_ = f32[128,512]{1,0:T(8,128)S(1)} collective-permute-done((f32[128,512]{1,0:T(8,128)S(1)}, f32[128,512]{1,0:T(8,128)S(1)}, u32[]{:S(2)}, u32[]{:S(2)}) %collective-permute-start.11) | collective-permute-done | bytes 262176 | tf_op jit(solution)/shard_map/ppermute | solution.py:342
  58.8 0.0 collective-permute-done.10.refs_2_
  58.8 0.6 collective-permute-done.9.refs_1_
  59.5 1.8 %partial_distances.1 = (f32[32,512]{1,0:T(8,128)S(1)}, f32[32,512]{1,0:T(8,128)S(1)}, f32[32,512]{1,0:T(8,128)S(1)}, f32[32,512]{1,0:T(8,128)S(1)}) custom-call(s32[3]{0:T(128)S(1)} %pad_add_fusion.place_ref, f32[128,512]{1,0:T(8,128)S(1)} %fusion.5.refs_0_, f32[128,512]{1,0:T(8,128)S(1)} %collective-permute-done.9.refs_1_, ...), custom_call_target="tpu_custom_call" | custom-call | tf_op jit(solution)/shard_map/partial_distances/pallas_call | solution.py:298
  61.2 0.6 collective-permute-start.12
  61.8 1.3 %collective-permute-start.13 = (f32[32,512]{1,0:T(8,128)S(1)}, f32[32,512]{1,0:T(8,128)S(1)}, u32[]{:S(2)}, u32[]{:S(2)}) collective-permute-start(f32[32,512]{1,0:T(8,128)S(1)} %get-tuple-element.33), channel_id=1, source_target_pairs={{0,8},{1,33},{2,10},{3,35},{4,12},{5,37},{6,14},{7,39},{8,0},{9,41... | collective-permute-start | bytes 196616 | tf_op jit(solution)/shard_map/ppermute | solution.py:342
  63.1 1.5 %collective-permute-start.14 = (f32[32,512]{1,0:T(8,128)S(1)}, f32[32,512]{1,0:T(8,128)S(1)}, u32[]{:S(2)}, u32[]{:S(2)}) collective-permute-start(f32[32,512]{1,0:T(8,128)S(1)} %get-tuple-element.34), channel_id=1, source_target_pairs={{0,24},{1,97},{2,26},{3,99},{4,28},{5,101},{6,30},{7,103},{8,16},{... | collective-permute-start | bytes 196616 | tf_op jit(solution)/shard_map/ppermute | solution.py:342
  64.6 1.5 %collective-permute-done.12 = f32[32,512]{1,0:T(8,128)S(1)} collective-permute-done((f32[32,512]{1,0:T(8,128)S(1)}, f32[32,512]{1,0:T(8,128)S(1)}, u32[]{:S(2)}, u32[]{:S(2)}) %collective-permute-start.12) | collective-permute-done | bytes 65568 | tf_op jit(solution)/shard_map/ppermute | solution.py:342
  66.1 1.3 %collective-permute-done.14 = f32[32,512]{1,0:T(8,128)S(1)} collective-permute-done((f32[32,512]{1,0:T(8,128)S(1)}, f32[32,512]{1,0:T(8,128)S(1)}, u32[]{:S(2)}, u32[]{:S(2)}) %collective-permute-start.14) | collective-permute-done | bytes 65568 | tf_op jit(solution)/shard_map/ppermute | solution.py:342
  67.5 2.6 %collective-permute-start.17 = (f32[32,512]{1,0:T(8,128)S(1)}, f32[32,512]{1,0:T(8,128)S(1)}, u32[]{:S(2)}, u32[]{:S(2)}) collective-permute-start(f32[32,512]{1,0:T(8,128)S(1)} %add_add_fusion.1), channel_id=1, source_target_pairs={{0,6},{1,7},{2,4},{3,5},{4,2},{5,3},{6,0},{7,1},{8,14},{9,15},{10,... | collective-permute-start | bytes 196616 | tf_op jit(solution)/shard_map/ppermute | solution.py:342
  70.0 1.4 %collective-permute-start.15 = (f32[32,512]{1,0:T(8,128)S(1)}, f32[32,512]{1,0:T(8,128)S(1)}, u32[]{:S(2)}, u32[]{:S(2)}) collective-permute-start(f32[32,512]{1,0:T(8,128)S(1)} %add_add_fusion.1), channel_id=1, source_target_pairs={{0,4},{1,5},{2,6},{3,7},{4,0},{5,1},{6,2},{7,3},{8,12},{9,13},{10,... | collective-permute-start | bytes 196616 | tf_op jit(solution)/shard_map/ppermute | solution.py:342
  71.4 0.5 collective-permute-done.17
  71.9 1.3 %collective-permute-done.16 = f32[32,512]{1,0:T(8,128)S(1)} collective-permute-done((f32[32,512]{1,0:T(8,128)S(1)}, f32[32,512]{1,0:T(8,128)S(1)}, u32[]{:S(2)}, u32[]{:S(2)}) %collective-permute-start.16) | collective-permute-done | bytes 65568 | tf_op jit(solution)/shard_map/ppermute | solution.py:342
  73.2 1.5 %collective-permute-done.15 = f32[32,512]{1,0:T(8,128)S(1)} collective-permute-done((f32[32,512]{1,0:T(8,128)S(1)}, f32[32,512]{1,0:T(8,128)S(1)}, u32[]{:S(2)}, u32[]{:S(2)}) %collective-permute-start.15) | collective-permute-done | bytes 65568 | tf_op jit(solution)/shard_map/ppermute | solution.py:342
  74.7 7.8 %collective-permute-start.18 = (f32[32,512]{1,0:T(8,128)S(1)}, f32[32,512]{1,0:T(8,128)S(1)}, u32[]{:S(2)}, u32[]{:S(2)}) collective-permute-start(f32[32,512]{1,0:T(8,128)S(1)} %add_add_fusion), channel_id=1, source_target_pairs={{0,1},{1,0},{2,3},{3,2},{4,5},{5,4},{6,7},{7,6},{8,9},{9,8},{10,11... | collective-permute-start | bytes 196616 | tf_op jit(solution)/shard_map/ppermute | solution.py:342
  82.5 0.9 %collective-permute-done.18 = f32[32,512]{1,0:T(8,128)S(1)} collective-permute-done((f32[32,512]{1,0:T(8,128)S(1)}, f32[32,512]{1,0:T(8,128)S(1)}, u32[]{:S(2)}, u32[]{:S(2)}) %collective-permute-start.18) | collective-permute-done | bytes 65568 | tf_op jit(solution)/shard_map/ppermute | solution.py:342
  83.4 0.6 add.74
  (9 shorter events, 0.1 us)
Async XLA Ops:
  9.4 11.2 %collective-permute-start = (f32[512,256]{1,0:T(8,128)S(1)}, f32[512,256]{1,0:T(8,128)S(1)}, u32[]{:S(2)}, u32[]{:S(2)}) collective-permute-start(f32[512,256]{1,0:T(8,128)S(1)} %get-tuple-element.24), channel_id=1, source_target_pairs={{0,8},{1,33},{2,10},{3,35},{4,12},{5,37},{6,14},{7,39},{8,0},{9,41... | collective-permute-start | bytes 1572872 | tf_op jit(solution)/shard_map/ppermute | solution.py:342
  11.6 9.5 %collective-permute-start.1 = (f32[512,256]{1,0:T(8,128)S(1)}, f32[512,256]{1,0:T(8,128)S(1)}, u32[]{:S(2)}, u32[]{:S(2)}) collective-permute-start(f32[512,256]{1,0:T(8,128)S(1)} %get-tuple-element.25), channel_id=1, source_target_pairs={{0,24},{1,97},{2,26},{3,99},{4,28},{5,101},{6,30},{7,103},{8,16},{... | collective-permute-start | bytes 1572872 | tf_op jit(solution)/shard_map/ppermute | solution.py:342
  19.5 9.8 %collective-permute-start.2 = (f32[512,256]{1,0:T(8,128)S(1)}, f32[512,256]{1,0:T(8,128)S(1)}, u32[]{:S(2)}, u32[]{:S(2)}) collective-permute-start(f32[512,256]{1,0:T(8,128)S(1)} %get-tuple-element.27), channel_id=1, source_target_pairs={{0,8},{1,33},{2,10},{3,35},{4,12},{5,37},{6,14},{7,39},{8,0},{9,41... | collective-permute-start | bytes 1572872 | tf_op jit(solution)/shard_map/ppermute | solution.py:342
  20.0 9.5 %collective-permute-start.3 = (f32[512,256]{1,0:T(8,128)S(1)}, f32[512,256]{1,0:T(8,128)S(1)}, u32[]{:S(2)}, u32[]{:S(2)}) collective-permute-start(f32[512,256]{1,0:T(8,128)S(1)} %get-tuple-element.28), channel_id=1, source_target_pairs={{0,24},{1,97},{2,26},{3,99},{4,28},{5,101},{6,30},{7,103},{8,16},{... | collective-permute-start | bytes 1572872 | tf_op jit(solution)/shard_map/ppermute | solution.py:342
  27.2 9.6 %collective-permute-start.4 = (f32[512,256]{1,0:T(8,128)S(1)}, f32[512,256]{1,0:T(8,128)S(1)}, u32[]{:S(2)}, u32[]{:S(2)}) collective-permute-start(f32[512,256]{1,0:T(8,128)S(1)} %get-tuple-element.29), channel_id=1, source_target_pairs={{0,24},{1,97},{2,26},{3,99},{4,28},{5,101},{6,30},{7,103},{8,16},{... | collective-permute-start | bytes 1572872 | tf_op jit(solution)/shard_map/ppermute | solution.py:342
  29.2 8.3 %collective-permute-start.5 = (f32[512,256]{1,0:T(8,128)S(1)}, f32[512,256]{1,0:T(8,128)S(1)}, u32[]{:S(2)}, u32[]{:S(2)}) collective-permute-start(f32[512,256]{1,0:T(8,128)S(1)} %get-tuple-element.30), channel_id=1, source_target_pairs={{0,8},{1,33},{2,10},{3,35},{4,12},{5,37},{6,14},{7,39},{8,0},{9,41... | collective-permute-start | bytes 1572872 | tf_op jit(solution)/shard_map/ppermute | solution.py:342
  29.5 12.7 %copy-start = (s32[512]{0:T(512)S(1)}, s32[512]{0:T(512)}, u32[]{:S(2)}) copy-start(s32[512]{0:T(512)} %param.9) | copy-start | bytes 6148
  37.8 7.0 %collective-permute-start.6 = (f32[128,512]{1,0:T(8,128)S(1)}, f32[128,512]{1,0:T(8,128)S(1)}, u32[]{:S(2)}, u32[]{:S(2)}) collective-permute-start(f32[128,512]{1,0:T(8,128)S(1)} %get-tuple-element.35), channel_id=1, source_target_pairs={{0,64},{1,17},{2,66},{3,19},{4,68},{5,21},{6,70},{7,23},{8,72},{9,... | collective-permute-start | bytes 786440 | tf_op jit(solution)/shard_map/ppermute | solution.py:342
  41.0 6.9 %collective-permute-start.8 = (f32[128,512]{1,0:T(8,128)S(1)}, f32[128,512]{1,0:T(8,128)S(1)}, u32[]{:S(2)}, u32[]{:S(2)}) collective-permute-start(f32[128,512]{1,0:T(8,128)S(1)} %get-tuple-element.36), channel_id=1, source_target_pairs={{0,96},{1,25},{2,98},{3,27},{4,100},{5,29},{6,102},{7,31},{8,104},... | collective-permute-start | bytes 786440 | tf_op jit(solution)/shard_map/ppermute | solution.py:342
  41.7 7.4 %collective-permute-start.7 = (f32[128,512]{1,0:T(8,128)S(1)}, f32[128,512]{1,0:T(8,128)S(1)}, u32[]{:S(2)}, u32[]{:S(2)}) collective-permute-start(f32[128,512]{1,0:T(8,128)S(1)} %get-tuple-element.37), channel_id=1, source_target_pairs={{0,32},{1,9},{2,34},{3,11},{4,36},{5,13},{6,38},{7,15},{8,40},{9,1... | collective-permute-start | bytes 786440 | tf_op jit(solution)/shard_map/ppermute | solution.py:342
  49.2 9.6 %collective-permute-start.11 = (f32[128,512]{1,0:T(8,128)S(1)}, f32[128,512]{1,0:T(8,128)S(1)}, u32[]{:S(2)}, u32[]{:S(2)}) collective-permute-start(f32[128,512]{1,0:T(8,128)S(1)} %fusion.5.refs_0_), channel_id=1, source_target_pairs={{0,96},{1,25},{2,98},{3,27},{4,100},{5,29},{6,102},{7,31},{8,104},... | collective-permute-start | bytes 786440 | tf_op jit(solution)/shard_map/ppermute | solution.py:342
  51.4 7.4 %collective-permute-start.10 = (f32[128,512]{1,0:T(8,128)S(1)}, f32[128,512]{1,0:T(8,128)S(1)}, u32[]{:S(2)}, u32[]{:S(2)}) collective-permute-start(f32[128,512]{1,0:T(8,128)S(1)} %fusion.5.refs_0_), channel_id=1, source_target_pairs={{0,64},{1,17},{2,66},{3,19},{4,68},{5,21},{6,70},{7,23},{8,72},{9,... | collective-permute-start | bytes 786440 | tf_op jit(solution)/shard_map/ppermute | solution.py:342
  51.5 8.0 %collective-permute-start.9 = (f32[128,512]{1,0:T(8,128)S(1)}, f32[128,512]{1,0:T(8,128)S(1)}, u32[]{:S(2)}, u32[]{:S(2)}) collective-permute-start(f32[128,512]{1,0:T(8,128)S(1)} %fusion.5.refs_0_), channel_id=1, source_target_pairs={{0,32},{1,9},{2,34},{3,11},{4,36},{5,13},{6,38},{7,15},{8,40},{9,1... | collective-permute-start | bytes 786440 | tf_op jit(solution)/shard_map/ppermute | solution.py:342
  61.2 4.9 %collective-permute-start.12 = (f32[32,512]{1,0:T(8,128)S(1)}, f32[32,512]{1,0:T(8,128)S(1)}, u32[]{:S(2)}, u32[]{:S(2)}) collective-permute-start(f32[32,512]{1,0:T(8,128)S(1)} %get-tuple-element.32), channel_id=1, source_target_pairs={{0,16},{1,65},{2,18},{3,67},{4,20},{5,69},{6,22},{7,71},{8,24},{9,... | collective-permute-start | bytes 196616 | tf_op jit(solution)/shard_map/ppermute | solution.py:342
  61.8 4.3 %collective-permute-start.13 = (f32[32,512]{1,0:T(8,128)S(1)}, f32[32,512]{1,0:T(8,128)S(1)}, u32[]{:S(2)}, u32[]{:S(2)}) collective-permute-start(f32[32,512]{1,0:T(8,128)S(1)} %get-tuple-element.33), channel_id=1, source_target_pairs={{0,8},{1,33},{2,10},{3,35},{4,12},{5,37},{6,14},{7,39},{8,0},{9,41... | collective-permute-start | bytes 196616 | tf_op jit(solution)/shard_map/ppermute | solution.py:342
  63.1 4.3 %collective-permute-start.14 = (f32[32,512]{1,0:T(8,128)S(1)}, f32[32,512]{1,0:T(8,128)S(1)}, u32[]{:S(2)}, u32[]{:S(2)}) collective-permute-start(f32[32,512]{1,0:T(8,128)S(1)} %get-tuple-element.34), channel_id=1, source_target_pairs={{0,24},{1,97},{2,26},{3,99},{4,28},{5,101},{6,30},{7,103},{8,16},{... | collective-permute-start | bytes 196616 | tf_op jit(solution)/shard_map/ppermute | solution.py:342
  67.5 4.4 %collective-permute-start.17 = (f32[32,512]{1,0:T(8,128)S(1)}, f32[32,512]{1,0:T(8,128)S(1)}, u32[]{:S(2)}, u32[]{:S(2)}) collective-permute-start(f32[32,512]{1,0:T(8,128)S(1)} %add_add_fusion.1), channel_id=1, source_target_pairs={{0,6},{1,7},{2,4},{3,5},{4,2},{5,3},{6,0},{7,1},{8,14},{9,15},{10,... | collective-permute-start | bytes 196616 | tf_op jit(solution)/shard_map/ppermute | solution.py:342
  70.0 3.1 %collective-permute-start.16 = (f32[32,512]{1,0:T(8,128)S(1)}, f32[32,512]{1,0:T(8,128)S(1)}, u32[]{:S(2)}, u32[]{:S(2)}) collective-permute-start(f32[32,512]{1,0:T(8,128)S(1)} %add_add_fusion.1), channel_id=1, source_target_pairs={{0,2},{1,3},{2,0},{3,1},{4,6},{5,7},{6,4},{7,5},{8,10},{9,11},{10,... | collective-permute-start | bytes 196616 | tf_op jit(solution)/shard_map/ppermute | solution.py:342
  70.0 4.6 %collective-permute-start.15 = (f32[32,512]{1,0:T(8,128)S(1)}, f32[32,512]{1,0:T(8,128)S(1)}, u32[]{:S(2)}, u32[]{:S(2)}) collective-permute-start(f32[32,512]{1,0:T(8,128)S(1)} %add_add_fusion.1), channel_id=1, source_target_pairs={{0,4},{1,5},{2,6},{3,7},{4,0},{5,1},{6,2},{7,3},{8,12},{9,13},{10,... | collective-permute-start | bytes 196616 | tf_op jit(solution)/shard_map/ppermute | solution.py:342
  74.7 8.7 %collective-permute-start.18 = (f32[32,512]{1,0:T(8,128)S(1)}, f32[32,512]{1,0:T(8,128)S(1)}, u32[]{:S(2)}, u32[]{:S(2)}) collective-permute-start(f32[32,512]{1,0:T(8,128)S(1)} %add_add_fusion), channel_id=1, source_target_pairs={{0,1},{1,0},{2,3},{3,2},{4,5},{5,4},{6,7},{7,6},{8,9},{9,8},{10,11... | collective-permute-start | bytes 196616 | tf_op jit(solution)/shard_map/ppermute | solution.py:342

commit v4 on v3

--- a/solution.py
+++ b/solution.py
@@ -15,6 +15,7 @@
 GROUP = K // RING
 OWNED = GROUP // RING
 DEEP = 4
+CHUNKS = [(0, 512), (512, 512), (1024, 1024), (2048, 1024), (3072, 1024)]
 
 TWO_PI = 2.0 * math.pi
 COS = (0.999999989056354, -19.73920449855692, 64.939117412055, -85.45013861233012, 60.16762307755228, -25.967568454490465, 6.528613369785716)
@@ -35,9 +36,10 @@
 
 
 def span_of(place_ref, piece, width):
-    offset, start, size = piece
-    first = (place_ref[0] ^ offset) * width + start
-    return pl.ds(pl.multiple_of(first, size), size)
+    offset, side = piece
+    half = width // 2
+    first = (place_ref[0] ^ offset) * width + ((place_ref[1] // 2) ^ side) * half
+    return pl.ds(pl.multiple_of(first, half), half)
 
 
 def copies_of(place_ref, pieces, width, proj_hbm, into, sems):
@@ -49,18 +51,18 @@
             k = pl.ds(i * deep, deep)
             copies.append(
                 pltpu.make_async_copy(
-                    proj_hbm.at[k, columns], into.at[k, pl.ds(at, piece[2])], sems.at[len(copies)]
+                    proj_hbm.at[k, columns], into.at[k, pl.ds(at, width // 2)], sems.at[len(copies)]
                 )
             )
-        at += piece[2]
+        at += width // 2
     return copies
 
 
 def phases_of(small_ref, place_ref, pieces, width):
-    rows = []
-    for offset, start, size in pieces:
-        first = ((place_ref[0] ^ offset) * width + start) // LANES
-        rows += [small_ref[pl.ds(first + i, 1)] for i in range(size // LANES)]
+    rows, half = [], width // 2
+    for offset, side in pieces:
+        first = ((place_ref[0] ^ offset) * width + ((place_ref[1] // 2) ^ side) * half) // LANES
+        rows += [small_ref[pl.ds(first + i, 1)] for i in range(half // LANES)]
     return jnp.concatenate(rows, axis=1) * (1.0 / TWO_PI)
 
 
@@ -88,26 +90,33 @@
 ):
     docs, depth = emb_hbm.shape
     width = proj.shape[1]
-    half, deep, tile = docs // 2, depth // DEEP, docs // 4
-    columns = span_of(place_ref, (offset, 0, width), width)
+    half, tile = docs // 2, docs // 4
+    pieces = [(offset, 0), (offset, 1)]
     outs = [low_ref, high_ref]
 
     copies, sides = [], (slice(0, half), slice(half, docs))
-    for i in range(DEEP):
-        k = pl.ds(i * deep, deep)
+    for i, (at, size) in enumerate(CHUNKS):
+        k = pl.ds(at, size)
         copies.append(
-            [pltpu.make_async_copy(proj_hbm.at[k, columns], proj.at[k], sems.at[3 * i])]
+            [
+                pltpu.make_async_copy(
+                    proj_hbm.at[k, span_of(place_ref, pieces[side], width)],
+                    proj.at[k, pl.ds(side * (width // 2), width // 2)],
+                    sems.at[4 * i + side],
+                )
+                for side in range(2)
+            ]
             + [
                 pltpu.make_async_copy(
                     emb_hbm.at[pl.ds(side * half, half), k],
                     emb_ref.at[pl.ds(side * half, half), k],
-                    sems.at[3 * i + 1 + side],
+                    sems.at[4 * i + 2 + side],
                 )
                 for side in range(2)
             ]
         )
     ahead = copies_of(
-        place_ref, after, width, proj_hbm, next_ref, sems.at[pl.ds(3 * DEEP, DEEP * len(after))]
+        place_ref, after, width, proj_hbm, next_ref, sems.at[pl.ds(4 * len(CHUNKS), DEEP * len(after))]
     )
     copies.append(ahead)
 
@@ -115,40 +124,32 @@
         for copy in copies[i]:
             copy.start()
 
-    for i in range(2):
+    for i in range(3):
         start(i)
-    row = lax.broadcasted_iota(jnp.int32, (K, 1), 0)
-    group = place_ref[1] ^ (row // GROUP)
-    inner = row % GROUP
-    domain = jnp.where(
-        place_ref[2] == 0,
-        group * GROUP + inner,
-        (inner // OWNED) * GROUP + group * OWNED + inner % OWNED,
-    )
-    domain = domain.astype(jnp.float32)
+    domain = lax.broadcasted_iota(jnp.int32, (K, 1), 0).astype(jnp.float32)
     first_row = RING * width // LANES
     for i in range(docs // LANES):
         ids = small_ref[first_row + i : first_row + i + 1]
         onehot_ref[:, i * LANES : (i + 1) * LANES] = (ids == domain).astype(jnp.bfloat16)
-    phase = phases_of(small_ref, place_ref, [(offset, 0, width)], width)
+    phase = phases_of(small_ref, place_ref, pieces, width)
 
     def multiply(i, side):
-        k = slice(i * deep, (i + 1) * deep)
+        k = slice(CHUNKS[i][0], sum(CHUNKS[i]))
         part = jnp.dot(emb_ref[sides[side], k], proj[k], preferred_element_type=jnp.float32)
         if i == 0:
             angle[sides[side]] = part
         else:
             angle[sides[side]] += part
 
-    for i in range(DEEP):
-        copies[i][0].wait()
-        copies[i][1].wait()
-        if i + 2 <= DEEP:
-            start(i + 2)
+    for i in range(len(CHUNKS)):
+        for copy in copies[i][:3]:
+            copy.wait()
+        if i + 3 <= len(CHUNKS):
+            start(i + 3)
         multiply(i, 0)
-        copies[i][2].wait()
+        copies[i][3].wait()
         multiply(i, 1)
-        if i == DEEP - 1:
+        if i == len(CHUNKS) - 1:
             collect(0, half, angle, phase, onehot_ref, outs)
     collect(half, tile, angle, phase, onehot_ref, outs)
     collect(half + tile, tile, angle, phase, onehot_ref, outs)
@@ -185,12 +186,12 @@
 
 
 def last_kernel(
-    place_ref, small_ref, emb_ref, onehot_ref, proj_ref, low_ref, high_ref, out_ref, angle
+    place_ref, small_ref, emb_ref, onehot_ref, proj_ref, low_ref, high_ref, *rest
 ):
     docs, width = emb_ref.shape[0], proj_ref.shape[1]
-    tile, half = docs // 4, width // 2
-    phase = phases_of(small_ref, place_ref, [(0, 0, width)], width)
-    outs = [out_ref.at[:, :half], out_ref.at[:, half:]]
+    outs, angle = rest[:2], rest[2]
+    tile = docs // 4
+    phase = phases_of(small_ref, place_ref, [(0, 0), (0, 1)], width)
     arrived = [low_ref, high_ref]
     for i in range(4):
         span = slice(i * tile, (i + 1) * tile)
@@ -225,7 +226,7 @@
         scratch_shapes=[
             pltpu.VMEM((depth, width), jnp.bfloat16),
             pltpu.VMEM((docs, width), jnp.float32),
-            pltpu.SemaphoreType.DMA((3 * DEEP + DEEP * len(after),)),
+            pltpu.SemaphoreType.DMA((4 * len(CHUNKS) + DEEP * len(after),)),
         ],
         compiler_params=pltpu.CompilerParams(vmem_limit_bytes=32 << 20),
         cost_estimate=work(docs, depth, width),
@@ -236,7 +237,7 @@
 def next_sums(pieces, after, place, small, emb, onehot, columns, projection, *arrived):
     docs, depth = emb.shape
     width = columns.shape[1]
-    out_shape = [jax.ShapeDtypeStruct((K, size), jnp.float32) for _, _, size in pieces]
+    out_shape = [jax.ShapeDtypeStruct((K, width // 2), jnp.float32) for _ in pieces]
     out_shape.append(jax.ShapeDtypeStruct((depth, width), jnp.bfloat16))
     return pl.pallas_call(
         functools.partial(next_kernel, pieces, after, len(arrived)),
@@ -258,9 +259,9 @@
     width = columns.shape[1]
     return pl.pallas_call(
         last_kernel,
-        out_shape=jax.ShapeDtypeStruct((K, width), jnp.float32),
+        out_shape=[jax.ShapeDtypeStruct((K, width // 2), jnp.float32)] * 2,
         in_specs=[SMEM] + [VMEM] * 6,
-        out_specs=VMEM,
+        out_specs=[VMEM] * 2,
         scratch_shapes=[pltpu.VMEM((docs, width), jnp.float32)],
         compiler_params=pltpu.CompilerParams(vmem_limit_bytes=24 << 20),
         cost_estimate=work(docs, depth, width),
@@ -268,45 +269,48 @@
     )(place, small, emb, onehot, columns, low, high)
 
 
-def distances_kernel(place_ref, *refs):
-    groups, outs, (means, rows) = refs[:RING], refs[RING : 2 * RING], refs[2 * RING :]
-    me1, me2, core = place_ref[0], place_ref[1], place_ref[2]
-    for s in range(RING):
-        group = me2 ^ s
-        for f in range(RING):
-            first = jnp.where(core == 0, group * GROUP + f * OWNED, f * GROUP + group * OWNED)
-            first = pl.multiple_of(first, OWNED)
-            means[pl.ds(first, OWNED)] = groups[s][f * OWNED : (f + 1) * OWNED]
-        owner = pl.multiple_of((me1 ^ s) * OWNED, OWNED)
-        rows[s * OWNED : (s + 1) * OWNED] = groups[0][pl.ds(owner, OWNED)]
+def distances_kernel(place_ref, counts_ref, mine_ref, other_ref, *rest):
+    outs, (means, rows, counts) = rest[:RING], rest[RING:]
+    y, z, core = place_ref[2], place_ref[3], place_ref[4]
+    counts[...] = jnp.broadcast_to(counts_ref[...].astype(jnp.float32), (LANES, K)).T
+    means[:, :LANES] = mine_ref[...] / counts[...]
+    means[:, LANES:] = other_ref[...] / counts[...]
+    part = OWNED // 2
+    for s1 in range(RING):
+        for s2 in range(RING):
+            along_y = y ^ jnp.where(core == 0, s2, s1)
+            along_z = z ^ jnp.where(core == 0, s1, s2)
+            first = pl.multiple_of(((along_y * RING + along_z) * 2 + core) * part, part)
+            spot = (s1 * RING + s2) * part
+            rows[spot : spot + part] = means[pl.ds(first, part)]
     nt = (((1,), (1,)), ((), ()))
     every, picked = means[...], rows[...]
     cross = lax.dot_general(
         picked, every, nt, precision=lax.Precision.HIGHEST, preferred_element_type=jnp.float32
     )
     squares = every * every
-    lanes = sum(squares[:, i : i + 128] for i in range(0, squares.shape[1], 128))
-    norms = jnp.sum(lanes.T, axis=0, keepdims=True)
+    norms = jnp.sum((squares[:, :LANES] + squares[:, LANES:]).T, axis=0, keepdims=True)
     own = jnp.sum(picked * picked, axis=1, keepdims=True)
     partial = own + norms - 2.0 * cross
     for s in range(RING):
-        outs[s][...] = partial[s * OWNED : (s + 1) * OWNED]
-
-
-def partial_distances(place, groups):
-    width = groups[0].shape[1]
+        outs[s][...] = partial[s * RING * part : (s + 1) * RING * part]
+
+
+def partial_distances(place, counts, mine, other):
+    rows = K // 2
     return pl.pallas_call(
         distances_kernel,
-        out_shape=[jax.ShapeDtypeStruct((OWNED, K), jnp.float32)] * RING,
-        in_specs=[SMEM] + [VMEM] * RING,
+        out_shape=[jax.ShapeDtypeStruct((rows // RING, K), jnp.float32)] * RING,
+        in_specs=[SMEM] + [VMEM] * 3,
         out_specs=[VMEM] * RING,
         scratch_shapes=[
-            pltpu.VMEM((K, width), jnp.float32),
-            pltpu.VMEM((GROUP, width), jnp.float32),
+            pltpu.VMEM((K, 2 * LANES), jnp.float32),
+            pltpu.VMEM((rows, 2 * LANES), jnp.float32),
+            pltpu.VMEM((K, LANES), jnp.float32),
         ],
         compiler_params=pltpu.CompilerParams(vmem_limit_bytes=16 << 20),
         name="partial_distances",
-    )(place, *groups)
+    )(place, counts, mine, other)
 
 
 def device(y, z, x, core):
@@ -342,27 +346,19 @@
     return lax.ppermute(value, ("doc", "feat"), pairs)
 
 
-def group_counts(domain_counts, me2, core):
-    by_y = lax.dynamic_slice_in_dim(domain_counts, me2 * GROUP, GROUP)
-    by_z = lax.dynamic_index_in_dim(domain_counts.reshape(RING, RING, OWNED), me2, 1, False)
-    return jnp.where(core == 0, by_y, by_z.reshape(GROUP)).astype(jnp.float32)
-
-
 def per_device(embeddings, projection, phases, domain_ids, domain_counts):
     doc, feat = lax.axis_index("doc"), lax.axis_index("feat")
     y, z, core = doc // RING, doc % RING, feat % 2
     me1 = jnp.where(core == 0, z, y)
     me2 = jnp.where(core == 0, y, z)
-    place = jnp.stack([me1, me2, core]).astype(jnp.int32)
+    place = jnp.stack([me1, me2, y, z, core]).astype(jnp.int32)
+    place, odd = lax.optimization_barrier((place, (me2 & 1) == 1))
     phases, ids = phases.reshape(-1, LANES), domain_ids.reshape(-1, LANES)
     small = jnp.pad(phases, ((0, ids.shape[0]), (0, 0)))
     small = small + jnp.pad(ids, ((phases.shape[0], 0), (0, 0))).astype(jnp.float32)
 
-    width = projection.shape[1] // RING
-    half = width // 2
-    first = [(1, 0, half), (3, half, half)]
-    second = [(3, 0, half), (1, half, half)]
-    kept = [(0, 0, width)]
+    first, second = [(1, 0), (3, 1)], [(3, 0), (1, 1)]
+    kept = [(0, 0), (0, 1)]
     low, high, emb, onehot, columns = first_sums(
         2, first, place, small, embeddings, projection
     )
@@ -375,23 +371,34 @@
         second, kept, place, small, emb, onehot, columns, projection, far_low, far_high
     )
     late_low, late_high = send(low, across_ring(0, 3)), send(high, across_ring(0, 1))
-    sums = last_sums(place, small, emb, onehot, columns, near_low, near_high)
-
-    sums = jnp.concatenate([sums[:, :half] + late_low, sums[:, half:] + late_high], axis=1)
-    sums = sums.reshape(RING, GROUP, width)
-    mine = sums[0]
+    low, high = last_sums(place, small, emb, onehot, columns, near_low, near_high)
+
+    low, high = low + late_low, high + late_high
+    pieces = []
+    for side in (low, high):
+        left, right = side[:, :LANES], side[:, LANES:]
+        pieces += [jnp.where(odd, right, left), jnp.where(odd, left, right)]
+    mine = pieces[0]
     for s in (2, 1, 3):
-        mine = mine + send(sums[s], across_ring(1, s))
-    mine = mine / group_counts(domain_counts, me2, core)[:, None]
-    groups = [mine] + [send(mine, across_ring(1, s)) for s in (1, 2, 3)]
-
-    parts = partial_distances(place, groups)
+        mine = mine + send(pieces[s], across_ring(1, s))
+    other = send(mine, across_core())
+
+    parts = partial_distances(place, domain_counts[None, :], mine, other)
     total = parts[0]
     for s in (2, 1, 3):
         total = total + send(parts[s], across_ring(0, s))
-    across = [send(total, across_x(s)) for s in (2, 1, 3)]
-    total = (total + across[0]) + (across[1] + across[2])
-    return total + send(total, across_core())
+    total = total.reshape(RING, OWNED // 2, K)
+    mine = total[0]
+    for s in (2, 1, 3):
+        mine = mine + send(total[s], across_ring(1, s))
+    near, *far = [send(mine, across_x(s)) for s in (2, 1, 3)]
+    mine = (mine + near) + (far[0] + far[1])
+    theirs = send(mine, across_core())
+    return jnp.where(
+        core == 0,
+        jnp.concatenate([mine, theirs], axis=0),
+        jnp.concatenate([theirs, mine], axis=0),
+    )
 
 
 def solution(mesh):

time: 84.2 us -> 83.9 us (level)
  starting transfers between devices: 30 us -> 30.9 us
    ppermute x19 -> x20, starting transfers between devices: 30 us -> 30.9 us  [send(): return lax.ppermute(value, ('doc', 'feat'), pairs)]
    ppermute x19 -> x20, waiting for transfers between devices: 23.6 us -> 23.1 us  [send(): return lax.ppermute(value, ('doc', 'feat'), pairs)]
  transfers between devices with their start and end apart: 19 -> 20, of which waited for: 15 -> 16; matrix products, arithmetic and copies ran while one was open for 0% -> 0% of each run, Pallas kernels for 21% -> 21%
where the time goes in v4:
time: 83.9 us; the launch traced here: 83.7 us
  starting transfers between devices  30.9 us (37%)
  Pallas kernels  27.7 us (33%)
  waiting for transfers between devices  23.1 us (28%)
  other arithmetic  1.71 us (2%)
    ppermute x20, starting transfers between devices, send(): return lax.ppermute(value, ('doc', 'feat'), pairs)  30.9 us
    ppermute x20, waiting for transfers between devices, send(): return lax.ppermute(value, ('doc', 'feat'), pairs)  23.1 us
    pallas_call x2, Pallas kernels, next_sums(): pl.pallas_call(functools.partial(next_kernel, pieces, after, len(arrived)...  12.1 us
    pallas_call x1, Pallas kernels, first_sums(): pl.pallas_call(functools.partial(first_kernel, offset, after), out_shape=...  8.5 us
    pallas_call x1, Pallas kernels, last_sums(): pl.pallas_call(last_kernel, out_shape=[jax.ShapeDtypeStruct((K, width //...  5.84 us
  transfers between devices with their start and end apart: 20, of which 16 were waited for; matrix products, arithmetic and copies ran while one was open for 0% of the time, Pallas kernels for 21%

profile of v4, /device:TPU:1, one launch (start us, length us, event | category | flops | bytes accessed | tf_op | source)
XLA Modules:
  0.0 83.7 jit_solution(3666389206273532604)
XLA Ops:
  0.0 0.1 stack.23.place_ref
  0.1 0.7 convert_add_fusion.small_ref
  0.8 8.5 %first_sums.1 = (f32[512,256]{1,0:T(8,128)S(1)}, f32[512,256]{1,0:T(8,128)S(1)}, bf16[1024,4096]{1,0:T(8,128)(2,1)S(1)}, bf16[512,1024]{1,0:T(8,128)(2,1)S(1)}, bf16[4096,512]{1,0:T(8,128)(2,1)S(1)}) custom-call(s32[5]{0:T(128)S(1)} %stack.23.place_ref, f32[24,128]{1,0:T(8,128)S(1)} %convert_add_fusion.small_ref, bf16[1024,4096]{1,0:T(8,128)(2,1)} %emb_hbm.1, ...), custom_call_target="tpu_custom_call" | custom-call | flops 4831838208 | bytes 1048576 | tf_op jit(solution)/shard_map/first_sums/pallas_call | solution.py:215
  9.3 2.2 %collective-permute-start = (f32[512,256]{1,0:T(8,128)S(1)}, f32[512,256]{1,0:T(8,128)S(1)}, u32[]{:S(2)}, u32[]{:S(2)}) collective-permute-start(f32[512,256]{1,0:T(8,128)S(1)} %get-tuple-element.30), channel_id=1, source_target_pairs={{0,8},{1,33},{2,10},{3,35},{4,12},{5,37},{6,14},{7,39},{8,0},{9,41... | collective-permute-start | bytes 1572872 | tf_op jit(solution)/shard_map/ppermute | solution.py:346
  11.5 1.9 %collective-permute-start.1 = (f32[512,256]{1,0:T(8,128)S(1)}, f32[512,256]{1,0:T(8,128)S(1)}, u32[]{:S(2)}, u32[]{:S(2)}) collective-permute-start(f32[512,256]{1,0:T(8,128)S(1)} %get-tuple-element.31), channel_id=1, source_target_pairs={{0,24},{1,97},{2,26},{3,99},{4,28},{5,101},{6,30},{7,103},{8,16},{... | collective-permute-start | bytes 1572872 | tf_op jit(solution)/shard_map/ppermute | solution.py:346
  13.4 6.0 %next_sums.2 = (f32[512,256]{1,0:T(8,128)S(1)}, f32[512,256]{1,0:T(8,128)S(1)}, bf16[4096,512]{1,0:T(8,128)(2,1)S(1)}) custom-call(s32[5]{0:T(128)S(1)} %stack.23.place_ref, f32[24,128]{1,0:T(8,128)S(1)} %convert_add_fusion.small_ref, bf16[1024,4096]{1,0:T(8,128)(2,1)S(1)} %get-tuple-element.26.emb_ref, bf16[512,1024]{1,0:T(8,128)(2,1)S(1)} %get-tuple-element.27.onehot_ref, ...), custom_call_target="tpu_custom_call" | custom-call | flops 4831838208 | bytes 1048576 | tf_op jit(solution)/shard_map/next_sums/pallas_call | solution.py:242
  19.4 0.5 collective-permute-start.2
  19.9 0.6 collective-permute-start.3
  20.5 0.0 collective-permute-done.rest_0_
  20.5 0.6 collective-permute-done.1.rest_1_
  21.1 6.1 %next_sums.3 = (f32[512,256]{1,0:T(8,128)S(1)}, f32[512,256]{1,0:T(8,128)S(1)}, bf16[4096,512]{1,0:T(8,128)(2,1)S(1)}) custom-call(s32[5]{0:T(128)S(1)} %stack.23.place_ref, f32[24,128]{1,0:T(8,128)S(1)} %convert_add_fusion.small_ref, bf16[1024,4096]{1,0:T(8,128)(2,1)S(1)} %get-tuple-element.26.emb_ref, bf16[512,1024]{1,0:T(8,128)(2,1)S(1)} %get-tuple-element.27.onehot_ref, ...), custom_call_target="tpu_custom_call" | custom-call | flops 4831838208 | bytes 1048576 | tf_op jit(solution)/shard_map/next_sums/pallas_call | solution.py:242
  27.2 0.1 collective-permute-start.5
  27.3 1.9 %collective-permute-start.4 = (f32[512,256]{1,0:T(8,128)S(1)}, f32[512,256]{1,0:T(8,128)S(1)}, u32[]{:S(2)}, u32[]{:S(2)}) collective-permute-start(f32[512,256]{1,0:T(8,128)S(1)} %get-tuple-element.36), channel_id=1, source_target_pairs={{0,24},{1,97},{2,26},{3,99},{4,28},{5,101},{6,30},{7,103},{8,16},{... | collective-permute-start | bytes 1572872 | tf_op jit(solution)/shard_map/ppermute | solution.py:346
  29.3 0.0 collective-permute-done.2.low_ref
  29.3 0.1 collective-permute-done.3.high_ref
  29.4 5.8 %last_sums.1 = (f32[512,256]{1,0:T(8,128)S(1)}, f32[512,256]{1,0:T(8,128)S(1)}) custom-call(s32[5]{0:T(128)S(1)} %stack.23.place_ref, f32[24,128]{1,0:T(8,128)S(1)} %convert_add_fusion.small_ref, bf16[1024,4096]{1,0:T(8,128)(2,1)S(1)} %get-tuple-element.26.emb_ref, bf16[512,1024]{1,0:T(8,128)(2,1)S(1)} %get-tuple-element.27.onehot_ref, ...), custom_call_target="tpu_custom_call" | custom-call | flops 4831838208 | bytes 1048576 | tf_op jit(solution)/shard_map/last_sums/pallas_call | solution.py:260
  35.3 0.4 collective-permute-done.5
  35.6 0.1 add.61
  35.7 1.2 %collective-permute-done.4 = f32[512,256]{1,0:T(8,128)S(1)} collective-permute-done((f32[512,256]{1,0:T(8,128)S(1)}, f32[512,256]{1,0:T(8,128)S(1)}, u32[]{:S(2)}, u32[]{:S(2)}) %collective-permute-start.4) | collective-permute-done | bytes 524320 | tf_op jit(solution)/shard_map/ppermute | solution.py:346
  36.9 0.1 add.60
  37.0 1.4 %collective-permute-start.7 = (f32[512,128]{1,0:T(8,128)S(1)}, f32[512,128]{1,0:T(8,128)S(1)}, u32[]{:S(2)}, u32[]{:S(2)}) collective-permute-start(f32[512,128]{1,0:T(8,128)S(1)} %slice_select_fusion.2), channel_id=1, source_target_pairs={{0,32},{1,9},{2,34},{3,11},{4,36},{5,13},{6,38},{7,15},{8,40},{9,1... | collective-permute-start | bytes 786440 | tf_op jit(solution)/shard_map/ppermute | solution.py:346
  38.4 3.6 %collective-permute-start.6 = (f32[512,128]{1,0:T(8,128)S(1)}, f32[512,128]{1,0:T(8,128)S(1)}, u32[]{:S(2)}, u32[]{:S(2)}) collective-permute-start(f32[512,128]{1,0:T(8,128)S(1)} %get-tuple-element.43), channel_id=1, source_target_pairs={{0,64},{1,17},{2,66},{3,19},{4,68},{5,21},{6,70},{7,23},{8,72},{9,... | collective-permute-start | bytes 786440 | tf_op jit(solution)/shard_map/ppermute | solution.py:346
  42.0 0.0 collective-permute-start.8
  42.0 0.3 collective-permute-done.7
  42.3 6.6 %collective-permute-done.6 = f32[512,128]{1,0:T(8,128)S(1)} collective-permute-done((f32[512,128]{1,0:T(8,128)S(1)}, f32[512,128]{1,0:T(8,128)S(1)}, u32[]{:S(2)}, u32[]{:S(2)}) %collective-permute-start.6) | collective-permute-done | bytes 262176 | tf_op jit(solution)/shard_map/ppermute | solution.py:346
  48.9 2.6 %collective-permute-done.8 = f32[512,128]{1,0:T(8,128)S(1)} collective-permute-done((f32[512,128]{1,0:T(8,128)S(1)}, f32[512,128]{1,0:T(8,128)S(1)}, u32[]{:S(2)}, u32[]{:S(2)}) %collective-permute-start.8) | collective-permute-done | bytes 262176 | tf_op jit(solution)/shard_map/ppermute | solution.py:346
  51.6 0.1 add_add_fusion.mine_ref
  51.7 3.3 %collective-permute-start.9 = (f32[512,128]{1,0:T(8,128)S(1)}, f32[512,128]{1,0:T(8,128)S(1)}, u32[]{:S(2)}, u32[]{:S(2)}) collective-permute-start(f32[512,128]{1,0:T(8,128)S(1)} %add_add_fusion.mine_ref), channel_id=1, source_target_pairs={{0,1},{1,0},{2,3},{3,2},{4,5},{5,4},{6,7},{7,6},{8,9},{9,8},{10,11... | collective-permute-start | bytes 786440 | tf_op jit(solution)/shard_map/ppermute | solution.py:346
  55.0 1.2 %collective-permute-done.9.other_ref = f32[512,128]{1,0:T(8,128)S(1)} collective-permute-done((f32[512,128]{1,0:T(8,128)S(1)}, f32[512,128]{1,0:T(8,128)S(1)}, u32[]{:S(2)}, u32[]{:S(2)}) %collective-permute-start.9) | collective-permute-done | bytes 262176 | tf_op jit(solution)/shard_map/ppermute | solution.py:346
  56.1 1.3 %partial_distances.1 = (f32[64,512]{1,0:T(8,128)S(1)}, f32[64,512]{1,0:T(8,128)S(1)}, f32[64,512]{1,0:T(8,128)S(1)}, f32[64,512]{1,0:T(8,128)S(1)}) custom-call(s32[5]{0:T(128)S(1)} %stack.23.place_ref, s32[1,512]{1,0:T(1,128)S(1)} %bitcast.8, f32[512,128]{1,0:T(8,128)S(1)} %add_add_fusion.mine_ref, f32[512,128]{1,0:T(8,128)S(1)} %collective-permute-done.9.other_ref), custom_call_target="tpu_custom_call" | custom-call | tf_op jit(solution)/shard_map/partial_distances/pallas_call | solution.py:301
  57.4 0.1 collective-permute-start.10
  57.5 0.5 collective-permute-start.11
  58.0 2.7 %collective-permute-start.12 = (f32[64,512]{1,0:T(8,128)S(1)}, f32[64,512]{1,0:T(8,128)S(1)}, u32[]{:S(2)}, u32[]{:S(2)}) collective-permute-start(f32[64,512]{1,0:T(8,128)S(1)} %get-tuple-element.42), channel_id=1, source_target_pairs={{0,24},{1,97},{2,26},{3,99},{4,28},{5,101},{6,30},{7,103},{8,16},{... | collective-permute-start | bytes 393224 | tf_op jit(solution)/shard_map/ppermute | solution.py:346
  60.8 2.4 %collective-permute-done.10 = f32[64,512]{1,0:T(8,128)S(1)} collective-permute-done((f32[64,512]{1,0:T(8,128)S(1)}, f32[64,512]{1,0:T(8,128)S(1)}, u32[]{:S(2)}, u32[]{:S(2)}) %collective-permute-start.10) | collective-permute-done | bytes 131104 | tf_op jit(solution)/shard_map/ppermute | solution.py:346
  63.1 1.1 %collective-permute-done.12 = f32[64,512]{1,0:T(8,128)S(1)} collective-permute-done((f32[64,512]{1,0:T(8,128)S(1)}, f32[64,512]{1,0:T(8,128)S(1)}, u32[]{:S(2)}, u32[]{:S(2)}) %collective-permute-start.12) | collective-permute-done | bytes 131104 | tf_op jit(solution)/shard_map/ppermute | solution.py:346
  64.3 2.2 %collective-permute-start.13 = (f32[16,512]{1,0:T(8,128)S(1)}, f32[16,512]{1,0:T(8,128)S(1)}, u32[]{:S(2)}, u32[]{:S(2)}) collective-permute-start(f32[16,512]{1,0:T(8,128)S(1)} %get-tuple-element.45), channel_id=1, source_target_pairs={{0,64},{1,17},{2,66},{3,19},{4,68},{5,21},{6,70},{7,23},{8,72},{9,... | collective-permute-start | bytes 98312 | tf_op jit(solution)/shard_map/ppermute | solution.py:346
  66.6 0.5 collective-permute-start.15
  67.1 0.5 collective-permute-start.14
  67.6 1.1 %collective-permute-done.13 = f32[16,512]{1,0:T(8,128)S(1)} collective-permute-done((f32[16,512]{1,0:T(8,128)S(1)}, f32[16,512]{1,0:T(8,128)S(1)}, u32[]{:S(2)}, u32[]{:S(2)}) %collective-permute-start.13) | collective-permute-done | bytes 32800 | tf_op jit(solution)/shard_map/ppermute | solution.py:346
  68.7 1.9 %collective-permute-done.15 = f32[16,512]{1,0:T(8,128)S(1)} collective-permute-done((f32[16,512]{1,0:T(8,128)S(1)}, f32[16,512]{1,0:T(8,128)S(1)}, u32[]{:S(2)}, u32[]{:S(2)}) %collective-permute-start.15) | collective-permute-done | bytes 32800 | tf_op jit(solution)/shard_map/ppermute | solution.py:346
  70.6 2.5 %collective-permute-start.18 = (f32[16,512]{1,0:T(8,128)S(1)}, f32[16,512]{1,0:T(8,128)S(1)}, u32[]{:S(2)}, u32[]{:S(2)}) collective-permute-start(f32[16,512]{1,0:T(8,128)S(1)} %fusion.1), channel_id=1, source_target_pairs={{0,6},{1,7},{2,4},{3,5},{4,2},{5,3},{6,0},{7,1},{8,14},{9,15},{10,... | collective-permute-start | bytes 98312 | tf_op jit(solution)/shard_map/ppermute | solution.py:346
  73.1 1.4 %collective-permute-start.16 = (f32[16,512]{1,0:T(8,128)S(1)}, f32[16,512]{1,0:T(8,128)S(1)}, u32[]{:S(2)}, u32[]{:S(2)}) collective-permute-start(f32[16,512]{1,0:T(8,128)S(1)} %fusion.1), channel_id=1, source_target_pairs={{0,4},{1,5},{2,6},{3,7},{4,0},{5,1},{6,2},{7,3},{8,12},{9,13},{10,... | collective-permute-start | bytes 98312 | tf_op jit(solution)/shard_map/ppermute | solution.py:346
  74.5 0.1 collective-permute-done.18
  74.6 1.3 %collective-permute-done.17 = f32[16,512]{1,0:T(8,128)S(1)} collective-permute-done((f32[16,512]{1,0:T(8,128)S(1)}, f32[16,512]{1,0:T(8,128)S(1)}, u32[]{:S(2)}, u32[]{:S(2)}) %collective-permute-start.17) | collective-permute-done | bytes 32800 | tf_op jit(solution)/shard_map/ppermute | solution.py:346
  75.9 1.5 %collective-permute-done.16 = f32[16,512]{1,0:T(8,128)S(1)} collective-permute-done((f32[16,512]{1,0:T(8,128)S(1)}, f32[16,512]{1,0:T(8,128)S(1)}, u32[]{:S(2)}, u32[]{:S(2)}) %collective-permute-start.16) | collective-permute-done | bytes 32800 | tf_op jit(solution)/shard_map/ppermute | solution.py:346
  77.4 4.8 %collective-permute-start.19 = (f32[16,512]{1,0:T(8,128)S(1)}, f32[16,512]{1,0:T(8,128)S(1)}, u32[]{:S(2)}, u32[]{:S(2)}) collective-permute-start(f32[16,512]{1,0:T(8,128)S(1)} %add_add_fusion.2), channel_id=1, source_target_pairs={{0,1},{1,0},{2,3},{3,2},{4,5},{5,4},{6,7},{7,6},{8,9},{9,8},{10,11... | collective-permute-start | bytes 98312 | tf_op jit(solution)/shard_map/ppermute | solution.py:346
  82.2 0.9 %collective-permute-done.19 = f32[16,512]{1,0:T(8,128)S(1)} collective-permute-done((f32[16,512]{1,0:T(8,128)S(1)}, f32[16,512]{1,0:T(8,128)S(1)}, u32[]{:S(2)}, u32[]{:S(2)}) %collective-permute-start.19) | collective-permute-done | bytes 32800 | tf_op jit(solution)/shard_map/ppermute | solution.py:346
  83.1 0.6 maximum_select_fusion
  (11 shorter events, 0.2 us)
Async XLA Ops:
  9.3 11.2 %collective-permute-start = (f32[512,256]{1,0:T(8,128)S(1)}, f32[512,256]{1,0:T(8,128)S(1)}, u32[]{:S(2)}, u32[]{:S(2)}) collective-permute-start(f32[512,256]{1,0:T(8,128)S(1)} %get-tuple-element.30), channel_id=1, source_target_pairs={{0,8},{1,33},{2,10},{3,35},{4,12},{5,37},{6,14},{7,39},{8,0},{9,41... | collective-permute-start | bytes 1572872 | tf_op jit(solution)/shard_map/ppermute | solution.py:346
  11.5 9.5 %collective-permute-start.1 = (f32[512,256]{1,0:T(8,128)S(1)}, f32[512,256]{1,0:T(8,128)S(1)}, u32[]{:S(2)}, u32[]{:S(2)}) collective-permute-start(f32[512,256]{1,0:T(8,128)S(1)} %get-tuple-element.31), channel_id=1, source_target_pairs={{0,24},{1,97},{2,26},{3,99},{4,28},{5,101},{6,30},{7,103},{8,16},{... | collective-permute-start | bytes 1572872 | tf_op jit(solution)/shard_map/ppermute | solution.py:346
  19.4 9.9 %collective-permute-start.2 = (f32[512,256]{1,0:T(8,128)S(1)}, f32[512,256]{1,0:T(8,128)S(1)}, u32[]{:S(2)}, u32[]{:S(2)}) collective-permute-start(f32[512,256]{1,0:T(8,128)S(1)} %get-tuple-element.33), channel_id=1, source_target_pairs={{0,8},{1,33},{2,10},{3,35},{4,12},{5,37},{6,14},{7,39},{8,0},{9,41... | collective-permute-start | bytes 1572872 | tf_op jit(solution)/shard_map/ppermute | solution.py:346
  19.9 9.5 %collective-permute-start.3 = (f32[512,256]{1,0:T(8,128)S(1)}, f32[512,256]{1,0:T(8,128)S(1)}, u32[]{:S(2)}, u32[]{:S(2)}) collective-permute-start(f32[512,256]{1,0:T(8,128)S(1)} %get-tuple-element.34), channel_id=1, source_target_pairs={{0,24},{1,97},{2,26},{3,99},{4,28},{5,101},{6,30},{7,103},{8,16},{... | collective-permute-start | bytes 1572872 | tf_op jit(solution)/shard_map/ppermute | solution.py:346
  27.2 8.4 %collective-permute-start.5 = (f32[512,256]{1,0:T(8,128)S(1)}, f32[512,256]{1,0:T(8,128)S(1)}, u32[]{:S(2)}, u32[]{:S(2)}) collective-permute-start(f32[512,256]{1,0:T(8,128)S(1)} %get-tuple-element.38), channel_id=1, source_target_pairs={{0,8},{1,33},{2,10},{3,35},{4,12},{5,37},{6,14},{7,39},{8,0},{9,41... | collective-permute-start | bytes 1572872 | tf_op jit(solution)/shard_map/ppermute | solution.py:346
  27.3 9.6 %collective-permute-start.4 = (f32[512,256]{1,0:T(8,128)S(1)}, f32[512,256]{1,0:T(8,128)S(1)}, u32[]{:S(2)}, u32[]{:S(2)}) collective-permute-start(f32[512,256]{1,0:T(8,128)S(1)} %get-tuple-element.36), channel_id=1, source_target_pairs={{0,24},{1,97},{2,26},{3,99},{4,28},{5,101},{6,30},{7,103},{8,16},{... | collective-permute-start | bytes 1572872 | tf_op jit(solution)/shard_map/ppermute | solution.py:346
  29.4 26.7 %copy-start = (s32[512]{0:T(512)S(1)}, s32[512]{0:T(512)}, u32[]{:S(2)}) copy-start(s32[512]{0:T(512)} %param.9) | copy-start | bytes 6148
  37.0 5.3 %collective-permute-start.7 = (f32[512,128]{1,0:T(8,128)S(1)}, f32[512,128]{1,0:T(8,128)S(1)}, u32[]{:S(2)}, u32[]{:S(2)}) collective-permute-start(f32[512,128]{1,0:T(8,128)S(1)} %slice_select_fusion.2), channel_id=1, source_target_pairs={{0,32},{1,9},{2,34},{3,11},{4,36},{5,13},{6,38},{7,15},{8,40},{9,1... | collective-permute-start | bytes 786440 | tf_op jit(solution)/shard_map/ppermute | solution.py:346
  38.4 10.5 %collective-permute-start.6 = (f32[512,128]{1,0:T(8,128)S(1)}, f32[512,128]{1,0:T(8,128)S(1)}, u32[]{:S(2)}, u32[]{:S(2)}) collective-permute-start(f32[512,128]{1,0:T(8,128)S(1)} %get-tuple-element.43), channel_id=1, source_target_pairs={{0,64},{1,17},{2,66},{3,19},{4,68},{5,21},{6,70},{7,23},{8,72},{9,... | collective-permute-start | bytes 786440 | tf_op jit(solution)/shard_map/ppermute | solution.py:346
  42.0 9.5 %collective-permute-start.8 = (f32[512,128]{1,0:T(8,128)S(1)}, f32[512,128]{1,0:T(8,128)S(1)}, u32[]{:S(2)}, u32[]{:S(2)}) collective-permute-start(f32[512,128]{1,0:T(8,128)S(1)} %get-tuple-element.44), channel_id=1, source_target_pairs={{0,96},{1,25},{2,98},{3,27},{4,100},{5,29},{6,102},{7,31},{8,104},... | collective-permute-start | bytes 786440 | tf_op jit(solution)/shard_map/ppermute | solution.py:346
  51.7 4.5 %collective-permute-start.9 = (f32[512,128]{1,0:T(8,128)S(1)}, f32[512,128]{1,0:T(8,128)S(1)}, u32[]{:S(2)}, u32[]{:S(2)}) collective-permute-start(f32[512,128]{1,0:T(8,128)S(1)} %add_add_fusion.mine_ref), channel_id=1, source_target_pairs={{0,1},{1,0},{2,3},{3,2},{4,5},{5,4},{6,7},{7,6},{8,9},{9,8},{10,11... | collective-permute-start | bytes 786440 | tf_op jit(solution)/shard_map/ppermute | solution.py:346
  57.4 5.7 %collective-permute-start.10 = (f32[64,512]{1,0:T(8,128)S(1)}, f32[64,512]{1,0:T(8,128)S(1)}, u32[]{:S(2)}, u32[]{:S(2)}) collective-permute-start(f32[64,512]{1,0:T(8,128)S(1)} %get-tuple-element.40), channel_id=1, source_target_pairs={{0,16},{1,65},{2,18},{3,67},{4,20},{5,69},{6,22},{7,71},{8,24},{9,... | collective-permute-start | bytes 393224 | tf_op jit(solution)/shard_map/ppermute | solution.py:346
  57.5 5.6 %collective-permute-start.11 = (f32[64,512]{1,0:T(8,128)S(1)}, f32[64,512]{1,0:T(8,128)S(1)}, u32[]{:S(2)}, u32[]{:S(2)}) collective-permute-start(f32[64,512]{1,0:T(8,128)S(1)} %get-tuple-element.41), channel_id=1, source_target_pairs={{0,8},{1,33},{2,10},{3,35},{4,12},{5,37},{6,14},{7,39},{8,0},{9,41... | collective-permute-start | bytes 393224 | tf_op jit(solution)/shard_map/ppermute | solution.py:346
  58.0 6.2 %collective-permute-start.12 = (f32[64,512]{1,0:T(8,128)S(1)}, f32[64,512]{1,0:T(8,128)S(1)}, u32[]{:S(2)}, u32[]{:S(2)}) collective-permute-start(f32[64,512]{1,0:T(8,128)S(1)} %get-tuple-element.42), channel_id=1, source_target_pairs={{0,24},{1,97},{2,26},{3,99},{4,28},{5,101},{6,30},{7,103},{8,16},{... | collective-permute-start | bytes 393224 | tf_op jit(solution)/shard_map/ppermute | solution.py:346
  64.3 4.3 %collective-permute-start.13 = (f32[16,512]{1,0:T(8,128)S(1)}, f32[16,512]{1,0:T(8,128)S(1)}, u32[]{:S(2)}, u32[]{:S(2)}) collective-permute-start(f32[16,512]{1,0:T(8,128)S(1)} %get-tuple-element.45), channel_id=1, source_target_pairs={{0,64},{1,17},{2,66},{3,19},{4,68},{5,21},{6,70},{7,23},{8,72},{9,... | collective-permute-start | bytes 98312 | tf_op jit(solution)/shard_map/ppermute | solution.py:346
  66.6 4.0 %collective-permute-start.15 = (f32[16,512]{1,0:T(8,128)S(1)}, f32[16,512]{1,0:T(8,128)S(1)}, u32[]{:S(2)}, u32[]{:S(2)}) collective-permute-start(f32[16,512]{1,0:T(8,128)S(1)} %get-tuple-element.46), channel_id=1, source_target_pairs={{0,96},{1,25},{2,98},{3,27},{4,100},{5,29},{6,102},{7,31},{8,104},... | collective-permute-start | bytes 98312 | tf_op jit(solution)/shard_map/ppermute | solution.py:346
  67.1 3.4 %collective-permute-start.14 = (f32[16,512]{1,0:T(8,128)S(1)}, f32[16,512]{1,0:T(8,128)S(1)}, u32[]{:S(2)}, u32[]{:S(2)}) collective-permute-start(f32[16,512]{1,0:T(8,128)S(1)} %get-tuple-element.47), channel_id=1, source_target_pairs={{0,32},{1,9},{2,34},{3,11},{4,36},{5,13},{6,38},{7,15},{8,40},{9,1... | collective-permute-start | bytes 98312 | tf_op jit(solution)/shard_map/ppermute | solution.py:346
  70.6 4.1 %collective-permute-start.18 = (f32[16,512]{1,0:T(8,128)S(1)}, f32[16,512]{1,0:T(8,128)S(1)}, u32[]{:S(2)}, u32[]{:S(2)}) collective-permute-start(f32[16,512]{1,0:T(8,128)S(1)} %fusion.1), channel_id=1, source_target_pairs={{0,6},{1,7},{2,4},{3,5},{4,2},{5,3},{6,0},{7,1},{8,14},{9,15},{10,... | collective-permute-start | bytes 98312 | tf_op jit(solution)/shard_map/ppermute | solution.py:346
  73.1 2.8 %collective-permute-start.17 = (f32[16,512]{1,0:T(8,128)S(1)}, f32[16,512]{1,0:T(8,128)S(1)}, u32[]{:S(2)}, u32[]{:S(2)}) collective-permute-start(f32[16,512]{1,0:T(8,128)S(1)} %fusion.1), channel_id=1, source_target_pairs={{0,2},{1,3},{2,0},{3,1},{4,6},{5,7},{6,4},{7,5},{8,10},{9,11},{10,... | collective-permute-start | bytes 98312 | tf_op jit(solution)/shard_map/ppermute | solution.py:346
  73.1 4.3 %collective-permute-start.16 = (f32[16,512]{1,0:T(8,128)S(1)}, f32[16,512]{1,0:T(8,128)S(1)}, u32[]{:S(2)}, u32[]{:S(2)}) collective-permute-start(f32[16,512]{1,0:T(8,128)S(1)} %fusion.1), channel_id=1, source_target_pairs={{0,4},{1,5},{2,6},{3,7},{4,0},{5,1},{6,2},{7,3},{8,12},{9,13},{10,... | collective-permute-start | bytes 98312 | tf_op jit(solution)/shard_map/ppermute | solution.py:346
  77.4 5.7 %collective-permute-start.19 = (f32[16,512]{1,0:T(8,128)S(1)}, f32[16,512]{1,0:T(8,128)S(1)}, u32[]{:S(2)}, u32[]{:S(2)}) collective-permute-start(f32[16,512]{1,0:T(8,128)S(1)} %add_add_fusion.2), channel_id=1, source_target_pairs={{0,1},{1,0},{2,3},{3,2},{4,5},{5,4},{6,7},{7,6},{8,9},{9,8},{10,11... | collective-permute-start | bytes 98312 | tf_op jit(solution)/shard_map/ppermute | solution.py:346

commit v5 on v4

--- a/solution.py
+++ b/solution.py
@@ -391,8 +391,8 @@
     mine = total[0]
     for s in (2, 1, 3):
         mine = mine + send(total[s], across_ring(1, s))
-    near, *far = [send(mine, across_x(s)) for s in (2, 1, 3)]
-    mine = (mine + near) + (far[0] + far[1])
+    first, third, second = [send(mine, across_x(s)) for s in (1, 3, 2)]
+    mine = (first + third) + (mine + second)
     theirs = send(mine, across_core())
     return jnp.where(
         core == 0,

time: 83.9 us -> 83.6 us (level)
  transfers between devices with their start and end apart: 20 -> 20, of which waited for: 16 -> 15; matrix products, arithmetic and copies ran while one was open for 0% -> 0% of each run, Pallas kernels for 21% -> 21%
where the time goes in v5:
time: 83.6 us; the launch traced here: 83.5 us
  starting transfers between devices  30.5 us (36%)
  Pallas kernels  27.7 us (33%)
  waiting for transfers between devices  23.3 us (28%)
  other arithmetic  1.71 us (2%)
    ppermute x20, starting transfers between devices, send(): return lax.ppermute(value, ('doc', 'feat'), pairs)  30.5 us
    ppermute x20, waiting for transfers between devices, send(): return lax.ppermute(value, ('doc', 'feat'), pairs)  23.3 us
    pallas_call x2, Pallas kernels, next_sums(): pl.pallas_call(functools.partial(next_kernel, pieces, after, len(arrived)...  12.1 us
    pallas_call x1, Pallas kernels, first_sums(): pl.pallas_call(functools.partial(first_kernel, offset, after), out_shape=...  8.5 us
    pallas_call x1, Pallas kernels, last_sums(): pl.pallas_call(last_kernel, out_shape=[jax.ShapeDtypeStruct((K, width //...  5.84 us
  transfers between devices with their start and end apart: 20, of which 15 were waited for; matrix products, arithmetic and copies ran while one was open for 0% of the time, Pallas kernels for 21%

profile of v5, /device:TPU:1, one launch (start us, length us, event | category | flops | bytes accessed | tf_op | source)
XLA Modules:
  0.0 83.5 jit_solution(2165123314305733735)
XLA Ops:
  0.0 0.1 stack.23.place_ref
  0.1 0.7 convert_add_fusion.small_ref
  0.8 8.5 %first_sums.1 = (f32[512,256]{1,0:T(8,128)S(1)}, f32[512,256]{1,0:T(8,128)S(1)}, bf16[1024,4096]{1,0:T(8,128)(2,1)S(1)}, bf16[512,1024]{1,0:T(8,128)(2,1)S(1)}, bf16[4096,512]{1,0:T(8,128)(2,1)S(1)}) custom-call(s32[5]{0:T(128)S(1)} %stack.23.place_ref, f32[24,128]{1,0:T(8,128)S(1)} %convert_add_fusion.small_ref, bf16[1024,4096]{1,0:T(8,128)(2,1)} %emb_hbm.1, ...), custom_call_target="tpu_custom_call" | custom-call | flops 4831838208 | bytes 1048576 | tf_op jit(solution)/shard_map/first_sums/pallas_call | solution.py:215
  9.3 2.2 %collective-permute-start = (f32[512,256]{1,0:T(8,128)S(1)}, f32[512,256]{1,0:T(8,128)S(1)}, u32[]{:S(2)}, u32[]{:S(2)}) collective-permute-start(f32[512,256]{1,0:T(8,128)S(1)} %get-tuple-element.30), channel_id=1, source_target_pairs={{0,8},{1,33},{2,10},{3,35},{4,12},{5,37},{6,14},{7,39},{8,0},{9,41... | collective-permute-start | bytes 1572872 | tf_op jit(solution)/shard_map/ppermute | solution.py:346
  11.5 1.9 %collective-permute-start.1 = (f32[512,256]{1,0:T(8,128)S(1)}, f32[512,256]{1,0:T(8,128)S(1)}, u32[]{:S(2)}, u32[]{:S(2)}) collective-permute-start(f32[512,256]{1,0:T(8,128)S(1)} %get-tuple-element.31), channel_id=1, source_target_pairs={{0,24},{1,97},{2,26},{3,99},{4,28},{5,101},{6,30},{7,103},{8,16},{... | collective-permute-start | bytes 1572872 | tf_op jit(solution)/shard_map/ppermute | solution.py:346
  13.4 6.0 %next_sums.2 = (f32[512,256]{1,0:T(8,128)S(1)}, f32[512,256]{1,0:T(8,128)S(1)}, bf16[4096,512]{1,0:T(8,128)(2,1)S(1)}) custom-call(s32[5]{0:T(128)S(1)} %stack.23.place_ref, f32[24,128]{1,0:T(8,128)S(1)} %convert_add_fusion.small_ref, bf16[1024,4096]{1,0:T(8,128)(2,1)S(1)} %get-tuple-element.26.emb_ref, bf16[512,1024]{1,0:T(8,128)(2,1)S(1)} %get-tuple-element.27.onehot_ref, ...), custom_call_target="tpu_custom_call" | custom-call | flops 4831838208 | bytes 1048576 | tf_op jit(solution)/shard_map/next_sums/pallas_call | solution.py:242
  19.4 0.5 collective-permute-start.2
  19.9 0.6 collective-permute-start.3
  20.5 0.0 collective-permute-done.rest_0_
  20.5 0.6 collective-permute-done.1.rest_1_
  21.1 6.1 %next_sums.3 = (f32[512,256]{1,0:T(8,128)S(1)}, f32[512,256]{1,0:T(8,128)S(1)}, bf16[4096,512]{1,0:T(8,128)(2,1)S(1)}) custom-call(s32[5]{0:T(128)S(1)} %stack.23.place_ref, f32[24,128]{1,0:T(8,128)S(1)} %convert_add_fusion.small_ref, bf16[1024,4096]{1,0:T(8,128)(2,1)S(1)} %get-tuple-element.26.emb_ref, bf16[512,1024]{1,0:T(8,128)(2,1)S(1)} %get-tuple-element.27.onehot_ref, ...), custom_call_target="tpu_custom_call" | custom-call | flops 4831838208 | bytes 1048576 | tf_op jit(solution)/shard_map/next_sums/pallas_call | solution.py:242
  27.2 0.1 collective-permute-start.5
  27.3 1.9 %collective-permute-start.4 = (f32[512,256]{1,0:T(8,128)S(1)}, f32[512,256]{1,0:T(8,128)S(1)}, u32[]{:S(2)}, u32[]{:S(2)}) collective-permute-start(f32[512,256]{1,0:T(8,128)S(1)} %get-tuple-element.36), channel_id=1, source_target_pairs={{0,24},{1,97},{2,26},{3,99},{4,28},{5,101},{6,30},{7,103},{8,16},{... | collective-permute-start | bytes 1572872 | tf_op jit(solution)/shard_map/ppermute | solution.py:346
  29.3 0.0 collective-permute-done.2.low_ref
  29.3 0.1 collective-permute-done.3.high_ref
  29.4 5.8 %last_sums.1 = (f32[512,256]{1,0:T(8,128)S(1)}, f32[512,256]{1,0:T(8,128)S(1)}) custom-call(s32[5]{0:T(128)S(1)} %stack.23.place_ref, f32[24,128]{1,0:T(8,128)S(1)} %convert_add_fusion.small_ref, bf16[1024,4096]{1,0:T(8,128)(2,1)S(1)} %get-tuple-element.26.emb_ref, bf16[512,1024]{1,0:T(8,128)(2,1)S(1)} %get-tuple-element.27.onehot_ref, ...), custom_call_target="tpu_custom_call" | custom-call | flops 4831838208 | bytes 1048576 | tf_op jit(solution)/shard_map/last_sums/pallas_call | solution.py:260
  35.3 0.4 collective-permute-done.5
  35.6 0.1 add.61
  35.7 1.2 %collective-permute-done.4 = f32[512,256]{1,0:T(8,128)S(1)} collective-permute-done((f32[512,256]{1,0:T(8,128)S(1)}, f32[512,256]{1,0:T(8,128)S(1)}, u32[]{:S(2)}, u32[]{:S(2)}) %collective-permute-start.4) | collective-permute-done | bytes 524320 | tf_op jit(solution)/shard_map/ppermute | solution.py:346
  36.9 0.1 add.60
  37.0 1.4 %collective-permute-start.7 = (f32[512,128]{1,0:T(8,128)S(1)}, f32[512,128]{1,0:T(8,128)S(1)}, u32[]{:S(2)}, u32[]{:S(2)}) collective-permute-start(f32[512,128]{1,0:T(8,128)S(1)} %slice_select_fusion.2), channel_id=1, source_target_pairs={{0,32},{1,9},{2,34},{3,11},{4,36},{5,13},{6,38},{7,15},{8,40},{9,1... | collective-permute-start | bytes 786440 | tf_op jit(solution)/shard_map/ppermute | solution.py:346
  38.4 3.6 %collective-permute-start.6 = (f32[512,128]{1,0:T(8,128)S(1)}, f32[512,128]{1,0:T(8,128)S(1)}, u32[]{:S(2)}, u32[]{:S(2)}) collective-permute-start(f32[512,128]{1,0:T(8,128)S(1)} %get-tuple-element.43), channel_id=1, source_target_pairs={{0,64},{1,17},{2,66},{3,19},{4,68},{5,21},{6,70},{7,23},{8,72},{9,... | collective-permute-start | bytes 786440 | tf_op jit(solution)/shard_map/ppermute | solution.py:346
  42.0 0.3 collective-permute-done.7
  42.3 6.6 %collective-permute-done.6 = f32[512,128]{1,0:T(8,128)S(1)} collective-permute-done((f32[512,128]{1,0:T(8,128)S(1)}, f32[512,128]{1,0:T(8,128)S(1)}, u32[]{:S(2)}, u32[]{:S(2)}) %collective-permute-start.6) | collective-permute-done | bytes 262176 | tf_op jit(solution)/shard_map/ppermute | solution.py:346
  48.9 2.6 %collective-permute-done.8 = f32[512,128]{1,0:T(8,128)S(1)} collective-permute-done((f32[512,128]{1,0:T(8,128)S(1)}, f32[512,128]{1,0:T(8,128)S(1)}, u32[]{:S(2)}, u32[]{:S(2)}) %collective-permute-start.8) | collective-permute-done | bytes 262176 | tf_op jit(solution)/shard_map/ppermute | solution.py:346
  51.6 0.1 add_add_fusion.mine_ref
  51.7 3.3 %collective-permute-start.9 = (f32[512,128]{1,0:T(8,128)S(1)}, f32[512,128]{1,0:T(8,128)S(1)}, u32[]{:S(2)}, u32[]{:S(2)}) collective-permute-start(f32[512,128]{1,0:T(8,128)S(1)} %add_add_fusion.mine_ref), channel_id=1, source_target_pairs={{0,1},{1,0},{2,3},{3,2},{4,5},{5,4},{6,7},{7,6},{8,9},{9,8},{10,11... | collective-permute-start | bytes 786440 | tf_op jit(solution)/shard_map/ppermute | solution.py:346
  55.0 1.2 %collective-permute-done.9.other_ref = f32[512,128]{1,0:T(8,128)S(1)} collective-permute-done((f32[512,128]{1,0:T(8,128)S(1)}, f32[512,128]{1,0:T(8,128)S(1)}, u32[]{:S(2)}, u32[]{:S(2)}) %collective-permute-start.9) | collective-permute-done | bytes 262176 | tf_op jit(solution)/shard_map/ppermute | solution.py:346
  56.1 1.3 %partial_distances.1 = (f32[64,512]{1,0:T(8,128)S(1)}, f32[64,512]{1,0:T(8,128)S(1)}, f32[64,512]{1,0:T(8,128)S(1)}, f32[64,512]{1,0:T(8,128)S(1)}) custom-call(s32[5]{0:T(128)S(1)} %stack.23.place_ref, s32[1,512]{1,0:T(1,128)S(1)} %bitcast.8, f32[512,128]{1,0:T(8,128)S(1)} %add_add_fusion.mine_ref, f32[512,128]{1,0:T(8,128)S(1)} %collective-permute-done.9.other_ref), custom_call_target="tpu_custom_call" | custom-call | tf_op jit(solution)/shard_map/partial_distances/pallas_call | solution.py:301
  57.4 0.1 collective-permute-start.10
  57.5 0.5 collective-permute-start.11
  58.0 2.7 %collective-permute-start.12 = (f32[64,512]{1,0:T(8,128)S(1)}, f32[64,512]{1,0:T(8,128)S(1)}, u32[]{:S(2)}, u32[]{:S(2)}) collective-permute-start(f32[64,512]{1,0:T(8,128)S(1)} %get-tuple-element.42), channel_id=1, source_target_pairs={{0,24},{1,97},{2,26},{3,99},{4,28},{5,101},{6,30},{7,103},{8,16},{... | collective-permute-start | bytes 393224 | tf_op jit(solution)/shard_map/ppermute | solution.py:346
  60.8 2.4 %collective-permute-done.10 = f32[64,512]{1,0:T(8,128)S(1)} collective-permute-done((f32[64,512]{1,0:T(8,128)S(1)}, f32[64,512]{1,0:T(8,128)S(1)}, u32[]{:S(2)}, u32[]{:S(2)}) %collective-permute-start.10) | collective-permute-done | bytes 131104 | tf_op jit(solution)/shard_map/ppermute | solution.py:346
  63.1 0.0 collective-permute-done.11
  63.1 1.1 %collective-permute-done.12 = f32[64,512]{1,0:T(8,128)S(1)} collective-permute-done((f32[64,512]{1,0:T(8,128)S(1)}, f32[64,512]{1,0:T(8,128)S(1)}, u32[]{:S(2)}, u32[]{:S(2)}) %collective-permute-start.12) | collective-permute-done | bytes 131104 | tf_op jit(solution)/shard_map/ppermute | solution.py:346
  64.3 2.2 %collective-permute-start.13 = (f32[16,512]{1,0:T(8,128)S(1)}, f32[16,512]{1,0:T(8,128)S(1)}, u32[]{:S(2)}, u32[]{:S(2)}) collective-permute-start(f32[16,512]{1,0:T(8,128)S(1)} %get-tuple-element.45), channel_id=1, source_target_pairs={{0,64},{1,17},{2,66},{3,19},{4,68},{5,21},{6,70},{7,23},{8,72},{9,... | collective-permute-start | bytes 98312 | tf_op jit(solution)/shard_map/ppermute | solution.py:346
  66.6 0.5 collective-permute-start.15
  67.1 0.5 collective-permute-start.14
  67.6 1.1 %collective-permute-done.13 = f32[16,512]{1,0:T(8,128)S(1)} collective-permute-done((f32[16,512]{1,0:T(8,128)S(1)}, f32[16,512]{1,0:T(8,128)S(1)}, u32[]{:S(2)}, u32[]{:S(2)}) %collective-permute-start.13) | collective-permute-done | bytes 32800 | tf_op jit(solution)/shard_map/ppermute | solution.py:346
  68.7 1.9 %collective-permute-done.15 = f32[16,512]{1,0:T(8,128)S(1)} collective-permute-done((f32[16,512]{1,0:T(8,128)S(1)}, f32[16,512]{1,0:T(8,128)S(1)}, u32[]{:S(2)}, u32[]{:S(2)}) %collective-permute-start.15) | collective-permute-done | bytes 32800 | tf_op jit(solution)/shard_map/ppermute | solution.py:346
  70.6 2.8 %collective-permute-start.18 = (f32[16,512]{1,0:T(8,128)S(1)}, f32[16,512]{1,0:T(8,128)S(1)}, u32[]{:S(2)}, u32[]{:S(2)}) collective-permute-start(f32[16,512]{1,0:T(8,128)S(1)} %fusion.1), channel_id=1, source_target_pairs={{0,4},{1,5},{2,6},{3,7},{4,0},{5,1},{6,2},{7,3},{8,12},{9,13},{10,... | collective-permute-start | bytes 98312 | tf_op jit(solution)/shard_map/ppermute | solution.py:346
  73.4 0.9 %collective-permute-start.17 = (f32[16,512]{1,0:T(8,128)S(1)}, f32[16,512]{1,0:T(8,128)S(1)}, u32[]{:S(2)}, u32[]{:S(2)}) collective-permute-start(f32[16,512]{1,0:T(8,128)S(1)} %fusion.1), channel_id=1, source_target_pairs={{0,6},{1,7},{2,4},{3,5},{4,2},{5,3},{6,0},{7,1},{8,14},{9,15},{10,... | collective-permute-start | bytes 98312 | tf_op jit(solution)/shard_map/ppermute | solution.py:346
  74.2 0.7 collective-permute-done.18
  74.9 2.4 %collective-permute-done.17 = f32[16,512]{1,0:T(8,128)S(1)} collective-permute-done((f32[16,512]{1,0:T(8,128)S(1)}, f32[16,512]{1,0:T(8,128)S(1)}, u32[]{:S(2)}, u32[]{:S(2)}) %collective-permute-start.17) | collective-permute-done | bytes 32800 | tf_op jit(solution)/shard_map/ppermute | solution.py:346
  77.3 0.0 collective-permute-done.16
  77.4 4.6 %collective-permute-start.19 = (f32[16,512]{1,0:T(8,128)S(1)}, f32[16,512]{1,0:T(8,128)S(1)}, u32[]{:S(2)}, u32[]{:S(2)}) collective-permute-start(f32[16,512]{1,0:T(8,128)S(1)} %add_add_fusion.2), channel_id=1, source_target_pairs={{0,1},{1,0},{2,3},{3,2},{4,5},{5,4},{6,7},{7,6},{8,9},{9,8},{10,11... | collective-permute-start | bytes 98312 | tf_op jit(solution)/shard_map/ppermute | solution.py:346
  82.0 0.9 %collective-permute-done.19 = f32[16,512]{1,0:T(8,128)S(1)} collective-permute-done((f32[16,512]{1,0:T(8,128)S(1)}, f32[16,512]{1,0:T(8,128)S(1)}, u32[]{:S(2)}, u32[]{:S(2)}) %collective-permute-start.19) | collective-permute-done | bytes 32800 | tf_op jit(solution)/shard_map/ppermute | solution.py:346
  82.8 0.6 maximum_select_fusion
  (11 shorter events, 0.2 us)
Async XLA Ops:
  9.3 11.2 %collective-permute-start = (f32[512,256]{1,0:T(8,128)S(1)}, f32[512,256]{1,0:T(8,128)S(1)}, u32[]{:S(2)}, u32[]{:S(2)}) collective-permute-start(f32[512,256]{1,0:T(8,128)S(1)} %get-tuple-element.30), channel_id=1, source_target_pairs={{0,8},{1,33},{2,10},{3,35},{4,12},{5,37},{6,14},{7,39},{8,0},{9,41... | collective-permute-start | bytes 1572872 | tf_op jit(solution)/shard_map/ppermute | solution.py:346
  11.5 9.5 %collective-permute-start.1 = (f32[512,256]{1,0:T(8,128)S(1)}, f32[512,256]{1,0:T(8,128)S(1)}, u32[]{:S(2)}, u32[]{:S(2)}) collective-permute-start(f32[512,256]{1,0:T(8,128)S(1)} %get-tuple-element.31), channel_id=1, source_target_pairs={{0,24},{1,97},{2,26},{3,99},{4,28},{5,101},{6,30},{7,103},{8,16},{... | collective-permute-start | bytes 1572872 | tf_op jit(solution)/shard_map/ppermute | solution.py:346
  19.4 9.9 %collective-permute-start.2 = (f32[512,256]{1,0:T(8,128)S(1)}, f32[512,256]{1,0:T(8,128)S(1)}, u32[]{:S(2)}, u32[]{:S(2)}) collective-permute-start(f32[512,256]{1,0:T(8,128)S(1)} %get-tuple-element.33), channel_id=1, source_target_pairs={{0,8},{1,33},{2,10},{3,35},{4,12},{5,37},{6,14},{7,39},{8,0},{9,41... | collective-permute-start | bytes 1572872 | tf_op jit(solution)/shard_map/ppermute | solution.py:346
  19.9 9.5 %collective-permute-start.3 = (f32[512,256]{1,0:T(8,128)S(1)}, f32[512,256]{1,0:T(8,128)S(1)}, u32[]{:S(2)}, u32[]{:S(2)}) collective-permute-start(f32[512,256]{1,0:T(8,128)S(1)} %get-tuple-element.34), channel_id=1, source_target_pairs={{0,24},{1,97},{2,26},{3,99},{4,28},{5,101},{6,30},{7,103},{8,16},{... | collective-permute-start | bytes 1572872 | tf_op jit(solution)/shard_map/ppermute | solution.py:346
  27.2 8.4 %collective-permute-start.5 = (f32[512,256]{1,0:T(8,128)S(1)}, f32[512,256]{1,0:T(8,128)S(1)}, u32[]{:S(2)}, u32[]{:S(2)}) collective-permute-start(f32[512,256]{1,0:T(8,128)S(1)} %get-tuple-element.38), channel_id=1, source_target_pairs={{0,8},{1,33},{2,10},{3,35},{4,12},{5,37},{6,14},{7,39},{8,0},{9,41... | collective-permute-start | bytes 1572872 | tf_op jit(solution)/shard_map/ppermute | solution.py:346
  27.3 9.6 %collective-permute-start.4 = (f32[512,256]{1,0:T(8,128)S(1)}, f32[512,256]{1,0:T(8,128)S(1)}, u32[]{:S(2)}, u32[]{:S(2)}) collective-permute-start(f32[512,256]{1,0:T(8,128)S(1)} %get-tuple-element.36), channel_id=1, source_target_pairs={{0,24},{1,97},{2,26},{3,99},{4,28},{5,101},{6,30},{7,103},{8,16},{... | collective-permute-start | bytes 1572872 | tf_op jit(solution)/shard_map/ppermute | solution.py:346
  29.4 26.7 %copy-start = (s32[512]{0:T(512)S(1)}, s32[512]{0:T(512)}, u32[]{:S(2)}) copy-start(s32[512]{0:T(512)} %param.9) | copy-start | bytes 6148
  37.0 5.3 %collective-permute-start.7 = (f32[512,128]{1,0:T(8,128)S(1)}, f32[512,128]{1,0:T(8,128)S(1)}, u32[]{:S(2)}, u32[]{:S(2)}) collective-permute-start(f32[512,128]{1,0:T(8,128)S(1)} %slice_select_fusion.2), channel_id=1, source_target_pairs={{0,32},{1,9},{2,34},{3,11},{4,36},{5,13},{6,38},{7,15},{8,40},{9,1... | collective-permute-start | bytes 786440 | tf_op jit(solution)/shard_map/ppermute | solution.py:346
  38.4 10.5 %collective-permute-start.6 = (f32[512,128]{1,0:T(8,128)S(1)}, f32[512,128]{1,0:T(8,128)S(1)}, u32[]{:S(2)}, u32[]{:S(2)}) collective-permute-start(f32[512,128]{1,0:T(8,128)S(1)} %get-tuple-element.43), channel_id=1, source_target_pairs={{0,64},{1,17},{2,66},{3,19},{4,68},{5,21},{6,70},{7,23},{8,72},{9,... | collective-permute-start | bytes 786440 | tf_op jit(solution)/shard_map/ppermute | solution.py:346
  42.0 9.5 %collective-permute-start.8 = (f32[512,128]{1,0:T(8,128)S(1)}, f32[512,128]{1,0:T(8,128)S(1)}, u32[]{:S(2)}, u32[]{:S(2)}) collective-permute-start(f32[512,128]{1,0:T(8,128)S(1)} %get-tuple-element.44), channel_id=1, source_target_pairs={{0,96},{1,25},{2,98},{3,27},{4,100},{5,29},{6,102},{7,31},{8,104},... | collective-permute-start | bytes 786440 | tf_op jit(solution)/shard_map/ppermute | solution.py:346
  51.7 4.5 %collective-permute-start.9 = (f32[512,128]{1,0:T(8,128)S(1)}, f32[512,128]{1,0:T(8,128)S(1)}, u32[]{:S(2)}, u32[]{:S(2)}) collective-permute-start(f32[512,128]{1,0:T(8,128)S(1)} %add_add_fusion.mine_ref), channel_id=1, source_target_pairs={{0,1},{1,0},{2,3},{3,2},{4,5},{5,4},{6,7},{7,6},{8,9},{9,8},{10,11... | collective-permute-start | bytes 786440 | tf_op jit(solution)/shard_map/ppermute | solution.py:346
  57.4 5.7 %collective-permute-start.10 = (f32[64,512]{1,0:T(8,128)S(1)}, f32[64,512]{1,0:T(8,128)S(1)}, u32[]{:S(2)}, u32[]{:S(2)}) collective-permute-start(f32[64,512]{1,0:T(8,128)S(1)} %get-tuple-element.40), channel_id=1, source_target_pairs={{0,16},{1,65},{2,18},{3,67},{4,20},{5,69},{6,22},{7,71},{8,24},{9,... | collective-permute-start | bytes 393224 | tf_op jit(solution)/shard_map/ppermute | solution.py:346
  57.5 5.6 %collective-permute-start.11 = (f32[64,512]{1,0:T(8,128)S(1)}, f32[64,512]{1,0:T(8,128)S(1)}, u32[]{:S(2)}, u32[]{:S(2)}) collective-permute-start(f32[64,512]{1,0:T(8,128)S(1)} %get-tuple-element.41), channel_id=1, source_target_pairs={{0,8},{1,33},{2,10},{3,35},{4,12},{5,37},{6,14},{7,39},{8,0},{9,41... | collective-permute-start | bytes 393224 | tf_op jit(solution)/shard_map/ppermute | solution.py:346
  58.0 6.2 %collective-permute-start.12 = (f32[64,512]{1,0:T(8,128)S(1)}, f32[64,512]{1,0:T(8,128)S(1)}, u32[]{:S(2)}, u32[]{:S(2)}) collective-permute-start(f32[64,512]{1,0:T(8,128)S(1)} %get-tuple-element.42), channel_id=1, source_target_pairs={{0,24},{1,97},{2,26},{3,99},{4,28},{5,101},{6,30},{7,103},{8,16},{... | collective-permute-start | bytes 393224 | tf_op jit(solution)/shard_map/ppermute | solution.py:346
  64.3 4.3 %collective-permute-start.13 = (f32[16,512]{1,0:T(8,128)S(1)}, f32[16,512]{1,0:T(8,128)S(1)}, u32[]{:S(2)}, u32[]{:S(2)}) collective-permute-start(f32[16,512]{1,0:T(8,128)S(1)} %get-tuple-element.45), channel_id=1, source_target_pairs={{0,64},{1,17},{2,66},{3,19},{4,68},{5,21},{6,70},{7,23},{8,72},{9,... | collective-permute-start | bytes 98312 | tf_op jit(solution)/shard_map/ppermute | solution.py:346
  66.6 4.0 %collective-permute-start.15 = (f32[16,512]{1,0:T(8,128)S(1)}, f32[16,512]{1,0:T(8,128)S(1)}, u32[]{:S(2)}, u32[]{:S(2)}) collective-permute-start(f32[16,512]{1,0:T(8,128)S(1)} %get-tuple-element.46), channel_id=1, source_target_pairs={{0,96},{1,25},{2,98},{3,27},{4,100},{5,29},{6,102},{7,31},{8,104},... | collective-permute-start | bytes 98312 | tf_op jit(solution)/shard_map/ppermute | solution.py:346
  67.1 3.4 %collective-permute-start.14 = (f32[16,512]{1,0:T(8,128)S(1)}, f32[16,512]{1,0:T(8,128)S(1)}, u32[]{:S(2)}, u32[]{:S(2)}) collective-permute-start(f32[16,512]{1,0:T(8,128)S(1)} %get-tuple-element.47), channel_id=1, source_target_pairs={{0,32},{1,9},{2,34},{3,11},{4,36},{5,13},{6,38},{7,15},{8,40},{9,1... | collective-permute-start | bytes 98312 | tf_op jit(solution)/shard_map/ppermute | solution.py:346
  70.6 4.3 %collective-permute-start.18 = (f32[16,512]{1,0:T(8,128)S(1)}, f32[16,512]{1,0:T(8,128)S(1)}, u32[]{:S(2)}, u32[]{:S(2)}) collective-permute-start(f32[16,512]{1,0:T(8,128)S(1)} %fusion.1), channel_id=1, source_target_pairs={{0,4},{1,5},{2,6},{3,7},{4,0},{5,1},{6,2},{7,3},{8,12},{9,13},{10,... | collective-permute-start | bytes 98312 | tf_op jit(solution)/shard_map/ppermute | solution.py:346
  73.4 4.0 %collective-permute-start.17 = (f32[16,512]{1,0:T(8,128)S(1)}, f32[16,512]{1,0:T(8,128)S(1)}, u32[]{:S(2)}, u32[]{:S(2)}) collective-permute-start(f32[16,512]{1,0:T(8,128)S(1)} %fusion.1), channel_id=1, source_target_pairs={{0,6},{1,7},{2,4},{3,5},{4,2},{5,3},{6,0},{7,1},{8,14},{9,15},{10,... | collective-permute-start | bytes 98312 | tf_op jit(solution)/shard_map/ppermute | solution.py:346
  74.2 3.1 %collective-permute-start.16 = (f32[16,512]{1,0:T(8,128)S(1)}, f32[16,512]{1,0:T(8,128)S(1)}, u32[]{:S(2)}, u32[]{:S(2)}) collective-permute-start(f32[16,512]{1,0:T(8,128)S(1)} %fusion.1), channel_id=1, source_target_pairs={{0,2},{1,3},{2,0},{3,1},{4,6},{5,7},{6,4},{7,5},{8,10},{9,11},{10,... | collective-permute-start | bytes 98312 | tf_op jit(solution)/shard_map/ppermute | solution.py:346
  77.4 5.5 %collective-permute-start.19 = (f32[16,512]{1,0:T(8,128)S(1)}, f32[16,512]{1,0:T(8,128)S(1)}, u32[]{:S(2)}, u32[]{:S(2)}) collective-permute-start(f32[16,512]{1,0:T(8,128)S(1)} %add_add_fusion.2), channel_id=1, source_target_pairs={{0,1},{1,0},{2,3},{3,2},{4,5},{5,4},{6,7},{7,6},{8,9},{9,8},{10,11... | collective-permute-start | bytes 98312 | tf_op jit(solution)/shard_map/ppermute | solution.py:346

commit v6 on v5

--- a/solution.py
+++ b/solution.py
@@ -269,12 +269,12 @@
     )(place, small, emb, onehot, columns, low, high)
 
 
-def distances_kernel(place_ref, counts_ref, mine_ref, other_ref, *rest):
+def distances_kernel(n_before, place_ref, counts_ref, sums_ref, *rest):
+    before, rest = rest[:n_before], rest[n_before:]
     outs, (means, rows, counts) = rest[:RING], rest[RING:]
     y, z, core = place_ref[2], place_ref[3], place_ref[4]
     counts[...] = jnp.broadcast_to(counts_ref[...].astype(jnp.float32), (LANES, K)).T
-    means[:, :LANES] = mine_ref[...] / counts[...]
-    means[:, LANES:] = other_ref[...] / counts[...]
+    means[...] = sums_ref[...] / counts[...]
     part = OWNED // 2
     for s1 in range(RING):
         for s2 in range(RING):
@@ -289,28 +289,29 @@
         picked, every, nt, precision=lax.Precision.HIGHEST, preferred_element_type=jnp.float32
     )
     squares = every * every
-    norms = jnp.sum((squares[:, :LANES] + squares[:, LANES:]).T, axis=0, keepdims=True)
+    norms = jnp.sum(squares.T, axis=0, keepdims=True)
     own = jnp.sum(picked * picked, axis=1, keepdims=True)
     partial = own + norms - 2.0 * cross
     for s in range(RING):
-        outs[s][...] = partial[s * RING * part : (s + 1) * RING * part]
-
-
-def partial_distances(place, counts, mine, other):
+        block = partial[s * RING * part : (s + 1) * RING * part]
+        outs[s][...] = before[s][...] + block if before else block
+
+
+def partial_distances(place, counts, sums, *before):
     rows = K // 2
     return pl.pallas_call(
-        distances_kernel,
+        functools.partial(distances_kernel, len(before)),
         out_shape=[jax.ShapeDtypeStruct((rows // RING, K), jnp.float32)] * RING,
-        in_specs=[SMEM] + [VMEM] * 3,
+        in_specs=[SMEM] + [VMEM] * (2 + len(before)),
         out_specs=[VMEM] * RING,
         scratch_shapes=[
-            pltpu.VMEM((K, 2 * LANES), jnp.float32),
-            pltpu.VMEM((rows, 2 * LANES), jnp.float32),
+            pltpu.VMEM((K, LANES), jnp.float32),
+            pltpu.VMEM((rows, LANES), jnp.float32),
             pltpu.VMEM((K, LANES), jnp.float32),
         ],
         compiler_params=pltpu.CompilerParams(vmem_limit_bytes=16 << 20),
         name="partial_distances",
-    )(place, counts, mine, other)
+    )(place, counts, sums, *before)
 
 
 def device(y, z, x, core):
@@ -383,7 +384,9 @@
         mine = mine + send(pieces[s], across_ring(1, s))
     other = send(mine, across_core())
 
-    parts = partial_distances(place, domain_counts[None, :], mine, other)
+    counts = domain_counts[None, :]
+    parts = partial_distances(place, counts, mine)
+    parts = partial_distances(place, counts, other, *parts)
     total = parts[0]
     for s in (2, 1, 3):
         total = total + send(parts[s], across_ring(0, s))

time: 83.6 us -> 83.6 us (level)
  Pallas kernels: 27.7 us -> 28.9 us
  waiting for transfers between devices: 23.3 us -> 22.2 us
    pallas_call x1 -> x2, Pallas kernels: 1.3 us -> 2.47 us  [partial_distances(): pl.pallas_call(functools.partial(distances_kernel, len(before)), out_shap...]
    ppermute x20, waiting for transfers between devices: 23.3 us -> 22.2 us  [send(): return lax.ppermute(value, ('doc', 'feat'), pairs)]
  transfers between devices with their start and end apart: 20 -> 20, of which waited for: 15 -> 14; matrix products, arithmetic and copies ran while one was open for 0% -> 0% of each run, Pallas kernels for 21% -> 23%
where the time goes in v6:
time: 83.6 us; the launch traced here: 83.4 us
  starting transfers between devices  30.4 us (36%)
  Pallas kernels  28.9 us (35%)
  waiting for transfers between devices  22.2 us (27%)
  other arithmetic  1.71 us (2%)
    ppermute x20, starting transfers between devices, send(): return lax.ppermute(value, ('doc', 'feat'), pairs)  30.4 us
    ppermute x20, waiting for transfers between devices, send(): return lax.ppermute(value, ('doc', 'feat'), pairs)  22.2 us
    pallas_call x2, Pallas kernels, next_sums(): pl.pallas_call(functools.partial(next_kernel, pieces, after, len(arrived)...  12.1 us
    pallas_call x1, Pallas kernels, first_sums(): pl.pallas_call(functools.partial(first_kernel, offset, after), out_shape=...  8.5 us
    pallas_call x1, Pallas kernels, last_sums(): pl.pallas_call(last_kernel, out_shape=[jax.ShapeDtypeStruct((K, width //...  5.84 us
    pallas_call x2, Pallas kernels, partial_distances(): pl.pallas_call(functools.partial(distances_kernel, len(before)), out_shap...  2.47 us
  transfers between devices with their start and end apart: 20, of which 14 were waited for; matrix products, arithmetic and copies ran while one was open for 0% of the time, Pallas kernels for 23%

profile of v6, /device:TPU:1, one launch (start us, length us, event | category | flops | bytes accessed | tf_op | source)
XLA Modules:
  0.0 83.4 jit_solution(10181697876795931990)
XLA Ops:
  0.0 0.1 stack.23.place_ref
  0.1 0.7 convert_add_fusion.small_ref
  0.8 8.5 %first_sums.1 = (f32[512,256]{1,0:T(8,128)S(1)}, f32[512,256]{1,0:T(8,128)S(1)}, bf16[1024,4096]{1,0:T(8,128)(2,1)S(1)}, bf16[512,1024]{1,0:T(8,128)(2,1)S(1)}, bf16[4096,512]{1,0:T(8,128)(2,1)S(1)}) custom-call(s32[5]{0:T(128)S(1)} %stack.23.place_ref, f32[24,128]{1,0:T(8,128)S(1)} %convert_add_fusion.small_ref, bf16[1024,4096]{1,0:T(8,128)(2,1)} %emb_hbm.1, ...), custom_call_target="tpu_custom_call" | custom-call | flops 4831838208 | bytes 1048576 | tf_op jit(solution)/shard_map/first_sums/pallas_call | solution.py:215
  9.3 2.2 %collective-permute-start = (f32[512,256]{1,0:T(8,128)S(1)}, f32[512,256]{1,0:T(8,128)S(1)}, u32[]{:S(2)}, u32[]{:S(2)}) collective-permute-start(f32[512,256]{1,0:T(8,128)S(1)} %get-tuple-element.34), channel_id=1, source_target_pairs={{0,8},{1,33},{2,10},{3,35},{4,12},{5,37},{6,14},{7,39},{8,0},{9,41... | collective-permute-start | bytes 1572872 | tf_op jit(solution)/shard_map/ppermute | solution.py:347
  11.5 1.9 %collective-permute-start.1 = (f32[512,256]{1,0:T(8,128)S(1)}, f32[512,256]{1,0:T(8,128)S(1)}, u32[]{:S(2)}, u32[]{:S(2)}) collective-permute-start(f32[512,256]{1,0:T(8,128)S(1)} %get-tuple-element.35), channel_id=1, source_target_pairs={{0,24},{1,97},{2,26},{3,99},{4,28},{5,101},{6,30},{7,103},{8,16},{... | collective-permute-start | bytes 1572872 | tf_op jit(solution)/shard_map/ppermute | solution.py:347
  13.4 6.0 %next_sums.2 = (f32[512,256]{1,0:T(8,128)S(1)}, f32[512,256]{1,0:T(8,128)S(1)}, bf16[4096,512]{1,0:T(8,128)(2,1)S(1)}) custom-call(s32[5]{0:T(128)S(1)} %stack.23.place_ref, f32[24,128]{1,0:T(8,128)S(1)} %convert_add_fusion.small_ref, bf16[1024,4096]{1,0:T(8,128)(2,1)S(1)} %get-tuple-element.30.emb_ref, bf16[512,1024]{1,0:T(8,128)(2,1)S(1)} %get-tuple-element.31.onehot_ref, ...), custom_call_target="tpu_custom_call" | custom-call | flops 4831838208 | bytes 1048576 | tf_op jit(solution)/shard_map/next_sums/pallas_call | solution.py:242
  19.4 0.5 collective-permute-start.2
  19.9 0.6 collective-permute-start.3
  20.5 0.6 collective-permute-done.1.rest_1_
  21.1 6.1 %next_sums.3 = (f32[512,256]{1,0:T(8,128)S(1)}, f32[512,256]{1,0:T(8,128)S(1)}, bf16[4096,512]{1,0:T(8,128)(2,1)S(1)}) custom-call(s32[5]{0:T(128)S(1)} %stack.23.place_ref, f32[24,128]{1,0:T(8,128)S(1)} %convert_add_fusion.small_ref, bf16[1024,4096]{1,0:T(8,128)(2,1)S(1)} %get-tuple-element.30.emb_ref, bf16[512,1024]{1,0:T(8,128)(2,1)S(1)} %get-tuple-element.31.onehot_ref, ...), custom_call_target="tpu_custom_call" | custom-call | flops 4831838208 | bytes 1048576 | tf_op jit(solution)/shard_map/next_sums/pallas_call | solution.py:242
  27.2 0.1 collective-permute-start.5
  27.3 1.9 %collective-permute-start.4 = (f32[512,256]{1,0:T(8,128)S(1)}, f32[512,256]{1,0:T(8,128)S(1)}, u32[]{:S(2)}, u32[]{:S(2)}) collective-permute-start(f32[512,256]{1,0:T(8,128)S(1)} %get-tuple-element.40), channel_id=1, source_target_pairs={{0,24},{1,97},{2,26},{3,99},{4,28},{5,101},{6,30},{7,103},{8,16},{... | collective-permute-start | bytes 1572872 | tf_op jit(solution)/shard_map/ppermute | solution.py:347
  29.3 0.1 collective-permute-done.3.high_ref
  29.4 5.8 %last_sums.1 = (f32[512,256]{1,0:T(8,128)S(1)}, f32[512,256]{1,0:T(8,128)S(1)}) custom-call(s32[5]{0:T(128)S(1)} %stack.23.place_ref, f32[24,128]{1,0:T(8,128)S(1)} %convert_add_fusion.small_ref, bf16[1024,4096]{1,0:T(8,128)(2,1)S(1)} %get-tuple-element.30.emb_ref, bf16[512,1024]{1,0:T(8,128)(2,1)S(1)} %get-tuple-element.31.onehot_ref, ...), custom_call_target="tpu_custom_call" | custom-call | flops 4831838208 | bytes 1048576 | tf_op jit(solution)/shard_map/last_sums/pallas_call | solution.py:260
  35.3 0.4 collective-permute-done.5
  35.6 0.1 add.61
  35.7 1.2 %collective-permute-done.4 = f32[512,256]{1,0:T(8,128)S(1)} collective-permute-done((f32[512,256]{1,0:T(8,128)S(1)}, f32[512,256]{1,0:T(8,128)S(1)}, u32[]{:S(2)}, u32[]{:S(2)}) %collective-permute-start.4) | collective-permute-done | bytes 524320 | tf_op jit(solution)/shard_map/ppermute | solution.py:347
  36.9 0.1 add.60
  37.0 1.4 %collective-permute-start.7 = (f32[512,128]{1,0:T(8,128)S(1)}, f32[512,128]{1,0:T(8,128)S(1)}, u32[]{:S(2)}, u32[]{:S(2)}) collective-permute-start(f32[512,128]{1,0:T(8,128)S(1)} %slice_select_fusion.2), channel_id=1, source_target_pairs={{0,32},{1,9},{2,34},{3,11},{4,36},{5,13},{6,38},{7,15},{8,40},{9,1... | collective-permute-start | bytes 786440 | tf_op jit(solution)/shard_map/ppermute | solution.py:347
  38.4 3.6 %collective-permute-start.6 = (f32[512,128]{1,0:T(8,128)S(1)}, f32[512,128]{1,0:T(8,128)S(1)}, u32[]{:S(2)}, u32[]{:S(2)}) collective-permute-start(f32[512,128]{1,0:T(8,128)S(1)} %get-tuple-element.51), channel_id=1, source_target_pairs={{0,64},{1,17},{2,66},{3,19},{4,68},{5,21},{6,70},{7,23},{8,72},{9,... | collective-permute-start | bytes 786440 | tf_op jit(solution)/shard_map/ppermute | solution.py:347
  42.0 0.0 collective-permute-start.8
  42.0 0.3 collective-permute-done.7
  42.3 6.6 %collective-permute-done.6 = f32[512,128]{1,0:T(8,128)S(1)} collective-permute-done((f32[512,128]{1,0:T(8,128)S(1)}, f32[512,128]{1,0:T(8,128)S(1)}, u32[]{:S(2)}, u32[]{:S(2)}) %collective-permute-start.6) | collective-permute-done | bytes 262176 | tf_op jit(solution)/shard_map/ppermute | solution.py:347
  48.9 2.6 %collective-permute-done.8 = f32[512,128]{1,0:T(8,128)S(1)} collective-permute-done((f32[512,128]{1,0:T(8,128)S(1)}, f32[512,128]{1,0:T(8,128)S(1)}, u32[]{:S(2)}, u32[]{:S(2)}) %collective-permute-start.8) | collective-permute-done | bytes 262176 | tf_op jit(solution)/shard_map/ppermute | solution.py:347
  51.6 0.1 add_add_fusion.sums_ref
  51.7 3.3 %collective-permute-start.9 = (f32[512,128]{1,0:T(8,128)S(1)}, f32[512,128]{1,0:T(8,128)S(1)}, u32[]{:S(2)}, u32[]{:S(2)}) collective-permute-start(f32[512,128]{1,0:T(8,128)S(1)} %add_add_fusion.sums_ref), channel_id=1, source_target_pairs={{0,1},{1,0},{2,3},{3,2},{4,5},{5,4},{6,7},{7,6},{8,9},{9,8},{10,11... | collective-permute-start | bytes 786440 | tf_op jit(solution)/shard_map/ppermute | solution.py:347
  55.0 1.2 %partial_distances.2 = (f32[64,512]{1,0:T(8,128)S(1)}, f32[64,512]{1,0:T(8,128)S(1)}, f32[64,512]{1,0:T(8,128)S(1)}, f32[64,512]{1,0:T(8,128)S(1)}) custom-call(s32[5]{0:T(128)S(1)} %stack.23.place_ref, s32[1,512]{1,0:T(1,128)S(1)} %bitcast.8, f32[512,128]{1,0:T(8,128)S(1)} %add_add_fusion.sums_ref), custom_call_target="tpu_custom_call" | custom-call | tf_op jit(solution)/shard_map/partial_distances/pallas_call | solution.py:302
  56.2 1.2 %partial_distances.3 = (f32[64,512]{1,0:T(8,128)S(1)}, f32[64,512]{1,0:T(8,128)S(1)}, f32[64,512]{1,0:T(8,128)S(1)}, f32[64,512]{1,0:T(8,128)S(1)}) custom-call(s32[5]{0:T(128)S(1)} %stack.23.place_ref, s32[1,512]{1,0:T(1,128)S(1)} %bitcast.9, f32[512,128]{1,0:T(8,128)S(1)} %collective-permute-done.9.sums_ref, f32[64,512]{1,0:T(8,128)S(1)} %get-tuple-element.43.rest_0_, ...), custom_call_target="tpu_custom_call" | custom-call | tf_op jit(solution)/shard_map/partial_distances/pallas_call | solution.py:302
  57.5 0.1 collective-permute-start.10
  57.6 0.5 collective-permute-start.11
  58.1 2.7 %collective-permute-start.12 = (f32[64,512]{1,0:T(8,128)S(1)}, f32[64,512]{1,0:T(8,128)S(1)}, u32[]{:S(2)}, u32[]{:S(2)}) collective-permute-start(f32[64,512]{1,0:T(8,128)S(1)} %get-tuple-element.50), channel_id=1, source_target_pairs={{0,24},{1,97},{2,26},{3,99},{4,28},{5,101},{6,30},{7,103},{8,16},{... | collective-permute-start | bytes 393224 | tf_op jit(solution)/shard_map/ppermute | solution.py:347
  60.8 2.4 %collective-permute-done.10 = f32[64,512]{1,0:T(8,128)S(1)} collective-permute-done((f32[64,512]{1,0:T(8,128)S(1)}, f32[64,512]{1,0:T(8,128)S(1)}, u32[]{:S(2)}, u32[]{:S(2)}) %collective-permute-start.10) | collective-permute-done | bytes 131104 | tf_op jit(solution)/shard_map/ppermute | solution.py:347
  63.2 1.1 %collective-permute-done.12 = f32[64,512]{1,0:T(8,128)S(1)} collective-permute-done((f32[64,512]{1,0:T(8,128)S(1)}, f32[64,512]{1,0:T(8,128)S(1)}, u32[]{:S(2)}, u32[]{:S(2)}) %collective-permute-start.12) | collective-permute-done | bytes 131104 | tf_op jit(solution)/shard_map/ppermute | solution.py:347
  64.3 2.2 %collective-permute-start.13 = (f32[16,512]{1,0:T(8,128)S(1)}, f32[16,512]{1,0:T(8,128)S(1)}, u32[]{:S(2)}, u32[]{:S(2)}) collective-permute-start(f32[16,512]{1,0:T(8,128)S(1)} %get-tuple-element.53), channel_id=1, source_target_pairs={{0,64},{1,17},{2,66},{3,19},{4,68},{5,21},{6,70},{7,23},{8,72},{9,... | collective-permute-start | bytes 98312 | tf_op jit(solution)/shard_map/ppermute | solution.py:347
  66.6 0.5 collective-permute-start.15
  67.1 0.5 collective-permute-start.14
  67.6 1.1 %collective-permute-done.13 = f32[16,512]{1,0:T(8,128)S(1)} collective-permute-done((f32[16,512]{1,0:T(8,128)S(1)}, f32[16,512]{1,0:T(8,128)S(1)}, u32[]{:S(2)}, u32[]{:S(2)}) %collective-permute-start.13) | collective-permute-done | bytes 32800 | tf_op jit(solution)/shard_map/ppermute | solution.py:347
  68.7 1.9 %collective-permute-done.15 = f32[16,512]{1,0:T(8,128)S(1)} collective-permute-done((f32[16,512]{1,0:T(8,128)S(1)}, f32[16,512]{1,0:T(8,128)S(1)}, u32[]{:S(2)}, u32[]{:S(2)}) %collective-permute-start.15) | collective-permute-done | bytes 32800 | tf_op jit(solution)/shard_map/ppermute | solution.py:347
  70.6 0.0 collective-permute-done.14
  70.6 2.8 %collective-permute-start.18 = (f32[16,512]{1,0:T(8,128)S(1)}, f32[16,512]{1,0:T(8,128)S(1)}, u32[]{:S(2)}, u32[]{:S(2)}) collective-permute-start(f32[16,512]{1,0:T(8,128)S(1)} %fusion.1), channel_id=1, source_target_pairs={{0,4},{1,5},{2,6},{3,7},{4,0},{5,1},{6,2},{7,3},{8,12},{9,13},{10,... | collective-permute-start | bytes 98312 | tf_op jit(solution)/shard_map/ppermute | solution.py:347
  73.4 0.9 %collective-permute-start.17 = (f32[16,512]{1,0:T(8,128)S(1)}, f32[16,512]{1,0:T(8,128)S(1)}, u32[]{:S(2)}, u32[]{:S(2)}) collective-permute-start(f32[16,512]{1,0:T(8,128)S(1)} %fusion.1), channel_id=1, source_target_pairs={{0,6},{1,7},{2,4},{3,5},{4,2},{5,3},{6,0},{7,1},{8,14},{9,15},{10,... | collective-permute-start | bytes 98312 | tf_op jit(solution)/shard_map/ppermute | solution.py:347
  74.3 0.0 collective-permute-start.16
  74.3 0.7 collective-permute-done.18
  74.9 2.4 %collective-permute-done.17 = f32[16,512]{1,0:T(8,128)S(1)} collective-permute-done((f32[16,512]{1,0:T(8,128)S(1)}, f32[16,512]{1,0:T(8,128)S(1)}, u32[]{:S(2)}, u32[]{:S(2)}) %collective-permute-start.17) | collective-permute-done | bytes 32800 | tf_op jit(solution)/shard_map/ppermute | solution.py:347
  77.4 0.0 collective-permute-done.16
  77.4 4.5 %collective-permute-start.19 = (f32[16,512]{1,0:T(8,128)S(1)}, f32[16,512]{1,0:T(8,128)S(1)}, u32[]{:S(2)}, u32[]{:S(2)}) collective-permute-start(f32[16,512]{1,0:T(8,128)S(1)} %add_add_fusion.2), channel_id=1, source_target_pairs={{0,1},{1,0},{2,3},{3,2},{4,5},{5,4},{6,7},{7,6},{8,9},{9,8},{10,11... | collective-permute-start | bytes 98312 | tf_op jit(solution)/shard_map/ppermute | solution.py:347
  81.9 0.9 %collective-permute-done.19 = f32[16,512]{1,0:T(8,128)S(1)} collective-permute-done((f32[16,512]{1,0:T(8,128)S(1)}, f32[16,512]{1,0:T(8,128)S(1)}, u32[]{:S(2)}, u32[]{:S(2)}) %collective-permute-start.19) | collective-permute-done | bytes 32800 | tf_op jit(solution)/shard_map/ppermute | solution.py:347
  82.8 0.6 maximum_select_fusion
  (12 shorter events, 0.2 us)
Async XLA Ops:
  9.3 11.2 %collective-permute-start = (f32[512,256]{1,0:T(8,128)S(1)}, f32[512,256]{1,0:T(8,128)S(1)}, u32[]{:S(2)}, u32[]{:S(2)}) collective-permute-start(f32[512,256]{1,0:T(8,128)S(1)} %get-tuple-element.34), channel_id=1, source_target_pairs={{0,8},{1,33},{2,10},{3,35},{4,12},{5,37},{6,14},{7,39},{8,0},{9,41... | collective-permute-start | bytes 1572872 | tf_op jit(solution)/shard_map/ppermute | solution.py:347
  11.5 9.5 %collective-permute-start.1 = (f32[512,256]{1,0:T(8,128)S(1)}, f32[512,256]{1,0:T(8,128)S(1)}, u32[]{:S(2)}, u32[]{:S(2)}) collective-permute-start(f32[512,256]{1,0:T(8,128)S(1)} %get-tuple-element.35), channel_id=1, source_target_pairs={{0,24},{1,97},{2,26},{3,99},{4,28},{5,101},{6,30},{7,103},{8,16},{... | collective-permute-start | bytes 1572872 | tf_op jit(solution)/shard_map/ppermute | solution.py:347
  19.4 9.9 %collective-permute-start.2 = (f32[512,256]{1,0:T(8,128)S(1)}, f32[512,256]{1,0:T(8,128)S(1)}, u32[]{:S(2)}, u32[]{:S(2)}) collective-permute-start(f32[512,256]{1,0:T(8,128)S(1)} %get-tuple-element.37), channel_id=1, source_target_pairs={{0,8},{1,33},{2,10},{3,35},{4,12},{5,37},{6,14},{7,39},{8,0},{9,41... | collective-permute-start | bytes 1572872 | tf_op jit(solution)/shard_map/ppermute | solution.py:347
  19.9 9.5 %collective-permute-start.3 = (f32[512,256]{1,0:T(8,128)S(1)}, f32[512,256]{1,0:T(8,128)S(1)}, u32[]{:S(2)}, u32[]{:S(2)}) collective-permute-start(f32[512,256]{1,0:T(8,128)S(1)} %get-tuple-element.38), channel_id=1, source_target_pairs={{0,24},{1,97},{2,26},{3,99},{4,28},{5,101},{6,30},{7,103},{8,16},{... | collective-permute-start | bytes 1572872 | tf_op jit(solution)/shard_map/ppermute | solution.py:347
  27.2 8.4 %collective-permute-start.5 = (f32[512,256]{1,0:T(8,128)S(1)}, f32[512,256]{1,0:T(8,128)S(1)}, u32[]{:S(2)}, u32[]{:S(2)}) collective-permute-start(f32[512,256]{1,0:T(8,128)S(1)} %get-tuple-element.42), channel_id=1, source_target_pairs={{0,8},{1,33},{2,10},{3,35},{4,12},{5,37},{6,14},{7,39},{8,0},{9,41... | collective-permute-start | bytes 1572872 | tf_op jit(solution)/shard_map/ppermute | solution.py:347
  27.3 9.6 %collective-permute-start.4 = (f32[512,256]{1,0:T(8,128)S(1)}, f32[512,256]{1,0:T(8,128)S(1)}, u32[]{:S(2)}, u32[]{:S(2)}) collective-permute-start(f32[512,256]{1,0:T(8,128)S(1)} %get-tuple-element.40), channel_id=1, source_target_pairs={{0,24},{1,97},{2,26},{3,99},{4,28},{5,101},{6,30},{7,103},{8,16},{... | collective-permute-start | bytes 1572872 | tf_op jit(solution)/shard_map/ppermute | solution.py:347
  29.4 25.6 %copy-start = (s32[512]{0:T(512)S(1)}, s32[512]{0:T(512)}, u32[]{:S(2)}) copy-start(s32[512]{0:T(512)} %param.9) | copy-start | bytes 6148
  37.0 5.3 %collective-permute-start.7 = (f32[512,128]{1,0:T(8,128)S(1)}, f32[512,128]{1,0:T(8,128)S(1)}, u32[]{:S(2)}, u32[]{:S(2)}) collective-permute-start(f32[512,128]{1,0:T(8,128)S(1)} %slice_select_fusion.2), channel_id=1, source_target_pairs={{0,32},{1,9},{2,34},{3,11},{4,36},{5,13},{6,38},{7,15},{8,40},{9,1... | collective-permute-start | bytes 786440 | tf_op jit(solution)/shard_map/ppermute | solution.py:347
  38.4 10.5 %collective-permute-start.6 = (f32[512,128]{1,0:T(8,128)S(1)}, f32[512,128]{1,0:T(8,128)S(1)}, u32[]{:S(2)}, u32[]{:S(2)}) collective-permute-start(f32[512,128]{1,0:T(8,128)S(1)} %get-tuple-element.51), channel_id=1, source_target_pairs={{0,64},{1,17},{2,66},{3,19},{4,68},{5,21},{6,70},{7,23},{8,72},{9,... | collective-permute-start | bytes 786440 | tf_op jit(solution)/shard_map/ppermute | solution.py:347
  42.0 9.5 %collective-permute-start.8 = (f32[512,128]{1,0:T(8,128)S(1)}, f32[512,128]{1,0:T(8,128)S(1)}, u32[]{:S(2)}, u32[]{:S(2)}) collective-permute-start(f32[512,128]{1,0:T(8,128)S(1)} %get-tuple-element.52), channel_id=1, source_target_pairs={{0,96},{1,25},{2,98},{3,27},{4,100},{5,29},{6,102},{7,31},{8,104},... | collective-permute-start | bytes 786440 | tf_op jit(solution)/shard_map/ppermute | solution.py:347
  51.7 4.5 %collective-permute-start.9 = (f32[512,128]{1,0:T(8,128)S(1)}, f32[512,128]{1,0:T(8,128)S(1)}, u32[]{:S(2)}, u32[]{:S(2)}) collective-permute-start(f32[512,128]{1,0:T(8,128)S(1)} %add_add_fusion.sums_ref), channel_id=1, source_target_pairs={{0,1},{1,0},{2,3},{3,2},{4,5},{5,4},{6,7},{7,6},{8,9},{9,8},{10,11... | collective-permute-start | bytes 786440 | tf_op jit(solution)/shard_map/ppermute | solution.py:347
  57.5 5.7 %collective-permute-start.10 = (f32[64,512]{1,0:T(8,128)S(1)}, f32[64,512]{1,0:T(8,128)S(1)}, u32[]{:S(2)}, u32[]{:S(2)}) collective-permute-start(f32[64,512]{1,0:T(8,128)S(1)} %get-tuple-element.48), channel_id=1, source_target_pairs={{0,16},{1,65},{2,18},{3,67},{4,20},{5,69},{6,22},{7,71},{8,24},{9,... | collective-permute-start | bytes 393224 | tf_op jit(solution)/shard_map/ppermute | solution.py:347
  57.6 5.6 %collective-permute-start.11 = (f32[64,512]{1,0:T(8,128)S(1)}, f32[64,512]{1,0:T(8,128)S(1)}, u32[]{:S(2)}, u32[]{:S(2)}) collective-permute-start(f32[64,512]{1,0:T(8,128)S(1)} %get-tuple-element.49), channel_id=1, source_target_pairs={{0,8},{1,33},{2,10},{3,35},{4,12},{5,37},{6,14},{7,39},{8,0},{9,41... | collective-permute-start | bytes 393224 | tf_op jit(solution)/shard_map/ppermute | solution.py:347
  58.1 6.2 %collective-permute-start.12 = (f32[64,512]{1,0:T(8,128)S(1)}, f32[64,512]{1,0:T(8,128)S(1)}, u32[]{:S(2)}, u32[]{:S(2)}) collective-permute-start(f32[64,512]{1,0:T(8,128)S(1)} %get-tuple-element.50), channel_id=1, source_target_pairs={{0,24},{1,97},{2,26},{3,99},{4,28},{5,101},{6,30},{7,103},{8,16},{... | collective-permute-start | bytes 393224 | tf_op jit(solution)/shard_map/ppermute | solution.py:347
  64.3 4.3 %collective-permute-start.13 = (f32[16,512]{1,0:T(8,128)S(1)}, f32[16,512]{1,0:T(8,128)S(1)}, u32[]{:S(2)}, u32[]{:S(2)}) collective-permute-start(f32[16,512]{1,0:T(8,128)S(1)} %get-tuple-element.53), channel_id=1, source_target_pairs={{0,64},{1,17},{2,66},{3,19},{4,68},{5,21},{6,70},{7,23},{8,72},{9,... | collective-permute-start | bytes 98312 | tf_op jit(solution)/shard_map/ppermute | solution.py:347
  66.6 4.0 %collective-permute-start.15 = (f32[16,512]{1,0:T(8,128)S(1)}, f32[16,512]{1,0:T(8,128)S(1)}, u32[]{:S(2)}, u32[]{:S(2)}) collective-permute-start(f32[16,512]{1,0:T(8,128)S(1)} %get-tuple-element.54), channel_id=1, source_target_pairs={{0,96},{1,25},{2,98},{3,27},{4,100},{5,29},{6,102},{7,31},{8,104},... | collective-permute-start | bytes 98312 | tf_op jit(solution)/shard_map/ppermute | solution.py:347
  67.1 3.4 %collective-permute-start.14 = (f32[16,512]{1,0:T(8,128)S(1)}, f32[16,512]{1,0:T(8,128)S(1)}, u32[]{:S(2)}, u32[]{:S(2)}) collective-permute-start(f32[16,512]{1,0:T(8,128)S(1)} %get-tuple-element.55), channel_id=1, source_target_pairs={{0,32},{1,9},{2,34},{3,11},{4,36},{5,13},{6,38},{7,15},{8,40},{9,1... | collective-permute-start | bytes 98312 | tf_op jit(solution)/shard_map/ppermute | solution.py:347
  70.6 4.3 %collective-permute-start.18 = (f32[16,512]{1,0:T(8,128)S(1)}, f32[16,512]{1,0:T(8,128)S(1)}, u32[]{:S(2)}, u32[]{:S(2)}) collective-permute-start(f32[16,512]{1,0:T(8,128)S(1)} %fusion.1), channel_id=1, source_target_pairs={{0,4},{1,5},{2,6},{3,7},{4,0},{5,1},{6,2},{7,3},{8,12},{9,13},{10,... | collective-permute-start | bytes 98312 | tf_op jit(solution)/shard_map/ppermute | solution.py:347
  73.4 4.0 %collective-permute-start.17 = (f32[16,512]{1,0:T(8,128)S(1)}, f32[16,512]{1,0:T(8,128)S(1)}, u32[]{:S(2)}, u32[]{:S(2)}) collective-permute-start(f32[16,512]{1,0:T(8,128)S(1)} %fusion.1), channel_id=1, source_target_pairs={{0,6},{1,7},{2,4},{3,5},{4,2},{5,3},{6,0},{7,1},{8,14},{9,15},{10,... | collective-permute-start | bytes 98312 | tf_op jit(solution)/shard_map/ppermute | solution.py:347
  74.3 3.1 %collective-permute-start.16 = (f32[16,512]{1,0:T(8,128)S(1)}, f32[16,512]{1,0:T(8,128)S(1)}, u32[]{:S(2)}, u32[]{:S(2)}) collective-permute-start(f32[16,512]{1,0:T(8,128)S(1)} %fusion.1), channel_id=1, source_target_pairs={{0,2},{1,3},{2,0},{3,1},{4,6},{5,7},{6,4},{7,5},{8,10},{9,11},{10,... | collective-permute-start | bytes 98312 | tf_op jit(solution)/shard_map/ppermute | solution.py:347
  77.4 5.4 %collective-permute-start.19 = (f32[16,512]{1,0:T(8,128)S(1)}, f32[16,512]{1,0:T(8,128)S(1)}, u32[]{:S(2)}, u32[]{:S(2)}) collective-permute-start(f32[16,512]{1,0:T(8,128)S(1)} %add_add_fusion.2), channel_id=1, source_target_pairs={{0,1},{1,0},{2,3},{3,2},{4,5},{5,4},{6,7},{7,6},{8,9},{9,8},{10,11... | collective-permute-start | bytes 98312 | tf_op jit(solution)/shard_map/ppermute | solution.py:347
